TPU v7x, 32 devices: a whole 2x2x4 slice. The times are simulated.
32 devices in a mesh: groups: 2 (over x), space: 16 (over z, y, core).
Axes of the slice: x: 2, y: 2, z: 4, core: 2. Of those that a mesh axis runs over, the one named last changes fastest.
Arguments:
- eigvecs: bfloat16 [32, 64, 2, 3, 128], P('groups', 'space'), parts along dimension 0, may hold values from -1.3515625 to 1.3515625
- phase_index: int32 [128], P('groups'), parts along dimension 0, may hold values from 0 to 47
- perambulator: bfloat16 [512, 2, 128, 128], P(('groups', 'space')), parts along dimension 0, may hold values from -0.046875 to 0.046875
- tile_sink: int32 [512, 1], P(('groups', 'space')), parts along dimension 0, may hold values from 0 to 15; in each aligned block of 16 rows (0 to 15, 16 to 31, ...) at most 2 rows name the same one
- tile_sep: int32 [512], P(('groups', 'space')), parts along dimension 0, may hold values from 0 to 7
- tile_diagram: int32 [512], P(('groups', 'space')), parts along dimension 0, may hold values from 0 to 1
Outputs:
- elementals: bfloat16 [32, 2, 128, 128], P(('groups', 'space')), parts along dimension 0
- correlator: float32 [512, 2], P(('groups', 'space')), parts along dimension 0
There are 2 independent parts, one for each index of `groups`. A program takes and returns all parts, laid end to end along the dimension named above; each array names one. Nothing has to cross between parts.
Inputs may be any that keep to these rules, and one draw needn't show every extreme that they name: `tile_sink`: in the tiles of one device no sink time is named by more than 2 tiles.
All inputs are finite; a program needn't handle non-finite values.
Results may differ from a plain program's by a relative error of at most 0.0048.
Values may be sent and summed in bfloat16 or wider, within the bound.
No kernel may reach another device: no remote copies, remote signals or barrier semaphores. Data moves between devices by JAX's collectives and lax.ppermute only.
A program may use at most 128 MiB of HBM per device.

v0:
```python
import math

import jax
import jax.numpy as jnp
from jax import lax
from jax.sharding import PartitionSpec as P

PERIOD = 48


def make_right(vecs, cosine, sine):
    real_part = vecs[..., 0, :, :].astype(jnp.float32)
    imag_part = vecs[..., 1, :, :].astype(jnp.float32)
    cos_col = cosine[:, None, None]
    sin_col = sine[:, None, None]
    first = (cos_col * real_part - sin_col * imag_part).astype(jnp.bfloat16)
    second = (sin_col * real_part + cos_col * imag_part).astype(jnp.bfloat16)
    top = jnp.stack([first, second], -2)
    bottom = jnp.stack([second, -first], -2)
    return jnp.stack([top, bottom], -4)


def phases(indices):
    angle = 2.0 * math.pi / PERIOD * indices.astype(jnp.float32)
    return (jnp.cos(angle), jnp.sin(angle))


def contract_tiles(sink_mat, source_mat, tiles, diagram):

    def mult(left, right):
        return jnp.einsum("bij,bjk->bik", left, right, preferred_element_type=jnp.float32)

    tile_re = tiles[:, 0]
    tile_im = tiles[:, 1]
    trans_re = jnp.swapaxes(tile_re, 1, 2)
    trans_im = -jnp.swapaxes(tile_im, 1, 2)
    flag = (diagram == 1)[:, None, None]
    left_re = jnp.where(flag, trans_re, tile_re)
    left_im = jnp.where(flag, trans_im, tile_im)
    right_re = jnp.where(flag, tile_re, trans_re)
    right_im = jnp.where(flag, tile_im, trans_im)
    sink_re = sink_mat[:, 0]
    sink_im = sink_mat[:, 1]
    src_re = jnp.swapaxes(source_mat[:, 0], 1, 2)
    src_im = -jnp.swapaxes(source_mat[:, 1], 1, 2)
    first_re = mult(sink_re, left_re) - mult(sink_im, left_im)
    first_im = mult(sink_re, left_im) + mult(sink_im, left_re)
    second_re = jnp.swapaxes(mult(src_re, right_re) - mult(src_im, right_im), 1, 2)
    second_im = jnp.swapaxes(mult(src_re, right_im) + mult(src_im, right_re), 1, 2)
    trace_re = jnp.sum(first_re * second_re - first_im * second_im, axis=(1, 2))
    trace_im = jnp.sum(first_re * second_im + first_im * second_re, axis=(1, 2))
    return jnp.stack([trace_re, trace_im], -1)


def run_blocks(step_fn, items, total):
    block = math.gcd(32, total)
    shaped = tuple((item.reshape((total // block, block) + item.shape[1:]) for item in items))
    result = lax.map(step_fn, shaped)
    return result.reshape((total,) + result.shape[2:])


def local(eigvecs, phase_index, perambulator, tile_sink, tile_sep, tile_diagram):
    tile_count = perambulator.shape[0]
    sinks = tile_sink[:, 0]
    cosine, sine = phases(phase_index)
    slices = lax.all_to_all(eigvecs, "space", split_axis=0, concat_axis=1, tiled=True)
    vecs = slices[0]
    right = make_right(vecs, cosine, sine)
    value = jnp.einsum("spck,spcol->okl", vecs, right, preferred_element_type=jnp.float32)
    elemental = value.astype(jnp.bfloat16)[None]
    gathered = lax.all_gather(elemental, "space", axis=0, tiled=True)
    time_count = gathered.shape[0]
    sources = jnp.mod(sinks - tile_sep, time_count)

    def holder_block(items):
        tiles, sink_ids, source_ids, diagram = items
        return contract_tiles(gathered[sink_ids], gathered[source_ids], tiles, diagram)

    correlator = run_blocks(holder_block, (perambulator, sinks, sources, tile_diagram), tile_count)
    return (elemental, correlator)


def solution(mesh):
    return jax.shard_map(
        local,
        mesh=mesh,
        in_specs=(
            P("groups", "space", None, None, None),
            P("groups"),
            P(("groups", "space"), None, None, None),
            P(("groups", "space"), None),
            P(("groups", "space")),
            P(("groups", "space")),
        ),
        out_specs=(P(("groups", "space"), None, None, None), P(("groups", "space"), None)),
        check_vma=False,
    )
```

profile of v0, /device:TPU:0, one launch (start us, length us, event | category | flops | bytes accessed | tf_op | source)
XLA Modules:
  0.0 76.8 jit_solution(16801960626893713510)
XLA Ops:
  7.2 7.5 %all-to-all-start = ((bf16[16,4,2,3,128]{4,2,3,1,0:T(2,128)(2,1)}), bf16[16,4,2,3,128]{4,2,3,1,0:T(2,128)(2,1)S(1)}, u32[]{:S(2)}, u32[]{:S(2)}) async-start(bf16[16,4,2,3,128]{4,2,3,1,0:T(2,128)(2,1)} %param.6), calls=%async_computation | async-start | bytes 196608 | tf_op jit(solution)/shard_map/all_to_all | solution.py:66
  14.8 7.3 %all-to-all-done = bf16[16,4,2,3,128]{4,2,3,1,0:T(2,128)(2,1)S(1)} async-done(((bf16[16,4,2,3,128]{4,2,3,1,0:T(2,128)(2,1)}), bf16[16,4,2,3,128]{4,2,3,1,0:T(2,128)(2,1)S(1)}, u32[]{:S(2)}, u32[]{:S(2)}) %all-to-all-start) | async-done | bytes 98336 | tf_op jit(solution)/shard_map/all_to_all | solution.py:66
  22.3 0.1 fusion.21
  22.4 0.3 fusion
  22.7 0.7 copy.37
  23.5 0.3 copy.40
  23.8 0.3 copy.42
  24.1 0.4 copy-done.4
  24.5 0.6 copy-done.3
  25.2 0.6 copy-done.5
  25.8 0.7 copy.49
  26.5 32.5 %all-gather.3.cloned.1.call-done = bf16[32,128,128]{2,1,0:T(8,128)(2,1)} async-done(((bf16[2,128,128]{2,1,0:T(8,128)(2,1)}), bf16[32,128,128]{2,1,0:T(8,128)(2,1)}) %all-gather.3.cloned.1.call-update) | async-done | bytes 1048592 | tf_op jit(solution)/shard_map/all_gather | solution.py:71
  59.0 2.9 %gather_fusion.1 = bf16[16,2,128,128]{3,2,1,0:T(8,128)(2,1)} fusion(bf16[16,2,128,128]{3,2,1,0:T(8,128)(2,1)} %bitcast.124, s32[1024]{0:T(1024)S(1)} %pad_clamp_fusion), kind=kCustom, calls=%fused_computation.1 | custom fusion | bytes 2097216 | tf_op jit(solution)/shard_map/while/body/eval_jaxpr/gather | solution.py:77
  61.9 2.0 %gather_fusion = bf16[16,2,128,128]{3,2,1,0:T(8,128)(2,1)S(1)} fusion(bf16[16,2,128,128]{3,2,1,0:T(8,128)(2,1)} %bitcast.125, s32[1024]{0:T(1024)S(1)} %pad_clamp_fusion.1), kind=kCustom, calls=%fused_computation | custom fusion | bytes 2097216 | tf_op jit(solution)/shard_map/while/body/eval_jaxpr/gather | solution.py:77
  63.9 1.5 %fusion.5 = f32[16,128,128]{2,1,0:T(8,128)S(1)} fusion(bf16[16,2,128,128]{3,2,1,0:T(8,128)(2,1)} %gather_fusion.1, pred[16]{0:T(512)(128)(4,1)S(1)} %broadcast_compare_fusion, bf16[16,128,128]{1,2,0:T(8,128)(2,1)S(1)} %copy.42, bf16[16,2,128,128]{3,2,1,0:T(8,128)(2,1)S(1)} %copy-done), kind=kOutput, calls=%fused_computation.24 | convolution fusion | flops 67633152 | bytes 2621952 | tf_op jit(solution)/shard_map/while/body/eval_jaxpr/bij,bjk->bik/dot_general | solution.py:31
  65.4 0.4 fusion.3
  65.8 0.8 %copy-done.1 = bf16[16,2,128,128]{3,2,1,0:T(8,128)(2,1)S(1)} copy-done((bf16[16,2,128,128]{3,2,1,0:T(8,128)(2,1)S(1)}, bf16[16,2,128,128]{3,2,1,0:T(8,128)(2,1)}, u32[]{:S(2)}) %copy-start.1) | copy-done | bytes 1048600
  66.6 0.4 fusion.6
  67.0 0.4 fusion.4
  67.4 0.4 convolution_add_fusion
  67.8 0.4 convolution_subtract_fusion
  68.3 0.4 convolution_subtract_fusion.1
  68.7 0.7 subtract_reduce_fusion
  69.4 0.6 pad_maximum_fusion
  (20 shorter events, 0.4 us)
Async XLA Ops:
  7.2 7.6 %copy-start.2 = (s32[64]{0:T(128)S(1)}, s32[64]{0:T(128)}, u32[]{:S(2)}) copy-start(s32[64]{0:T(128)} %param.7) | copy-start | bytes 772
  7.2 16.3 %copy-start = (bf16[16,2,128,128]{3,2,1,0:T(8,128)(2,1)S(1)}, bf16[16,2,128,128]{3,2,1,0:T(8,128)(2,1)}, u32[]{:S(2)}) copy-start(bf16[16,2,128,128]{3,2,1,0:T(8,128)(2,1)} %param.8) | copy-start | bytes 3145732
  7.2 14.9 %all-to-all-start = ((bf16[16,4,2,3,128]{4,2,3,1,0:T(2,128)(2,1)}), bf16[16,4,2,3,128]{4,2,3,1,0:T(2,128)(2,1)S(1)}, u32[]{:S(2)}, u32[]{:S(2)}) async-start(bf16[16,4,2,3,128]{4,2,3,1,0:T(2,128)(2,1)} %param.6), calls=%async_computation | async-start | bytes 196608 | tf_op jit(solution)/shard_map/all_to_all | solution.py:66
  14.7 44.3 %all-gather.3.cloned.1.call-start = ((), (), s32[]{:S(2)}) async-start(), calls=%async_computation.1 | async-start | bytes 1114112 | tf_op jit(solution)/shard_map/all_gather | solution.py:71
  23.8 0.7 copy-start.4
  24.5 0.7 copy-start.3
  25.1 0.7 copy-start.5
  65.4 1.2 %copy-start.1 = (bf16[16,2,128,128]{3,2,1,0:T(8,128)(2,1)S(1)}, bf16[16,2,128,128]{3,2,1,0:T(8,128)(2,1)}, u32[]{:S(2)}) copy-start(bf16[16,2,128,128]{3,2,1,0:T(8,128)(2,1)} %gather_fusion.1) | copy-start | bytes 3145732
Sparse Core Ops, SparseCore 0:
  23.5 35.4 all-gather.2
where the time goes:
time: 77.2 us; the launch traced here: 76.8 us
  waiting for transfers between devices  39.8 us (52%)
  between operations  14.2 us (18%)
  local copies, waits for them, and re-layouts  9.55 us (12%)
  starting transfers between devices  7.57 us (10%)
  matrix products  4.82 us (6%)
  other arithmetic  0.85 us (1%)
    all_gather x1, waiting for transfers between devices, local(): gathered = lax.all_gather(elemental, 'space', axis=0, tiled=True)  32.5 us
    all_to_all x1, starting transfers between devices, local(): lax.all_to_all(eigvecs, 'space', split_axis=0, concat_axis=1, tiled=True)  7.53 us
    all_to_all x1, waiting for transfers between devices, local(): lax.all_to_all(eigvecs, 'space', split_axis=0, concat_axis=1, tiled=True)  7.31 us
    dot_general x8, matrix products, mult(): jnp.einsum('bij,bjk->bik', left, right, preferred_element_type=jnp.float32)  4.56 us
    unnamed x13, local copies, waits for them, and re-layouts  3.24 us
    gather x1, local copies, waits for them, and re-layouts, holder_block(): gathered[source_ids]  2.92 us
    gather x1, local copies, waits for them, and re-layouts, holder_block(): gathered[sink_ids]  1.97 us
  transfers between devices with their start and end apart: 2, of which 2 were waited for; matrix products, arithmetic and copies ran while one was open for 2% of the time, Pallas kernels for 0%

commit v1 on v0

v1 whole, which is shorter than its diff:
```python
import functools
import math

import jax
import jax.numpy as jnp
from jax import lax
from jax.experimental import pallas as pl
from jax.experimental.pallas import tpu as pltpu
from jax.sharding import PartitionSpec as P

PERIOD = 48
AXIS = "space"
GATHER_BYTES = 8 << 20
VMEM_LIMIT = 48 << 20


def phases(indices):
    angle = 2.0 * math.pi / PERIOD * indices.astype(jnp.float32)
    return (jnp.cos(angle), jnp.sin(angle))


def swap(block, offset):
    size = lax.axis_size(AXIS)
    return lax.ppermute(block, AXIS, [(i, i ^ offset) for i in range(size)])


def exchange(block):
    held = {0: block}
    bit = lax.axis_size(AXIS) // 2
    while bit >= 8:
        held.update({k ^ bit: swap(b, bit) for k, b in list(held.items())})
        bit //= 2
    for stage in ((4, 2, 6), (1,)):
        fresh = {}
        for step in stage:
            if step < lax.axis_size(AXIS):
                fresh.update({k ^ step: swap(b, step) for k, b in held.items()})
        held.update(fresh)
    return held


def rotated(vecs, cosine, sine):
    rows = vecs.shape[0]
    groups = vecs.reshape(rows // 8, 8, vecs.shape[1])
    even = lax.broadcasted_iota(jnp.int32, groups.shape, 1) % 2 == 0
    turned = jnp.where(even, -pltpu.roll(groups, 7, 1), pltpu.roll(groups, 1, 1)).reshape(vecs.shape)
    first = cosine * vecs + sine * turned
    second = sine * vecs - cosine * turned
    return first.astype(jnp.bfloat16), second.astype(jnp.bfloat16)


def tile_terms(left, right, left_turned, right_turned, tile_re, tile_im):
    n = tile_re.shape[0]
    dot = functools.partial(jnp.dot, preferred_element_type=jnp.float32)
    tile = jnp.concatenate([tile_re, tile_im], 1)
    turned = jnp.concatenate([-tile_im, tile_re], 1)
    first = dot(left, jnp.concatenate([tile, turned], 0))
    second = dot(tile, jnp.concatenate([right, right_turned], 0))
    fr, fi, sr, si = first[:, :n], first[:, n:], second[:, :n], second[:, n:]
    return (
        jnp.sum(fr * sr + fi * si, axis=0, keepdims=True),
        jnp.sum(fi * sr - fr * si, axis=0, keepdims=True),
    )


def contract(left_ref, right_ref, sign_ref, plain, turned, tiles_ref, re_ref, im_ref, corr_ref):
    count = tiles_ref.shape[0]

    def step(i, carry):
        a, b = left_ref[i], right_ref[i]
        re, im = tile_terms(plain[a], plain[b], turned[a], turned[b], tiles_ref[i, 0], tiles_ref[i, 1])
        re_ref[pl.ds(i, 1), :] = re
        im_ref[pl.ds(i, 1), :] = im * sign_ref[i].astype(jnp.float32)
        return carry

    lax.fori_loop(0, count, step, 0, unroll=4)
    corr_ref[...] = jnp.concatenate(
        [jnp.sum(re_ref[...], axis=1, keepdims=True), jnp.sum(im_ref[...], axis=1, keepdims=True)], 1
    )


def fused_kernel(offsets, left_ref, right_ref, sign_ref, me_ref, cos_ref, sin_ref, tiles_ref, *refs):
    blocks = refs[: len(offsets)]
    own_ref, corr_ref, plain, turned, re_ref, im_ref = refs[len(offsets):]
    times, n = blocks[0].shape[0], blocks[0].shape[2]
    me = me_ref[0]
    cosine = jnp.concatenate([cos_ref[me ^ k] for k in offsets], 0)
    sine = jnp.concatenate([sin_ref[me ^ k] for k in offsets], 0)

    def slice_step(t, carry):
        vecs = jnp.concatenate([b[t].astype(jnp.float32) for b in blocks], 0)
        first, second = rotated(vecs, cosine, sine)
        value = lax.dot_general(
            vecs.astype(jnp.bfloat16),
            jnp.concatenate([first, second], 1),
            (((0,), (0,)), ((), ())),
            preferred_element_type=jnp.float32,
        ).astype(jnp.bfloat16)
        plain[t] = value
        turned[t] = jnp.concatenate([-value[:, n:], value[:, :n]], 1)
        return carry

    lax.fori_loop(0, times, slice_step, 0, unroll=2)
    own = plain[me]
    own_ref[0, 0] = own[:, :n]
    own_ref[0, 1] = own[:, n:]
    contract(left_ref, right_ref, sign_ref, plain, turned, tiles_ref, re_ref, im_ref, corr_ref)


def tile_operands(tile_sink, tile_sep, tile_diagram, times):
    sinks = tile_sink[:, 0]
    sources = jnp.mod(sinks - tile_sep, times)
    flipped = tile_diagram == 1
    left = jnp.where(flipped, sources, sinks).astype(jnp.int32)
    right = jnp.where(flipped, sinks, sources).astype(jnp.int32)
    sign = jnp.where(flipped, -1, 1).astype(jnp.int32)
    return left, right, sign


def by_gathered_vectors(eigvecs, phase_index, perambulator, tile_sink, tile_sep, tile_diagram):
    times, sites, parts, colors, n = eigvecs.shape
    devices = lax.axis_size(AXIS)
    rows = sites * colors * parts
    block = eigvecs.transpose(0, 1, 3, 2, 4).reshape(times, rows, n)
    held = exchange(block)
    offsets = tuple(sorted(held))
    cosine, sine = phases(phase_index)

    def spread(column):
        return jnp.broadcast_to(column.reshape(devices, sites, 1, 1), (devices, sites, colors * parts, n)).reshape(devices, rows, n)

    left, right, sign = tile_operands(tile_sink, tile_sep, tile_diagram, times)
    me = lax.axis_index(AXIS).astype(jnp.int32)[None]
    tiles = perambulator.shape[0]
    smem = pl.BlockSpec(memory_space=pltpu.SMEM)
    vmem = pl.BlockSpec(memory_space=pltpu.VMEM)
    return pl.pallas_call(
        functools.partial(fused_kernel, offsets),
        out_shape=(
            jax.ShapeDtypeStruct((1, 2, n, n), jnp.bfloat16),
            jax.ShapeDtypeStruct((tiles, 2), jnp.float32),
        ),
        in_specs=[smem] * 4 + [vmem] * (3 + len(offsets)),
        out_specs=(vmem, vmem),
        scratch_shapes=[
            pltpu.VMEM((times, n, 2 * n), jnp.bfloat16),
            pltpu.VMEM((times, n, 2 * n), jnp.bfloat16),
            pltpu.VMEM((tiles, n), jnp.float32),
            pltpu.VMEM((tiles, n), jnp.float32),
        ],
        compiler_params=pltpu.CompilerParams(vmem_limit_bytes=VMEM_LIMIT),
    )(left, right, sign, me, spread(cosine), spread(sine), perambulator, *[held[k] for k in offsets])


def contract_kernel(left_ref, right_ref, sign_ref, elementals_ref, tiles_ref, corr_ref, plain, turned, re_ref, im_ref):
    times = elementals_ref.shape[0]

    def widen(t, carry):
        re, im = elementals_ref[t, 0], elementals_ref[t, 1]
        plain[t] = jnp.concatenate([re, im], 1)
        turned[t] = jnp.concatenate([-im, re], 1)
        return carry

    lax.fori_loop(0, times, widen, 0)
    contract(left_ref, right_ref, sign_ref, plain, turned, tiles_ref, re_ref, im_ref, corr_ref)


def by_gathered_elementals(eigvecs, phase_index, perambulator, tile_sink, tile_sep, tile_diagram):
    cosine, sine = phases(phase_index)
    vecs = lax.all_to_all(eigvecs, AXIS, split_axis=0, concat_axis=1, tiled=True)[0].astype(jnp.float32)
    cosine, sine = cosine[:, None, None], sine[:, None, None]
    first = cosine * vecs[:, 0] - sine * vecs[:, 1]
    second = sine * vecs[:, 0] + cosine * vecs[:, 1]
    right = jnp.stack([jnp.stack([first, second], -2), jnp.stack([second, -first], -2)], -4).astype(jnp.bfloat16)
    value = jnp.einsum("spck,spcol->okl", vecs.astype(jnp.bfloat16), right, preferred_element_type=jnp.float32)
    elemental = value.astype(jnp.bfloat16)[None]
    gathered = lax.all_gather(elemental, AXIS, axis=0, tiled=True)
    times, _, n, _ = gathered.shape
    tiles = perambulator.shape[0]
    left, right, sign = tile_operands(tile_sink, tile_sep, tile_diagram, times)
    smem = pl.BlockSpec(memory_space=pltpu.SMEM)
    vmem = pl.BlockSpec(memory_space=pltpu.VMEM)
    correlator = pl.pallas_call(
        contract_kernel,
        out_shape=jax.ShapeDtypeStruct((tiles, 2), jnp.float32),
        in_specs=[smem] * 3 + [vmem] * 2,
        out_specs=vmem,
        scratch_shapes=[
            pltpu.VMEM((times, n, 2 * n), jnp.bfloat16),
            pltpu.VMEM((times, n, 2 * n), jnp.bfloat16),
            pltpu.VMEM((tiles, n), jnp.float32),
            pltpu.VMEM((tiles, n), jnp.float32),
        ],
        compiler_params=pltpu.CompilerParams(vmem_limit_bytes=VMEM_LIMIT),
    )(left, right, sign, gathered, perambulator)
    return elemental, correlator


def local(eigvecs, *rest):
    devices = lax.axis_size(AXIS)
    small = eigvecs.size * eigvecs.dtype.itemsize * devices <= GATHER_BYTES
    if small and devices & (devices - 1) == 0:
        return by_gathered_vectors(eigvecs, *rest)
    return by_gathered_elementals(eigvecs, *rest)


def solution(mesh):
    return jax.shard_map(
        local,
        mesh=mesh,
        in_specs=(
            P("groups", "space", None, None, None),
            P("groups"),
            P(("groups", "space"), None, None, None),
            P(("groups", "space"), None),
            P(("groups", "space")),
            P(("groups", "space")),
        ),
        out_specs=(P(("groups", "space"), None, None, None), P(("groups", "space"), None)),
        check_vma=False,
    )
```

time: 77.2 us -> 28.4 us (0.37)
  waiting for transfers between devices: 39.8 us -> 6.44 us
  between operations: 14.2 us -> 0.73 us
  local copies, waits for them, and re-layouts: 9.55 us -> 3.37 us
  Pallas kernels: 0 us -> 5.08 us
  starting transfers between devices: 7.57 us -> 12.5 us
  matrix products: 4.82 us -> 0 us
  other arithmetic: 0.85 us -> 0.06 us
    all_gather x1 -> x0, waiting for transfers between devices: 32.5 us -> none  [local(): gathered = lax.all_gather(elemental, 'space', axis=0, tiled=True)]
    ppermute x0 -> x15, starting transfers between devices: none -> 12.5 us  [swap(): return lax.ppermute(block, AXIS, [(i, i ^ offset) for i in range(size)])]
    all_to_all x1 -> x0, starting transfers between devices: 7.53 us -> none  [local(): lax.all_to_all(eigvecs, 'space', split_axis=0, concat_axis=1, tiled=True)]
    all_to_all x1 -> x0, waiting for transfers between devices: 7.31 us -> none  [local(): lax.all_to_all(eigvecs, 'space', split_axis=0, concat_axis=1, tiled=True)]
    ppermute x0 -> x15, waiting for transfers between devices: none -> 6.44 us  [swap(): return lax.ppermute(block, AXIS, [(i, i ^ offset) for i in range(size)])]
    pallas_call x0 -> x1, Pallas kernels: none -> 5.08 us  [by_gathered_vectors(): pl.pallas_call(functools.partial(fused_kernel, offsets), out_shape=(jax.S...]
    gather x2 -> x0, local copies, waits for them, and re-layouts: 4.89 us -> none  [the longest x1 2.92 us: holder_block(): gathered[source_ids]]
    dot_general x9 -> x0, matrix products: 4.82 us -> none  [the longest x8 4.56 us: mult(): jnp.einsum('bij,bjk->bik', left, right, preferred_element_type=jnp.float32)]
  transfers between devices with their start and end apart: 2 -> 15, of which waited for: 2 -> 9; matrix products, arithmetic and copies ran while one was open for 2% -> 2% of each run, Pallas kernels for 0% -> 0%
where the time goes in v1:
time: 28.4 us; the launch traced here: 28.2 us
  starting transfers between devices  12.5 us (44%)
  waiting for transfers between devices  6.44 us (23%)
  Pallas kernels  5.08 us (18%)
  local copies, waits for them, and re-layouts  3.37 us (12%)
  between operations  0.73 us (3%)
    ppermute x15, starting transfers between devices, swap(): return lax.ppermute(block, AXIS, [(i, i ^ offset) for i in range(size)])  12.5 us
    ppermute x15, waiting for transfers between devices, swap(): return lax.ppermute(block, AXIS, [(i, i ^ offset) for i in range(size)])  6.44 us
    pallas_call x1, Pallas kernels, by_gathered_vectors(): pl.pallas_call(functools.partial(fused_kernel, offsets), out_shape=(jax.S...  5.08 us
    unnamed x12, local copies, waits for them, and re-layouts  2.02 us
    broadcast_in_dim x12, local copies, waits for them, and re-layouts, spread(): jnp.broadcast_to(column.reshape(devices, sites, 1, 1), (devices, sites, c...  0.72 us
    pallas_call x1, local copies, waits for them, and re-layouts, by_gathered_vectors(): pl.pallas_call(functools.partial(fused_kernel, offsets), out_shape=(jax.S...  0.64 us
  transfers between devices with their start and end apart: 15, of which 9 were waited for; matrix products, arithmetic and copies ran while one was open for 2% of the time, Pallas kernels for 0%

profile of v1, /device:TPU:0, one launch (start us, length us, event | category | flops | bytes accessed | tf_op | source)
XLA Modules:
  0.0 28.2 jit_solution(1248479956342407210)
XLA Ops:
  0.7 4.1 %collective-permute-start.7 = (bf16[16,24,128]{2,1,0:T(8,128)(2,1)}, bf16[16,24,128]{2,1,0:T(8,128)(2,1)S(1)}, u32[]{:S(2)}, u32[]{:S(2)}) collective-permute-start(bf16[16,24,128]{2,1,0:T(8,128)(2,1)} %bitcast.15), channel_id=1, source_target_pairs={{0,8},{1,9},{2,10},{3,11},{4,12},{5,13},{6,14},{7,15},{8,0},{9,1},... | collective-permute-start | bytes 294920 | tf_op jit(solution)/shard_map/ppermute | solution.py:24
  4.8 2.5 %collective-permute-start.5 = (bf16[16,24,128]{2,1,0:T(8,128)(2,1)}, bf16[16,24,128]{2,1,0:T(8,128)(2,1)S(1)}, u32[]{:S(2)}, u32[]{:S(2)}) collective-permute-start(bf16[16,24,128]{2,1,0:T(8,128)(2,1)} %bitcast.16), channel_id=1, source_target_pairs={{0,6},{1,7},{2,4},{3,5},{4,2},{5,3},{6,0},{7,1},{8,14},{9,15},{10,... | collective-permute-start | bytes 294920 | tf_op jit(solution)/shard_map/ppermute | solution.py:24
  7.3 0.4 %collective-permute-start.3 = (bf16[16,24,128]{2,1,0:T(8,128)(2,1)}, bf16[16,24,128]{2,1,0:T(8,128)(2,1)S(1)}, u32[]{:S(2)}, u32[]{:S(2)}) collective-permute-start(bf16[16,24,128]{2,1,0:T(8,128)(2,1)} %bitcast.17), channel_id=1, source_target_pairs={{0,4},{1,5},{2,6},{3,7},{4,0},{5,1},{6,2},{7,3},{8,12},{9,13},{10,... | collective-permute-start | bytes 294920 | tf_op jit(solution)/shard_map/ppermute | solution.py:24
  7.7 0.5 %collective-permute-start.1 = (bf16[16,24,128]{2,1,0:T(8,128)(2,1)}, bf16[16,24,128]{2,1,0:T(8,128)(2,1)S(1)}, u32[]{:S(2)}, u32[]{:S(2)}) collective-permute-start(bf16[16,24,128]{2,1,0:T(8,128)(2,1)} %bitcast.18), channel_id=1, source_target_pairs={{0,2},{1,3},{2,0},{3,1},{4,6},{5,7},{6,4},{7,5},{8,10},{9,11},{10,... | collective-permute-start | bytes 294920 | tf_op jit(solution)/shard_map/ppermute | solution.py:24
  8.3 1.5 %collective-permute-done.7.refs_8_ = bf16[16,24,128]{2,1,0:T(8,128)(2,1)S(1)} collective-permute-done((bf16[16,24,128]{2,1,0:T(8,128)(2,1)}, bf16[16,24,128]{2,1,0:T(8,128)(2,1)S(1)}, u32[]{:S(2)}, u32[]{:S(2)}) %collective-permute-start.7) | collective-permute-done | bytes 98336 | tf_op jit(solution)/shard_map/ppermute | solution.py:24
  9.8 1.9 %collective-permute-start.13 = (bf16[16,24,128]{2,1,0:T(8,128)(2,1)S(1)}, bf16[16,24,128]{2,1,0:T(8,128)(2,1)S(1)}, u32[]{:S(2)}, u32[]{:S(2)}) collective-permute-start(bf16[16,24,128]{2,1,0:T(8,128)(2,1)S(1)} %collective-permute-done.7.refs_8_), channel_id=1, source_target_pairs={{0,6},{1,7},{2,4},{3,5},{4,2},{5,3},{6,0},{7,1},{8,14},{9,15},{10,... | collective-permute-start | bytes 294920 | tf_op jit(solution)/shard_map/ppermute | solution.py:24
  11.7 0.6 %collective-permute-done.5.refs_6_ = bf16[16,24,128]{2,1,0:T(8,128)(2,1)S(1)} collective-permute-done((bf16[16,24,128]{2,1,0:T(8,128)(2,1)}, bf16[16,24,128]{2,1,0:T(8,128)(2,1)S(1)}, u32[]{:S(2)}, u32[]{:S(2)}) %collective-permute-start.5) | collective-permute-done | bytes 98336 | tf_op jit(solution)/shard_map/ppermute | solution.py:24
  12.3 1.3 %collective-permute-start.11 = (bf16[16,24,128]{2,1,0:T(8,128)(2,1)S(1)}, bf16[16,24,128]{2,1,0:T(8,128)(2,1)S(1)}, u32[]{:S(2)}, u32[]{:S(2)}) collective-permute-start(bf16[16,24,128]{2,1,0:T(8,128)(2,1)S(1)} %collective-permute-done.7.refs_8_), channel_id=1, source_target_pairs={{0,4},{1,5},{2,6},{3,7},{4,0},{5,1},{6,2},{7,3},{8,12},{9,13},{10,... | collective-permute-start | bytes 294920 | tf_op jit(solution)/shard_map/ppermute | solution.py:24
  13.6 0.2 collective-permute-done.3.refs_4_
  13.8 0.7 %collective-permute-start.9 = (bf16[16,24,128]{2,1,0:T(8,128)(2,1)S(1)}, bf16[16,24,128]{2,1,0:T(8,128)(2,1)S(1)}, u32[]{:S(2)}, u32[]{:S(2)}) collective-permute-start(bf16[16,24,128]{2,1,0:T(8,128)(2,1)S(1)} %collective-permute-done.7.refs_8_), channel_id=1, source_target_pairs={{0,2},{1,3},{2,0},{3,1},{4,6},{5,7},{6,4},{7,5},{8,10},{9,11},{10,... | collective-permute-start | bytes 294920 | tf_op jit(solution)/shard_map/ppermute | solution.py:24
  14.5 0.5 %collective-permute-start.6 = (bf16[16,24,128]{2,1,0:T(8,128)(2,1)S(1)}, bf16[16,24,128]{2,1,0:T(8,128)(2,1)S(1)}, u32[]{:S(2)}, u32[]{:S(2)}) collective-permute-start(bf16[16,24,128]{2,1,0:T(8,128)(2,1)S(1)} %collective-permute-done.5.refs_6_), channel_id=1, source_target_pairs={{0,1},{1,0},{2,3},{3,2},{4,5},{5,4},{6,7},{7,6},{8,9},{9,8},{10,11... | collective-permute-start | bytes 294920 | tf_op jit(solution)/shard_map/ppermute | solution.py:24
  15.0 1.4 %collective-permute-done.13.refs_14_ = bf16[16,24,128]{2,1,0:T(8,128)(2,1)S(1)} collective-permute-done((bf16[16,24,128]{2,1,0:T(8,128)(2,1)S(1)}, bf16[16,24,128]{2,1,0:T(8,128)(2,1)S(1)}, u32[]{:S(2)}, u32[]{:S(2)}) %collective-permute-start.13) | collective-permute-done | bytes 98336 | tf_op jit(solution)/shard_map/ppermute | solution.py:24
  16.4 0.9 %collective-permute-done.11.refs_12_ = bf16[16,24,128]{2,1,0:T(8,128)(2,1)S(1)} collective-permute-done((bf16[16,24,128]{2,1,0:T(8,128)(2,1)S(1)}, bf16[16,24,128]{2,1,0:T(8,128)(2,1)S(1)}, u32[]{:S(2)}, u32[]{:S(2)}) %collective-permute-start.11) | collective-permute-done | bytes 98336 | tf_op jit(solution)/shard_map/ppermute | solution.py:24
  17.4 1.1 %collective-permute-done.9.refs_10_ = bf16[16,24,128]{2,1,0:T(8,128)(2,1)S(1)} collective-permute-done((bf16[16,24,128]{2,1,0:T(8,128)(2,1)S(1)}, bf16[16,24,128]{2,1,0:T(8,128)(2,1)S(1)}, u32[]{:S(2)}, u32[]{:S(2)}) %collective-permute-start.9) | collective-permute-done | bytes 98336 | tf_op jit(solution)/shard_map/ppermute | solution.py:24
  18.4 0.5 %collective-permute-start.12 = (bf16[16,24,128]{2,1,0:T(8,128)(2,1)S(1)}, bf16[16,24,128]{2,1,0:T(8,128)(2,1)S(1)}, u32[]{:S(2)}, u32[]{:S(2)}) collective-permute-start(bf16[16,24,128]{2,1,0:T(8,128)(2,1)S(1)} %collective-permute-done.11.refs_12_), channel_id=1, source_target_pairs={{0,1},{1,0},{2,3},{3,2},{4,5},{5,4},{6,7},{7,6},{8,9},{9,8},{10,11... | collective-permute-start | bytes 294920 | tf_op jit(solution)/shard_map/ppermute | solution.py:24
  19.6 0.1 collective-permute-done.14.refs_15_
  19.7 0.2 collective-permute-done.12.refs_13_
  19.9 0.4 %collective-permute-done.10.refs_11_ = bf16[16,24,128]{2,1,0:T(8,128)(2,1)S(1)} collective-permute-done((bf16[16,24,128]{2,1,0:T(8,128)(2,1)S(1)}, bf16[16,24,128]{2,1,0:T(8,128)(2,1)S(1)}, u32[]{:S(2)}, u32[]{:S(2)}) %collective-permute-start.10) | collective-permute-done | bytes 98336 | tf_op jit(solution)/shard_map/ppermute | solution.py:24
  20.3 0.1 broadcast_in_dim.40.sin_ref
  20.4 0.1 broadcast_in_dim.36.cos_ref
  20.5 0.8 %copy-done.1 = bf16[16,4,2,3,128]{4,2,3,1,0:T(2,128)(2,1)S(1)} copy-done((bf16[16,4,2,3,128]{4,2,3,1,0:T(2,128)(2,1)S(1)}, bf16[16,4,2,3,128]{4,2,3,1,0:T(2,128)(2,1)}, u32[]{:S(2)}) %copy-start.1) | copy-done | bytes 98328
  21.3 1.2 %copy-done = bf16[16,2,128,128]{3,2,1,0:T(8,128)(2,1)S(1)} copy-done((bf16[16,2,128,128]{3,2,1,0:T(8,128)(2,1)S(1)}, bf16[16,2,128,128]{3,2,1,0:T(8,128)(2,1)}, u32[]{:S(2)}) %copy-start) | copy-done | bytes 1048600
  22.5 5.1 %shard_map.77 = (bf16[1,2,128,128]{3,2,1,0:T(8,128)(2,1)}, f32[16,2]{1,0:T(8,128)S(1)}) custom-call(s32[16]{0:T(128)S(1)} %bitcast_select_fusion.1.left_ref, s32[16]{0:T(128)S(1)} %get-tuple-element.6.right_ref, s32[16]{0:T(128)S(1)} %get-tuple-element.10.sign_ref, s32[1]{0:T(128)} %bitcast.1.me_ref, f32[16,24,128]{2,1,0:T(8,128)S(1)} %broadcast_in_dim.36.cos_ref, ...), custom_call_target="tpu_custom_call" | custom-call | tf_op jit(solution)/shard_map/pallas_call | solution.py:137
  27.6 0.6 %copy.13 = f32[16,2]{0,1:T(2,128)} copy(f32[16,2]{1,0:T(8,128)S(1)} %get-tuple-element.5) | data formatting | bytes 256 | tf_op jit(solution)/shard_map/pallas_call | solution.py:137
  (35 shorter events, 0.7 us)
Async XLA Ops:
  0.6 7.6 %copy-start.3 = (s32[16]{0:T(128)S(1)}, s32[16]{0:T(128)}, u32[]{:S(2)}) copy-start(s32[16]{0:T(128)} %param.11) | copy-start | bytes 196
  0.6 7.6 %copy-start.2 = (s32[16,1]{0,1:T(1,128)S(1)}, s32[16,1]{0,1:T(1,128)}, u32[]{:S(2)}) copy-start(s32[16,1]{0,1:T(1,128)} %param.9) | copy-start | bytes 196
  0.7 7.6 %copy-start.4 = (s32[16]{0:T(128)S(1)}, s32[16]{0:T(128)}, u32[]{:S(2)}) copy-start(s32[16]{0:T(128)} %param.10) | copy-start | bytes 196
  0.7 9.1 %collective-permute-start.7 = (bf16[16,24,128]{2,1,0:T(8,128)(2,1)}, bf16[16,24,128]{2,1,0:T(8,128)(2,1)S(1)}, u32[]{:S(2)}, u32[]{:S(2)}) collective-permute-start(bf16[16,24,128]{2,1,0:T(8,128)(2,1)} %bitcast.15), channel_id=1, source_target_pairs={{0,8},{1,9},{2,10},{3,11},{4,12},{5,13},{6,14},{7,15},{8,0},{9,1},... | collective-permute-start | bytes 294920 | tf_op jit(solution)/shard_map/ppermute | solution.py:24
  4.8 7.6 %collective-permute-start.5 = (bf16[16,24,128]{2,1,0:T(8,128)(2,1)}, bf16[16,24,128]{2,1,0:T(8,128)(2,1)S(1)}, u32[]{:S(2)}, u32[]{:S(2)}) collective-permute-start(bf16[16,24,128]{2,1,0:T(8,128)(2,1)} %bitcast.16), channel_id=1, source_target_pairs={{0,6},{1,7},{2,4},{3,5},{4,2},{5,3},{6,0},{7,1},{8,14},{9,15},{10,... | collective-permute-start | bytes 294920 | tf_op jit(solution)/shard_map/ppermute | solution.py:24
  7.3 6.5 %collective-permute-start.3 = (bf16[16,24,128]{2,1,0:T(8,128)(2,1)}, bf16[16,24,128]{2,1,0:T(8,128)(2,1)S(1)}, u32[]{:S(2)}, u32[]{:S(2)}) collective-permute-start(bf16[16,24,128]{2,1,0:T(8,128)(2,1)} %bitcast.17), channel_id=1, source_target_pairs={{0,4},{1,5},{2,6},{3,7},{4,0},{5,1},{6,2},{7,3},{8,12},{9,13},{10,... | collective-permute-start | bytes 294920 | tf_op jit(solution)/shard_map/ppermute | solution.py:24
  7.7 6.8 %collective-permute-start.1 = (bf16[16,24,128]{2,1,0:T(8,128)(2,1)}, bf16[16,24,128]{2,1,0:T(8,128)(2,1)S(1)}, u32[]{:S(2)}, u32[]{:S(2)}) collective-permute-start(bf16[16,24,128]{2,1,0:T(8,128)(2,1)} %bitcast.18), channel_id=1, source_target_pairs={{0,2},{1,3},{2,0},{3,1},{4,6},{5,7},{6,4},{7,5},{8,10},{9,11},{10,... | collective-permute-start | bytes 294920 | tf_op jit(solution)/shard_map/ppermute | solution.py:24
  8.3 6.3 %collective-permute-start = (bf16[16,24,128]{2,1,0:T(8,128)(2,1)}, bf16[16,24,128]{2,1,0:T(8,128)(2,1)S(1)}, u32[]{:S(2)}, u32[]{:S(2)}) collective-permute-start(bf16[16,24,128]{2,1,0:T(8,128)(2,1)} %bitcast.19), channel_id=1, source_target_pairs={{0,1},{1,0},{2,3},{3,2},{4,5},{5,4},{6,7},{7,6},{8,9},{9,8},{10,11... | collective-permute-start | bytes 294920 | tf_op jit(solution)/shard_map/ppermute | solution.py:24
  9.8 6.6 %collective-permute-start.13 = (bf16[16,24,128]{2,1,0:T(8,128)(2,1)S(1)}, bf16[16,24,128]{2,1,0:T(8,128)(2,1)S(1)}, u32[]{:S(2)}, u32[]{:S(2)}) collective-permute-start(bf16[16,24,128]{2,1,0:T(8,128)(2,1)S(1)} %collective-permute-done.7.refs_8_), channel_id=1, source_target_pairs={{0,6},{1,7},{2,4},{3,5},{4,2},{5,3},{6,0},{7,1},{8,14},{9,15},{10,... | collective-permute-start | bytes 294920 | tf_op jit(solution)/shard_map/ppermute | solution.py:24
  12.3 5.0 %collective-permute-start.11 = (bf16[16,24,128]{2,1,0:T(8,128)(2,1)S(1)}, bf16[16,24,128]{2,1,0:T(8,128)(2,1)S(1)}, u32[]{:S(2)}, u32[]{:S(2)}) collective-permute-start(bf16[16,24,128]{2,1,0:T(8,128)(2,1)S(1)} %collective-permute-done.7.refs_8_), channel_id=1, source_target_pairs={{0,4},{1,5},{2,6},{3,7},{4,0},{5,1},{6,2},{7,3},{8,12},{9,13},{10,... | collective-permute-start | bytes 294920 | tf_op jit(solution)/shard_map/ppermute | solution.py:24
  13.8 4.6 %collective-permute-start.9 = (bf16[16,24,128]{2,1,0:T(8,128)(2,1)S(1)}, bf16[16,24,128]{2,1,0:T(8,128)(2,1)S(1)}, u32[]{:S(2)}, u32[]{:S(2)}) collective-permute-start(bf16[16,24,128]{2,1,0:T(8,128)(2,1)S(1)} %collective-permute-done.7.refs_8_), channel_id=1, source_target_pairs={{0,2},{1,3},{2,0},{3,1},{4,6},{5,7},{6,4},{7,5},{8,10},{9,11},{10,... | collective-permute-start | bytes 294920 | tf_op jit(solution)/shard_map/ppermute | solution.py:24
  14.5 3.9 %collective-permute-start.8 = (bf16[16,24,128]{2,1,0:T(8,128)(2,1)S(1)}, bf16[16,24,128]{2,1,0:T(8,128)(2,1)S(1)}, u32[]{:S(2)}, u32[]{:S(2)}) collective-permute-start(bf16[16,24,128]{2,1,0:T(8,128)(2,1)S(1)} %collective-permute-done.7.refs_8_), channel_id=1, source_target_pairs={{0,1},{1,0},{2,3},{3,2},{4,5},{5,4},{6,7},{7,6},{8,9},{9,8},{10,11... | collective-permute-start | bytes 294920 | tf_op jit(solution)/shard_map/ppermute | solution.py:24
  14.5 4.5 %collective-permute-start.6 = (bf16[16,24,128]{2,1,0:T(8,128)(2,1)S(1)}, bf16[16,24,128]{2,1,0:T(8,128)(2,1)S(1)}, u32[]{:S(2)}, u32[]{:S(2)}) collective-permute-start(bf16[16,24,128]{2,1,0:T(8,128)(2,1)S(1)} %collective-permute-done.5.refs_6_), channel_id=1, source_target_pairs={{0,1},{1,0},{2,3},{3,2},{4,5},{5,4},{6,7},{7,6},{8,9},{9,8},{10,11... | collective-permute-start | bytes 294920 | tf_op jit(solution)/shard_map/ppermute | solution.py:24
  15.0 4.0 %copy-start.5 = (s32[64]{0:T(128)S(1)}, s32[64]{0:T(128)}, u32[]{:S(2)}) copy-start(s32[64]{0:T(128)} %param.7) | copy-start | bytes 772
  16.4 3.2 %collective-permute-start.4 = (bf16[16,24,128]{2,1,0:T(8,128)(2,1)S(1)}, bf16[16,24,128]{2,1,0:T(8,128)(2,1)S(1)}, u32[]{:S(2)}, u32[]{:S(2)}) collective-permute-start(bf16[16,24,128]{2,1,0:T(8,128)(2,1)S(1)} %collective-permute-done.3.refs_4_), channel_id=1, source_target_pairs={{0,1},{1,0},{2,3},{3,2},{4,5},{5,4},{6,7},{7,6},{8,9},{9,8},{10,11... | collective-permute-start | bytes 294920 | tf_op jit(solution)/shard_map/ppermute | solution.py:24
  17.4 2.2 %collective-permute-start.2 = (bf16[16,24,128]{2,1,0:T(8,128)(2,1)S(1)}, bf16[16,24,128]{2,1,0:T(8,128)(2,1)S(1)}, u32[]{:S(2)}, u32[]{:S(2)}) collective-permute-start(bf16[16,24,128]{2,1,0:T(8,128)(2,1)S(1)} %collective-permute-done.1.refs_2_), channel_id=1, source_target_pairs={{0,1},{1,0},{2,3},{3,2},{4,5},{5,4},{6,7},{7,6},{8,9},{9,8},{10,11... | collective-permute-start | bytes 294920 | tf_op jit(solution)/shard_map/ppermute | solution.py:24
  18.4 1.3 %collective-permute-start.14 = (bf16[16,24,128]{2,1,0:T(8,128)(2,1)S(1)}, bf16[16,24,128]{2,1,0:T(8,128)(2,1)S(1)}, u32[]{:S(2)}, u32[]{:S(2)}) collective-permute-start(bf16[16,24,128]{2,1,0:T(8,128)(2,1)S(1)} %collective-permute-done.13.refs_14_), channel_id=1, source_target_pairs={{0,1},{1,0},{2,3},{3,2},{4,5},{5,4},{6,7},{7,6},{8,9},{9,8},{10,11... | collective-permute-start | bytes 294920 | tf_op jit(solution)/shard_map/ppermute | solution.py:24
  18.4 1.5 %collective-permute-start.12 = (bf16[16,24,128]{2,1,0:T(8,128)(2,1)S(1)}, bf16[16,24,128]{2,1,0:T(8,128)(2,1)S(1)}, u32[]{:S(2)}, u32[]{:S(2)}) collective-permute-start(bf16[16,24,128]{2,1,0:T(8,128)(2,1)S(1)} %collective-permute-done.11.refs_12_), channel_id=1, source_target_pairs={{0,1},{1,0},{2,3},{3,2},{4,5},{5,4},{6,7},{7,6},{8,9},{9,8},{10,11... | collective-permute-start | bytes 294920 | tf_op jit(solution)/shard_map/ppermute | solution.py:24
  19.0 1.3 %collective-permute-start.10 = (bf16[16,24,128]{2,1,0:T(8,128)(2,1)S(1)}, bf16[16,24,128]{2,1,0:T(8,128)(2,1)S(1)}, u32[]{:S(2)}, u32[]{:S(2)}) collective-permute-start(bf16[16,24,128]{2,1,0:T(8,128)(2,1)S(1)} %collective-permute-done.9.refs_10_), channel_id=1, source_target_pairs={{0,1},{1,0},{2,3},{3,2},{4,5},{5,4},{6,7},{7,6},{8,9},{9,8},{10,11... | collective-permute-start | bytes 294920 | tf_op jit(solution)/shard_map/ppermute | solution.py:24
  20.4 0.9 %copy-start.1 = (bf16[16,4,2,3,128]{4,2,3,1,0:T(2,128)(2,1)S(1)}, bf16[16,4,2,3,128]{4,2,3,1,0:T(2,128)(2,1)}, u32[]{:S(2)}) copy-start(bf16[16,4,2,3,128]{4,2,3,1,0:T(2,128)(2,1)} %param.6) | copy-start | bytes 294916
  21.3 1.2 %copy-start = (bf16[16,2,128,128]{3,2,1,0:T(8,128)(2,1)S(1)}, bf16[16,2,128,128]{3,2,1,0:T(8,128)(2,1)}, u32[]{:S(2)}) copy-start(bf16[16,2,128,128]{3,2,1,0:T(8,128)(2,1)} %tiles_ref.1) | copy-start | bytes 3145732

commit v2 on v1

--- a/solution.py
+++ b/solution.py
@@ -39,21 +39,16 @@
     return held
 
 
-def rotated(vecs, cosine, sine):
-    rows = vecs.shape[0]
-    groups = vecs.reshape(rows // 8, 8, vecs.shape[1])
-    even = lax.broadcasted_iota(jnp.int32, groups.shape, 1) % 2 == 0
-    turned = jnp.where(even, -pltpu.roll(groups, 7, 1), pltpu.roll(groups, 1, 1)).reshape(vecs.shape)
-    first = cosine * vecs + sine * turned
-    second = sine * vecs - cosine * turned
-    return first.astype(jnp.bfloat16), second.astype(jnp.bfloat16)
-
-
-def tile_terms(left, right, left_turned, right_turned, tile_re, tile_im):
-    n = tile_re.shape[0]
+def swapped(values):
+    other = lax.broadcasted_iota(jnp.int32, (8, values.shape[1]), 0) ^ 1
+    pieces = [jnp.take_along_axis(values[i : i + 8], other, axis=0) for i in range(0, values.shape[0], 8)]
+    return jnp.concatenate(pieces, 0)
+
+
+def tile_terms(left, right, left_turned, right_turned, tile):
+    n = tile.shape[0]
     dot = functools.partial(jnp.dot, preferred_element_type=jnp.float32)
-    tile = jnp.concatenate([tile_re, tile_im], 1)
-    turned = jnp.concatenate([-tile_im, tile_re], 1)
+    turned = jnp.concatenate([-tile[:, n:], tile[:, :n]], 1)
     first = dot(left, jnp.concatenate([tile, turned], 0))
     second = dot(tile, jnp.concatenate([right, right_turned], 0))
     fr, fi, sr, si = first[:, :n], first[:, n:], second[:, :n], second[:, n:]
@@ -68,31 +63,50 @@
 
     def step(i, carry):
         a, b = left_ref[i], right_ref[i]
-        re, im = tile_terms(plain[a], plain[b], turned[a], turned[b], tiles_ref[i, 0], tiles_ref[i, 1])
+        re, im = tile_terms(plain[a], plain[b], turned[a], turned[b], tiles_ref[i])
         re_ref[pl.ds(i, 1), :] = re
         im_ref[pl.ds(i, 1), :] = im * sign_ref[i].astype(jnp.float32)
         return carry
 
-    lax.fori_loop(0, count, step, 0, unroll=4)
-    corr_ref[...] = jnp.concatenate(
-        [jnp.sum(re_ref[...], axis=1, keepdims=True), jnp.sum(im_ref[...], axis=1, keepdims=True)], 1
-    )
-
-
-def fused_kernel(offsets, left_ref, right_ref, sign_ref, me_ref, cos_ref, sin_ref, tiles_ref, *refs):
-    blocks = refs[: len(offsets)]
-    own_ref, corr_ref, plain, turned, re_ref, im_ref = refs[len(offsets):]
-    times, n = blocks[0].shape[0], blocks[0].shape[2]
+    lax.fori_loop(0, count, step, 0, unroll=math.gcd(count, 16))
+    corr_ref[0, :] = jnp.sum(re_ref[...], axis=1)
+    corr_ref[1, :] = jnp.sum(im_ref[...], axis=1)
+
+
+def fill_tables(blocks, rows, sites, owner, cos_ref, sin_ref, tables):
+    n = tables[0].shape[1]
+    row = lax.broadcasted_iota(jnp.int32, (rows, n), 0)
+    sign = jnp.where(row % 2 == 0, -1.0, 1.0)
+    for j in range(blocks):
+        first = owner(j) * sites
+        for source, plain, signed in ((cos_ref, tables[0], tables[2]), (sin_ref, tables[1], tables[3])):
+            value = jnp.full((rows, n), source[first], jnp.float32)
+            for q in range(1, sites):
+                value = jnp.where(row >= q * (rows // sites), source[first + q], value)
+            plain[pl.ds(j * rows, rows)] = value
+            signed[pl.ds(j * rows, rows)] = value * sign
+
+
+def fused_kernel(offsets, sites, left_ref, right_ref, sign_ref, me_ref, cos_ref, sin_ref, tiles_ref, own_hbm, *refs):
+    received = refs[: len(offsets) - 1]
+    own_ref, corr_ref, plain, turned, re_ref, im_ref, block_ref, sems, *tables = refs[len(offsets) - 1 :]
+    load_block = pltpu.make_async_copy(own_hbm, block_ref, sems.at[0])
+    load_block.start()
+    times, rows, n = block_ref.shape
     me = me_ref[0]
-    cosine = jnp.concatenate([cos_ref[me ^ k] for k in offsets], 0)
-    sine = jnp.concatenate([sin_ref[me ^ k] for k in offsets], 0)
+    fill_tables(len(offsets), rows, sites, lambda j: me ^ offsets[j], cos_ref, sin_ref, tables)
+    cosine, sine, cosine_signed, sine_signed = tables
+    load_block.wait()
+    blocks = (block_ref, *received)
 
     def slice_step(t, carry):
         vecs = jnp.concatenate([b[t].astype(jnp.float32) for b in blocks], 0)
-        first, second = rotated(vecs, cosine, sine)
+        other = swapped(vecs)
+        first = cosine[...] * vecs + sine_signed[...] * other
+        second = sine[...] * vecs - cosine_signed[...] * other
         value = lax.dot_general(
             vecs.astype(jnp.bfloat16),
-            jnp.concatenate([first, second], 1),
+            jnp.concatenate([first.astype(jnp.bfloat16), second.astype(jnp.bfloat16)], 1),
             (((0,), (0,)), ((), ())),
             preferred_element_type=jnp.float32,
         ).astype(jnp.bfloat16)
@@ -100,11 +114,15 @@
         turned[t] = jnp.concatenate([-value[:, n:], value[:, :n]], 1)
         return carry
 
-    lax.fori_loop(0, times, slice_step, 0, unroll=2)
+    lax.fori_loop(0, times, slice_step, 0, unroll=True)
     own = plain[me]
     own_ref[0, 0] = own[:, :n]
     own_ref[0, 1] = own[:, n:]
     contract(left_ref, right_ref, sign_ref, plain, turned, tiles_ref, re_ref, im_ref, corr_ref)
+
+
+def widened(perambulator):
+    return jnp.concatenate([perambulator[:, 0], perambulator[:, 1]], 2)
 
 
 def tile_operands(tile_sink, tile_sep, tile_diagram, times):
@@ -123,33 +141,35 @@
     rows = sites * colors * parts
     block = eigvecs.transpose(0, 1, 3, 2, 4).reshape(times, rows, n)
     held = exchange(block)
-    offsets = tuple(sorted(held))
+    offsets = (0, *sorted(held, reverse=True)[:-1])
     cosine, sine = phases(phase_index)
-
-    def spread(column):
-        return jnp.broadcast_to(column.reshape(devices, sites, 1, 1), (devices, sites, colors * parts, n)).reshape(devices, rows, n)
-
     left, right, sign = tile_operands(tile_sink, tile_sep, tile_diagram, times)
     me = lax.axis_index(AXIS).astype(jnp.int32)[None]
     tiles = perambulator.shape[0]
+    wide = widened(perambulator)
     smem = pl.BlockSpec(memory_space=pltpu.SMEM)
     vmem = pl.BlockSpec(memory_space=pltpu.VMEM)
-    return pl.pallas_call(
-        functools.partial(fused_kernel, offsets),
+    hbm = pl.BlockSpec(memory_space=pltpu.HBM)
+    elemental, correlator = pl.pallas_call(
+        functools.partial(fused_kernel, offsets, sites),
         out_shape=(
             jax.ShapeDtypeStruct((1, 2, n, n), jnp.bfloat16),
-            jax.ShapeDtypeStruct((tiles, 2), jnp.float32),
+            jax.ShapeDtypeStruct((2, tiles), jnp.float32),
         ),
-        in_specs=[smem] * 4 + [vmem] * (3 + len(offsets)),
+        in_specs=[smem] * 6 + [vmem, hbm] + [vmem] * (devices - 1),
         out_specs=(vmem, vmem),
         scratch_shapes=[
             pltpu.VMEM((times, n, 2 * n), jnp.bfloat16),
             pltpu.VMEM((times, n, 2 * n), jnp.bfloat16),
             pltpu.VMEM((tiles, n), jnp.float32),
             pltpu.VMEM((tiles, n), jnp.float32),
-        ],
+            pltpu.VMEM(block.shape, block.dtype),
+            pltpu.SemaphoreType.DMA((2,)),
+        ]
+        + [pltpu.VMEM((devices * rows, n), jnp.float32)] * 4,
         compiler_params=pltpu.CompilerParams(vmem_limit_bytes=VMEM_LIMIT),
-    )(left, right, sign, me, spread(cosine), spread(sine), perambulator, *[held[k] for k in offsets])
+    )(left, right, sign, me, cosine, sine, wide, block, *[held[k] for k in offsets[1:]])
+    return elemental, correlator.T
 
 
 def contract_kernel(left_ref, right_ref, sign_ref, elementals_ref, tiles_ref, corr_ref, plain, turned, re_ref, im_ref):
@@ -182,7 +202,7 @@
     vmem = pl.BlockSpec(memory_space=pltpu.VMEM)
     correlator = pl.pallas_call(
         contract_kernel,
-        out_shape=jax.ShapeDtypeStruct((tiles, 2), jnp.float32),
+        out_shape=jax.ShapeDtypeStruct((2, tiles), jnp.float32),
         in_specs=[smem] * 3 + [vmem] * 2,
         out_specs=vmem,
         scratch_shapes=[
@@ -192,8 +212,8 @@
             pltpu.VMEM((tiles, n), jnp.float32),
         ],
         compiler_params=pltpu.CompilerParams(vmem_limit_bytes=VMEM_LIMIT),
-    )(left, right, sign, gathered, perambulator)
-    return elemental, correlator
+    )(left, right, sign, gathered, widened(perambulator))
+    return elemental, correlator.T
 
 
 def local(eigvecs, *rest):

time: 28.4 us -> 24 us (0.85)
  local copies, waits for them, and re-layouts: 3.37 us -> 1.32 us
  waiting for transfers between devices: 6.44 us -> 4.45 us
  Pallas kernels: 5.08 us -> 3.8 us
  starting transfers between devices: 12.5 us -> 13.3 us
    unnamed x12 -> x10, local copies, waits for them, and re-layouts: 2.02 us -> 0.02 us
    ppermute x15, waiting for transfers between devices: 6.44 us -> 4.45 us  [swap(): return lax.ppermute(block, AXIS, [(i, i ^ offset) for i in range(size)])]
    squeeze x0 -> x1, local copies, waits for them, and re-layouts: none -> 1.3 us  [widened(): return jnp.concatenate([perambulator[:, 0], perambulator[:, 1]], 2)]
    pallas_call x1, Pallas kernels: 5.08 us -> 3.8 us  [by_gathered_vectors(): pl.pallas_call(functools.partial(fused_kernel, offsets, sites), out_shape...]
    ppermute x15, starting transfers between devices: 12.5 us -> 13.3 us  [swap(): return lax.ppermute(block, AXIS, [(i, i ^ offset) for i in range(size)])]
    broadcast_in_dim x12 -> x0, local copies, waits for them, and re-layouts: 0.72 us -> none  [spread(): jnp.broadcast_to(column.reshape(devices, sites, 1, 1), (devices, sites, c...]
    pallas_call x1 -> x0, local copies, waits for them, and re-layouts: 0.64 us -> none  [by_gathered_vectors(): pl.pallas_call(functools.partial(fused_kernel, offsets), out_shape=(jax.S...]
  transfers between devices with their start and end apart: 15 -> 15, of which waited for: 9 -> 9; matrix products, arithmetic and copies ran while one was open for 2% -> 6% of each run, Pallas kernels for 0% -> 0%
where the time goes in v2:
time: 24 us; the launch traced here: 23.8 us
  starting transfers between devices  13.3 us (55%)
  waiting for transfers between devices  4.45 us (19%)
  Pallas kernels  3.8 us (16%)
  local copies, waits for them, and re-layouts  1.32 us (6%)
  between operations  0.75 us (3%)
    ppermute x15, starting transfers between devices, swap(): return lax.ppermute(block, AXIS, [(i, i ^ offset) for i in range(size)])  13.3 us
    ppermute x15, waiting for transfers between devices, swap(): return lax.ppermute(block, AXIS, [(i, i ^ offset) for i in range(size)])  4.45 us
    pallas_call x1, Pallas kernels, by_gathered_vectors(): pl.pallas_call(functools.partial(fused_kernel, offsets, sites), out_shape...  3.8 us
    squeeze x1, local copies, waits for them, and re-layouts, widened(): return jnp.concatenate([perambulator[:, 0], perambulator[:, 1]], 2)  1.3 us
  transfers between devices with their start and end apart: 15, of which 9 were waited for; matrix products, arithmetic and copies ran while one was open for 6% of the time, Pallas kernels for 0%

profile of v2, /device:TPU:0, one launch (start us, length us, event | category | flops | bytes accessed | tf_op | source)
XLA Modules:
  0.0 23.8 jit_solution(6032672981368047021)
XLA Ops:
  0.7 4.1 %collective-permute-start = (bf16[16,24,128]{2,1,0:T(8,128)(2,1)}, bf16[16,24,128]{2,1,0:T(8,128)(2,1)S(1)}, u32[]{:S(2)}, u32[]{:S(2)}) collective-permute-start(bf16[16,24,128]{2,1,0:T(8,128)(2,1)} %bitcast.20), channel_id=1, source_target_pairs={{0,8},{1,9},{2,10},{3,11},{4,12},{5,13},{6,14},{7,15},{8,0},{9,1},... | collective-permute-start | bytes 294920 | tf_op jit(solution)/shard_map/ppermute | solution.py:24
  4.8 2.5 %collective-permute-start.8 = (bf16[16,24,128]{2,1,0:T(8,128)(2,1)}, bf16[16,24,128]{2,1,0:T(8,128)(2,1)S(1)}, u32[]{:S(2)}, u32[]{:S(2)}) collective-permute-start(bf16[16,24,128]{2,1,0:T(8,128)(2,1)} %bitcast.21), channel_id=1, source_target_pairs={{0,6},{1,7},{2,4},{3,5},{4,2},{5,3},{6,0},{7,1},{8,14},{9,15},{10,... | collective-permute-start | bytes 294920 | tf_op jit(solution)/shard_map/ppermute | solution.py:24
  7.3 0.4 %collective-permute-start.10 = (bf16[16,24,128]{2,1,0:T(8,128)(2,1)}, bf16[16,24,128]{2,1,0:T(8,128)(2,1)S(1)}, u32[]{:S(2)}, u32[]{:S(2)}) collective-permute-start(bf16[16,24,128]{2,1,0:T(8,128)(2,1)} %bitcast.22), channel_id=1, source_target_pairs={{0,4},{1,5},{2,6},{3,7},{4,0},{5,1},{6,2},{7,3},{8,12},{9,13},{10,... | collective-permute-start | bytes 294920 | tf_op jit(solution)/shard_map/ppermute | solution.py:24
  7.8 0.5 %collective-permute-start.12 = (bf16[16,24,128]{2,1,0:T(8,128)(2,1)}, bf16[16,24,128]{2,1,0:T(8,128)(2,1)S(1)}, u32[]{:S(2)}, u32[]{:S(2)}) collective-permute-start(bf16[16,24,128]{2,1,0:T(8,128)(2,1)} %bitcast.23), channel_id=1, source_target_pairs={{0,2},{1,3},{2,0},{3,1},{4,6},{5,7},{6,4},{7,5},{8,10},{9,11},{10,... | collective-permute-start | bytes 294920 | tf_op jit(solution)/shard_map/ppermute | solution.py:24
  8.3 1.3 %slice_bitcast_fusion.1 = (bf16[16,128,128]{2,1,0:T(8,128)(2,1)S(1)}, bf16[16,128,128]{2,1,0:T(8,128)(2,1)S(1)}) fusion(bf16[16,2,128,128]{3,2,1,0:T(8,128)(2,1)} %param.8), kind=kLoop, calls=%fused_computation.2 | loop fusion | bytes 2097152 | tf_op jit(solution)/shard_map/squeeze | solution.py:125
  9.6 0.2 collective-permute-done.refs_7_
  9.8 2.4 %collective-permute-start.1 = (bf16[16,24,128]{2,1,0:T(8,128)(2,1)S(1)}, bf16[16,24,128]{2,1,0:T(8,128)(2,1)S(1)}, u32[]{:S(2)}, u32[]{:S(2)}) collective-permute-start(bf16[16,24,128]{2,1,0:T(8,128)(2,1)S(1)} %collective-permute-done.refs_7_), channel_id=1, source_target_pairs={{0,6},{1,7},{2,4},{3,5},{4,2},{5,3},{6,0},{7,1},{8,14},{9,15},{10,... | collective-permute-start | bytes 294920 | tf_op jit(solution)/shard_map/ppermute | solution.py:24
  12.2 0.1 collective-permute-done.8.refs_9_
  12.3 1.3 %collective-permute-start.3 = (bf16[16,24,128]{2,1,0:T(8,128)(2,1)S(1)}, bf16[16,24,128]{2,1,0:T(8,128)(2,1)S(1)}, u32[]{:S(2)}, u32[]{:S(2)}) collective-permute-start(bf16[16,24,128]{2,1,0:T(8,128)(2,1)S(1)} %collective-permute-done.refs_7_), channel_id=1, source_target_pairs={{0,4},{1,5},{2,6},{3,7},{4,0},{5,1},{6,2},{7,3},{8,12},{9,13},{10,... | collective-permute-start | bytes 294920 | tf_op jit(solution)/shard_map/ppermute | solution.py:24
  13.6 0.7 %collective-permute-start.5 = (bf16[16,24,128]{2,1,0:T(8,128)(2,1)S(1)}, bf16[16,24,128]{2,1,0:T(8,128)(2,1)S(1)}, u32[]{:S(2)}, u32[]{:S(2)}) collective-permute-start(bf16[16,24,128]{2,1,0:T(8,128)(2,1)S(1)} %collective-permute-done.refs_7_), channel_id=1, source_target_pairs={{0,2},{1,3},{2,0},{3,1},{4,6},{5,7},{6,4},{7,5},{8,10},{9,11},{10,... | collective-permute-start | bytes 294920 | tf_op jit(solution)/shard_map/ppermute | solution.py:24
  14.3 0.0 collective-permute-done.12.refs_13_
  14.3 0.5 %collective-permute-start.9 = (bf16[16,24,128]{2,1,0:T(8,128)(2,1)S(1)}, bf16[16,24,128]{2,1,0:T(8,128)(2,1)S(1)}, u32[]{:S(2)}, u32[]{:S(2)}) collective-permute-start(bf16[16,24,128]{2,1,0:T(8,128)(2,1)S(1)} %collective-permute-done.8.refs_9_), channel_id=1, source_target_pairs={{0,1},{1,0},{2,3},{3,2},{4,5},{5,4},{6,7},{7,6},{8,9},{9,8},{10,11... | collective-permute-start | bytes 294920 | tf_op jit(solution)/shard_map/ppermute | solution.py:24
  14.9 1.4 %collective-permute-done.1.refs_1_ = bf16[16,24,128]{2,1,0:T(8,128)(2,1)S(1)} collective-permute-done((bf16[16,24,128]{2,1,0:T(8,128)(2,1)S(1)}, bf16[16,24,128]{2,1,0:T(8,128)(2,1)S(1)}, u32[]{:S(2)}, u32[]{:S(2)}) %collective-permute-start.1) | collective-permute-done | bytes 98336 | tf_op jit(solution)/shard_map/ppermute | solution.py:24
  16.3 1.7 %collective-permute-done.3.refs_3_ = bf16[16,24,128]{2,1,0:T(8,128)(2,1)S(1)} collective-permute-done((bf16[16,24,128]{2,1,0:T(8,128)(2,1)S(1)}, bf16[16,24,128]{2,1,0:T(8,128)(2,1)S(1)}, u32[]{:S(2)}, u32[]{:S(2)}) %collective-permute-start.3) | collective-permute-done | bytes 98336 | tf_op jit(solution)/shard_map/ppermute | solution.py:24
  18.0 0.2 %collective-permute-done.5.refs_5_ = bf16[16,24,128]{2,1,0:T(8,128)(2,1)S(1)} collective-permute-done((bf16[16,24,128]{2,1,0:T(8,128)(2,1)S(1)}, bf16[16,24,128]{2,1,0:T(8,128)(2,1)S(1)}, u32[]{:S(2)}, u32[]{:S(2)}) %collective-permute-start.5) | collective-permute-done | bytes 98336 | tf_op jit(solution)/shard_map/ppermute | solution.py:24
  18.2 0.3 %collective-permute-start.2 = (bf16[16,24,128]{2,1,0:T(8,128)(2,1)S(1)}, bf16[16,24,128]{2,1,0:T(8,128)(2,1)S(1)}, u32[]{:S(2)}, u32[]{:S(2)}) collective-permute-start(bf16[16,24,128]{2,1,0:T(8,128)(2,1)S(1)} %collective-permute-done.1.refs_1_), channel_id=1, source_target_pairs={{0,1},{1,0},{2,3},{3,2},{4,5},{5,4},{6,7},{7,6},{8,9},{9,8},{10,11... | collective-permute-start | bytes 294920 | tf_op jit(solution)/shard_map/ppermute | solution.py:24
  18.5 0.2 %collective-permute-start.4 = (bf16[16,24,128]{2,1,0:T(8,128)(2,1)S(1)}, bf16[16,24,128]{2,1,0:T(8,128)(2,1)S(1)}, u32[]{:S(2)}, u32[]{:S(2)}) collective-permute-start(bf16[16,24,128]{2,1,0:T(8,128)(2,1)S(1)} %collective-permute-done.3.refs_3_), channel_id=1, source_target_pairs={{0,1},{1,0},{2,3},{3,2},{4,5},{5,4},{6,7},{7,6},{8,9},{9,8},{10,11... | collective-permute-start | bytes 294920 | tf_op jit(solution)/shard_map/ppermute | solution.py:24
  18.7 0.3 %collective-permute-start.6 = (bf16[16,24,128]{2,1,0:T(8,128)(2,1)S(1)}, bf16[16,24,128]{2,1,0:T(8,128)(2,1)S(1)}, u32[]{:S(2)}, u32[]{:S(2)}) collective-permute-start(bf16[16,24,128]{2,1,0:T(8,128)(2,1)S(1)} %collective-permute-done.5.refs_5_), channel_id=1, source_target_pairs={{0,1},{1,0},{2,3},{3,2},{4,5},{5,4},{6,7},{7,6},{8,9},{9,8},{10,11... | collective-permute-start | bytes 294920 | tf_op jit(solution)/shard_map/ppermute | solution.py:24
  19.0 0.1 pad_maximum_fusion.tiles_ref
  19.2 0.1 collective-permute-done.13.refs_12_
  19.3 0.2 %collective-permute-done.2.refs_0_ = bf16[16,24,128]{2,1,0:T(8,128)(2,1)S(1)} collective-permute-done((bf16[16,24,128]{2,1,0:T(8,128)(2,1)S(1)}, bf16[16,24,128]{2,1,0:T(8,128)(2,1)S(1)}, u32[]{:S(2)}, u32[]{:S(2)}) %collective-permute-start.2) | collective-permute-done | bytes 98336 | tf_op jit(solution)/shard_map/ppermute | solution.py:24
  19.5 0.3 %collective-permute-done.4.refs_2_ = bf16[16,24,128]{2,1,0:T(8,128)(2,1)S(1)} collective-permute-done((bf16[16,24,128]{2,1,0:T(8,128)(2,1)S(1)}, bf16[16,24,128]{2,1,0:T(8,128)(2,1)S(1)}, u32[]{:S(2)}, u32[]{:S(2)}) %collective-permute-start.4) | collective-permute-done | bytes 98336 | tf_op jit(solution)/shard_map/ppermute | solution.py:24
  19.8 0.2 %collective-permute-done.6.refs_4_ = bf16[16,24,128]{2,1,0:T(8,128)(2,1)S(1)} collective-permute-done((bf16[16,24,128]{2,1,0:T(8,128)(2,1)S(1)}, bf16[16,24,128]{2,1,0:T(8,128)(2,1)S(1)}, u32[]{:S(2)}, u32[]{:S(2)}) %collective-permute-start.6) | collective-permute-done | bytes 98336 | tf_op jit(solution)/shard_map/ppermute | solution.py:24
  20.1 3.8 %shard_map.77 = (bf16[1,2,128,128]{3,2,1,0:T(8,128)(2,1)}, f32[2,16]{1,0:T(2,128)}) custom-call(s32[16]{0:T(128)S(1)} %bitcast_select_fusion.1.left_ref, s32[16]{0:T(128)S(1)} %get-tuple-element.6.right_ref, s32[16]{0:T(128)S(1)} %get-tuple-element.12.sign_ref, s32[1]{0:T(128)} %bitcast.1.me_ref, f32[64]{0:T(128)S(1)} %get-tuple-element.11.cos_ref, ...), custom_call_target="tpu_custom_call" | custom-call | tf_op jit(solution)/shard_map/pallas_call | solution.py:153
  (22 shorter events, 0.1 us)
Async XLA Ops:
  0.6 8.9 %copy-start.1 = (s32[16,1]{0,1:T(1,128)S(1)}, s32[16,1]{0,1:T(1,128)}, u32[]{:S(2)}) copy-start(s32[16,1]{0,1:T(1,128)} %param.9) | copy-start | bytes 196
  0.6 8.9 %copy-start.2 = (s32[16]{0:T(128)S(1)}, s32[16]{0:T(128)}, u32[]{:S(2)}) copy-start(s32[16]{0:T(128)} %param.11) | copy-start | bytes 196
  0.7 8.9 %copy-start.3 = (s32[16]{0:T(128)S(1)}, s32[16]{0:T(128)}, u32[]{:S(2)}) copy-start(s32[16]{0:T(128)} %param.10) | copy-start | bytes 196
  0.7 14.2 %copy-start.4 = (s32[64]{0:T(128)S(1)}, s32[64]{0:T(128)}, u32[]{:S(2)}) copy-start(s32[64]{0:T(128)} %param.7) | copy-start | bytes 772
  0.7 9.1 %collective-permute-start = (bf16[16,24,128]{2,1,0:T(8,128)(2,1)}, bf16[16,24,128]{2,1,0:T(8,128)(2,1)S(1)}, u32[]{:S(2)}, u32[]{:S(2)}) collective-permute-start(bf16[16,24,128]{2,1,0:T(8,128)(2,1)} %bitcast.20), channel_id=1, source_target_pairs={{0,8},{1,9},{2,10},{3,11},{4,12},{5,13},{6,14},{7,15},{8,0},{9,1},... | collective-permute-start | bytes 294920 | tf_op jit(solution)/shard_map/ppermute | solution.py:24
  4.8 7.6 %collective-permute-start.8 = (bf16[16,24,128]{2,1,0:T(8,128)(2,1)}, bf16[16,24,128]{2,1,0:T(8,128)(2,1)S(1)}, u32[]{:S(2)}, u32[]{:S(2)}) collective-permute-start(bf16[16,24,128]{2,1,0:T(8,128)(2,1)} %bitcast.21), channel_id=1, source_target_pairs={{0,6},{1,7},{2,4},{3,5},{4,2},{5,3},{6,0},{7,1},{8,14},{9,15},{10,... | collective-permute-start | bytes 294920 | tf_op jit(solution)/shard_map/ppermute | solution.py:24
  7.3 6.3 %collective-permute-start.10 = (bf16[16,24,128]{2,1,0:T(8,128)(2,1)}, bf16[16,24,128]{2,1,0:T(8,128)(2,1)S(1)}, u32[]{:S(2)}, u32[]{:S(2)}) collective-permute-start(bf16[16,24,128]{2,1,0:T(8,128)(2,1)} %bitcast.22), channel_id=1, source_target_pairs={{0,4},{1,5},{2,6},{3,7},{4,0},{5,1},{6,2},{7,3},{8,12},{9,13},{10,... | collective-permute-start | bytes 294920 | tf_op jit(solution)/shard_map/ppermute | solution.py:24
  7.8 6.6 %collective-permute-start.12 = (bf16[16,24,128]{2,1,0:T(8,128)(2,1)}, bf16[16,24,128]{2,1,0:T(8,128)(2,1)S(1)}, u32[]{:S(2)}, u32[]{:S(2)}) collective-permute-start(bf16[16,24,128]{2,1,0:T(8,128)(2,1)} %bitcast.23), channel_id=1, source_target_pairs={{0,2},{1,3},{2,0},{3,1},{4,6},{5,7},{6,4},{7,5},{8,10},{9,11},{10,... | collective-permute-start | bytes 294920 | tf_op jit(solution)/shard_map/ppermute | solution.py:24
  8.3 6.1 %collective-permute-start.14 = (bf16[16,24,128]{2,1,0:T(8,128)(2,1)}, bf16[16,24,128]{2,1,0:T(8,128)(2,1)S(1)}, u32[]{:S(2)}, u32[]{:S(2)}) collective-permute-start(bf16[16,24,128]{2,1,0:T(8,128)(2,1)} %bitcast.24), channel_id=1, source_target_pairs={{0,1},{1,0},{2,3},{3,2},{4,5},{5,4},{6,7},{7,6},{8,9},{9,8},{10,11... | collective-permute-start | bytes 294920 | tf_op jit(solution)/shard_map/ppermute | solution.py:24
  9.8 6.5 %collective-permute-start.1 = (bf16[16,24,128]{2,1,0:T(8,128)(2,1)S(1)}, bf16[16,24,128]{2,1,0:T(8,128)(2,1)S(1)}, u32[]{:S(2)}, u32[]{:S(2)}) collective-permute-start(bf16[16,24,128]{2,1,0:T(8,128)(2,1)S(1)} %collective-permute-done.refs_7_), channel_id=1, source_target_pairs={{0,6},{1,7},{2,4},{3,5},{4,2},{5,3},{6,0},{7,1},{8,14},{9,15},{10,... | collective-permute-start | bytes 294920 | tf_op jit(solution)/shard_map/ppermute | solution.py:24
  12.3 5.7 %collective-permute-start.3 = (bf16[16,24,128]{2,1,0:T(8,128)(2,1)S(1)}, bf16[16,24,128]{2,1,0:T(8,128)(2,1)S(1)}, u32[]{:S(2)}, u32[]{:S(2)}) collective-permute-start(bf16[16,24,128]{2,1,0:T(8,128)(2,1)S(1)} %collective-permute-done.refs_7_), channel_id=1, source_target_pairs={{0,4},{1,5},{2,6},{3,7},{4,0},{5,1},{6,2},{7,3},{8,12},{9,13},{10,... | collective-permute-start | bytes 294920 | tf_op jit(solution)/shard_map/ppermute | solution.py:24
  13.6 4.6 %collective-permute-start.5 = (bf16[16,24,128]{2,1,0:T(8,128)(2,1)S(1)}, bf16[16,24,128]{2,1,0:T(8,128)(2,1)S(1)}, u32[]{:S(2)}, u32[]{:S(2)}) collective-permute-start(bf16[16,24,128]{2,1,0:T(8,128)(2,1)S(1)} %collective-permute-done.refs_7_), channel_id=1, source_target_pairs={{0,2},{1,3},{2,0},{3,1},{4,6},{5,7},{6,4},{7,5},{8,10},{9,11},{10,... | collective-permute-start | bytes 294920 | tf_op jit(solution)/shard_map/ppermute | solution.py:24
  14.3 4.2 %collective-permute-start.7 = (bf16[16,24,128]{2,1,0:T(8,128)(2,1)S(1)}, bf16[16,24,128]{2,1,0:T(8,128)(2,1)S(1)}, u32[]{:S(2)}, u32[]{:S(2)}) collective-permute-start(bf16[16,24,128]{2,1,0:T(8,128)(2,1)S(1)} %collective-permute-done.refs_7_), channel_id=1, source_target_pairs={{0,1},{1,0},{2,3},{3,2},{4,5},{5,4},{6,7},{7,6},{8,9},{9,8},{10,11... | collective-permute-start | bytes 294920 | tf_op jit(solution)/shard_map/ppermute | solution.py:24
  14.3 4.4 %collective-permute-start.9 = (bf16[16,24,128]{2,1,0:T(8,128)(2,1)S(1)}, bf16[16,24,128]{2,1,0:T(8,128)(2,1)S(1)}, u32[]{:S(2)}, u32[]{:S(2)}) collective-permute-start(bf16[16,24,128]{2,1,0:T(8,128)(2,1)S(1)} %collective-permute-done.8.refs_9_), channel_id=1, source_target_pairs={{0,1},{1,0},{2,3},{3,2},{4,5},{5,4},{6,7},{7,6},{8,9},{9,8},{10,11... | collective-permute-start | bytes 294920 | tf_op jit(solution)/shard_map/ppermute | solution.py:24
  16.3 2.9 %collective-permute-start.11 = (bf16[16,24,128]{2,1,0:T(8,128)(2,1)S(1)}, bf16[16,24,128]{2,1,0:T(8,128)(2,1)S(1)}, u32[]{:S(2)}, u32[]{:S(2)}) collective-permute-start(bf16[16,24,128]{2,1,0:T(8,128)(2,1)S(1)} %collective-permute-done.10.refs_11_), channel_id=1, source_target_pairs={{0,1},{1,0},{2,3},{3,2},{4,5},{5,4},{6,7},{7,6},{8,9},{9,8},{10,11... | collective-permute-start | bytes 294920 | tf_op jit(solution)/shard_map/ppermute | solution.py:24
  18.0 1.3 %collective-permute-start.13 = (bf16[16,24,128]{2,1,0:T(8,128)(2,1)S(1)}, bf16[16,24,128]{2,1,0:T(8,128)(2,1)S(1)}, u32[]{:S(2)}, u32[]{:S(2)}) collective-permute-start(bf16[16,24,128]{2,1,0:T(8,128)(2,1)S(1)} %collective-permute-done.12.refs_13_), channel_id=1, source_target_pairs={{0,1},{1,0},{2,3},{3,2},{4,5},{5,4},{6,7},{7,6},{8,9},{9,8},{10,11... | collective-permute-start | bytes 294920 | tf_op jit(solution)/shard_map/ppermute | solution.py:24
  18.2 1.3 %collective-permute-start.2 = (bf16[16,24,128]{2,1,0:T(8,128)(2,1)S(1)}, bf16[16,24,128]{2,1,0:T(8,128)(2,1)S(1)}, u32[]{:S(2)}, u32[]{:S(2)}) collective-permute-start(bf16[16,24,128]{2,1,0:T(8,128)(2,1)S(1)} %collective-permute-done.1.refs_1_), channel_id=1, source_target_pairs={{0,1},{1,0},{2,3},{3,2},{4,5},{5,4},{6,7},{7,6},{8,9},{9,8},{10,11... | collective-permute-start | bytes 294920 | tf_op jit(solution)/shard_map/ppermute | solution.py:24
  18.5 1.3 %collective-permute-start.4 = (bf16[16,24,128]{2,1,0:T(8,128)(2,1)S(1)}, bf16[16,24,128]{2,1,0:T(8,128)(2,1)S(1)}, u32[]{:S(2)}, u32[]{:S(2)}) collective-permute-start(bf16[16,24,128]{2,1,0:T(8,128)(2,1)S(1)} %collective-permute-done.3.refs_3_), channel_id=1, source_target_pairs={{0,1},{1,0},{2,3},{3,2},{4,5},{5,4},{6,7},{7,6},{8,9},{9,8},{10,11... | collective-permute-start | bytes 294920 | tf_op jit(solution)/shard_map/ppermute | solution.py:24
  18.7 1.3 %collective-permute-start.6 = (bf16[16,24,128]{2,1,0:T(8,128)(2,1)S(1)}, bf16[16,24,128]{2,1,0:T(8,128)(2,1)S(1)}, u32[]{:S(2)}, u32[]{:S(2)}) collective-permute-start(bf16[16,24,128]{2,1,0:T(8,128)(2,1)S(1)} %collective-permute-done.5.refs_5_), channel_id=1, source_target_pairs={{0,1},{1,0},{2,3},{3,2},{4,5},{5,4},{6,7},{7,6},{8,9},{9,8},{10,11... | collective-permute-start | bytes 294920 | tf_op jit(solution)/shard_map/ppermute | solution.py:24
  19.0 1.0 %copy-start = (bf16[16,4,2,3,128]{4,2,3,1,0:T(2,128)(2,1)S(1)}, bf16[16,4,2,3,128]{4,2,3,1,0:T(2,128)(2,1)}, u32[]{:S(2)}) copy-start(bf16[16,4,2,3,128]{4,2,3,1,0:T(2,128)(2,1)} %param.6) | copy-start | bytes 294916

commit v3 on v2

v3 whole, which is shorter than its diff:
```python
import functools
import math

import jax
import jax.numpy as jnp
from jax import lax
from jax.experimental import pallas as pl
from jax.experimental.pallas import tpu as pltpu
from jax.sharding import PartitionSpec as P

PERIOD = 48
AXIS = "space"
GATHER_BYTES = 8 << 20
VMEM_LIMIT = 48 << 20


def phases(indices):
    angle = 2.0 * math.pi / PERIOD * indices.astype(jnp.float32)
    return (jnp.cos(angle), jnp.sin(angle))


def swap(block, offset):
    size = lax.axis_size(AXIS)
    return lax.ppermute(block, AXIS, [(i, i ^ offset) for i in range(size)])


def step(held, offset):
    return [(swap(array, offset), tuple(k ^ offset for k in owners)) for array, owners in held]


def stacked(held):
    return jnp.stack([array for array, _ in held], 0), sum((owners for _, owners in held), ())


def swapped(values):
    other = lax.broadcasted_iota(jnp.int32, (8, values.shape[1]), 0) ^ 1
    pieces = [jnp.take_along_axis(values[i : i + 8], other, axis=0) for i in range(0, values.shape[0], 8)]
    return jnp.concatenate(pieces, 0)


def tile_terms(left, right, left_turned, right_turned, tile):
    n = tile.shape[0]
    dot = functools.partial(jnp.dot, preferred_element_type=jnp.float32)
    turned = jnp.concatenate([-tile[:, n:], tile[:, :n]], 1)
    first = dot(left, jnp.concatenate([tile, turned], 0))
    second = dot(tile, jnp.concatenate([right, right_turned], 0))
    fr, fi, sr, si = first[:, :n], first[:, n:], second[:, :n], second[:, n:]
    return (
        jnp.sum(fr * sr + fi * si, axis=0, keepdims=True),
        jnp.sum(fi * sr - fr * si, axis=0, keepdims=True),
    )


def pick(sink_ref, sep_ref, diagram_ref, i, times):
    sink = sink_ref[i]
    source = lax.rem(lax.rem(sink - sep_ref[i], times) + times, times)
    flipped = diagram_ref[i] == 1
    return jnp.where(flipped, source, sink), jnp.where(flipped, sink, source), jnp.where(flipped, -1.0, 1.0)


def contract(ids, plain, turned, tiles_ref, re_ref, im_ref, corr_ref):
    count = tiles_ref.shape[0]

    def one(i, carry):
        a, b, sign = pick(*ids, i, plain.shape[0])
        re, im = tile_terms(plain[a], plain[b], turned[a], turned[b], tiles_ref[i])
        re_ref[pl.ds(i, 1), :] = re
        im_ref[pl.ds(i, 1), :] = im * sign
        return carry

    lax.fori_loop(0, count, one, 0, unroll=math.gcd(count, 16))
    corr_ref[0, :] = jnp.sum(re_ref[...], axis=1)
    corr_ref[1, :] = jnp.sum(im_ref[...], axis=1)


def block_list(refs, pieces):
    loads, owners = [], []
    for ref, piece in zip(refs, pieces):
        for i, k in enumerate(piece):
            loads.append(functools.partial(lambda r, t: r[t], ref if len(piece) == 1 else ref.at[i]))
            owners.append(k)
    return loads, owners


def fill_tables(owners, rows, me, phase_refs, tables):
    n, sites = tables[0].shape[-1], phase_refs[0].shape[1]
    row = lax.broadcasted_iota(jnp.int32, (rows, n), 0)
    sign = jnp.where(row % 2 == 0, -1.0, 1.0)
    for j, k in enumerate(owners):
        for source, plain, signed in zip(phase_refs, tables[:2], tables[2:]):
            line = source[pl.ds(me ^ k, 1), :]
            value = jnp.broadcast_to(line[:, :1], (rows, n))
            for q in range(1, sites):
                value = jnp.where(row >= q * (rows // sites), jnp.broadcast_to(line[:, q : q + 1], (rows, n)), value)
            plain[pl.ds(j * rows, rows)] = value
            signed[pl.ds(j * rows, rows)] = value * sign


def slice_values(loads, t, tables):
    cosine, sine, cosine_signed, sine_signed = tables
    vecs = jnp.concatenate([load(t).astype(jnp.float32) for load in loads], 0)
    other = swapped(vecs)
    first = cosine[...] * vecs + sine_signed[...] * other
    second = sine[...] * vecs - cosine_signed[...] * other
    return lax.dot_general(
        vecs.astype(jnp.bfloat16),
        jnp.concatenate([first.astype(jnp.bfloat16), second.astype(jnp.bfloat16)], 1),
        (((0,), (0,)), ((), ())),
        preferred_element_type=jnp.float32,
    )


def fused_kernel(pieces, cos_ref, sin_ref, sink_any, sep_any, diagram_any, own_any, tiles_ref, *refs):
    held = refs[: len(pieces)]
    elemental_any, corr_ref, plain, turned, re_ref, im_ref, block_ref, out_ref, *rest = refs[len(pieces) :]
    ids, sems, tables = rest[:3], rest[3], rest[4:]
    loads_in = [
        pltpu.make_async_copy(source, target, sems.at[i])
        for i, (source, target) in enumerate(zip((own_any, sink_any, sep_any, diagram_any), (block_ref, *ids)))
    ]
    for load in loads_in:
        load.start()
    loads, owners = block_list((block_ref, *held), ((0,), *pieces))
    times, rows, n = block_ref.shape
    me = lax.axis_index(AXIS).astype(jnp.int32)
    fill_tables(owners, rows, me, (cos_ref, sin_ref), tables)
    loads_in[0].wait()
    for t in range(times):
        value = slice_values(loads, t, tables).astype(jnp.bfloat16)
        plain[t] = value
        turned[t] = jnp.concatenate([-value[:, n:], value[:, :n]], 1)
    own = plain[me]
    out_ref[0, 0] = own[:, :n]
    out_ref[0, 1] = own[:, n:]
    store = pltpu.make_async_copy(out_ref, elemental_any, sems.at[4])
    store.start()
    for load in loads_in[1:]:
        load.wait()
    contract(ids, plain, turned, tiles_ref, re_ref, im_ref, corr_ref)
    store.wait()


def widened(perambulator):
    return jnp.concatenate([perambulator[:, 0], perambulator[:, 1]], 2)


def by_gathered_vectors(eigvecs, phase_index, perambulator, tile_sink, tile_sep, tile_diagram):
    times, sites, parts, colors, n = eigvecs.shape
    devices = lax.axis_size(AXIS)
    rows = sites * colors * parts
    block = eigvecs.transpose(0, 1, 3, 2, 4).reshape(times, rows, n)
    own = (block, (0,))
    [far] = step([own], 8)
    [d], [b], [y] = step([own], 6), step([own], 4), step([own], 2)
    [fd], [fb], [fy] = step([far], 6), step([far], 4), step([far], 2)
    near = stacked([far, d, b, y])
    so, sn = step([own, near], 1)
    rest = stacked([fd, fb, fy])
    [sr] = step([rest], 1)
    held = [rest, sn, sr, far, d, b, y, so]
    cosine, sine = (value.reshape(devices, sites) for value in phases(phase_index))
    tiles = perambulator.shape[0]
    vmem = pl.BlockSpec(memory_space=pltpu.VMEM)
    anywhere = pl.BlockSpec(memory_space=pl.ANY)
    elemental, correlator = pl.pallas_call(
        functools.partial(fused_kernel, [owners for _, owners in held]),
        out_shape=(
            jax.ShapeDtypeStruct((1, 2, n, n), jnp.bfloat16),
            jax.ShapeDtypeStruct((2, tiles), jnp.float32),
        ),
        in_specs=[vmem] * 2 + [anywhere] * 4 + [vmem] * (1 + len(held)),
        out_specs=(anywhere, vmem),
        scratch_shapes=[
            pltpu.VMEM((times, n, 2 * n), jnp.bfloat16),
            pltpu.VMEM((times, n, 2 * n), jnp.bfloat16),
            pltpu.VMEM((tiles, n), jnp.float32),
            pltpu.VMEM((tiles, n), jnp.float32),
            pltpu.VMEM(block.shape, block.dtype),
            pltpu.VMEM((1, 2, n, n), jnp.bfloat16),
            *[pltpu.SMEM((tiles,), jnp.int32)] * 3,
            pltpu.SemaphoreType.DMA((5,)),
        ]
        + [pltpu.VMEM((devices * rows, n), jnp.float32)] * 4,
        compiler_params=pltpu.CompilerParams(vmem_limit_bytes=VMEM_LIMIT),
    )(cosine, sine, tile_sink[:, 0], tile_sep, tile_diagram, block, widened(perambulator), *[array for array, _ in held])
    return elemental, correlator.T


def contract_kernel(sink_ref, sep_ref, diagram_ref, elementals_ref, tiles_ref, corr_ref, plain, turned, re_ref, im_ref):
    times = elementals_ref.shape[0]

    def widen(t, carry):
        re, im = elementals_ref[t, 0], elementals_ref[t, 1]
        plain[t] = jnp.concatenate([re, im], 1)
        turned[t] = jnp.concatenate([-im, re], 1)
        return carry

    lax.fori_loop(0, times, widen, 0)
    contract((sink_ref, sep_ref, diagram_ref), plain, turned, tiles_ref, re_ref, im_ref, corr_ref)


def by_gathered_elementals(eigvecs, phase_index, perambulator, tile_sink, tile_sep, tile_diagram):
    cosine, sine = phases(phase_index)
    vecs = lax.all_to_all(eigvecs, AXIS, split_axis=0, concat_axis=1, tiled=True)[0].astype(jnp.float32)
    cosine, sine = cosine[:, None, None], sine[:, None, None]
    first = cosine * vecs[:, 0] - sine * vecs[:, 1]
    second = sine * vecs[:, 0] + cosine * vecs[:, 1]
    right = jnp.stack([jnp.stack([first, second], -2), jnp.stack([second, -first], -2)], -4).astype(jnp.bfloat16)
    value = jnp.einsum("spck,spcol->okl", vecs.astype(jnp.bfloat16), right, preferred_element_type=jnp.float32)
    elemental = value.astype(jnp.bfloat16)[None]
    gathered = lax.all_gather(elemental, AXIS, axis=0, tiled=True)
    times, _, n, _ = gathered.shape
    tiles = perambulator.shape[0]
    smem = pl.BlockSpec(memory_space=pltpu.SMEM)
    vmem = pl.BlockSpec(memory_space=pltpu.VMEM)
    correlator = pl.pallas_call(
        contract_kernel,
        out_shape=jax.ShapeDtypeStruct((2, tiles), jnp.float32),
        in_specs=[smem] * 3 + [vmem] * 2,
        out_specs=vmem,
        scratch_shapes=[
            pltpu.VMEM((times, n, 2 * n), jnp.bfloat16),
            pltpu.VMEM((times, n, 2 * n), jnp.bfloat16),
            pltpu.VMEM((tiles, n), jnp.float32),
            pltpu.VMEM((tiles, n), jnp.float32),
        ],
        compiler_params=pltpu.CompilerParams(vmem_limit_bytes=VMEM_LIMIT),
    )(tile_sink[:, 0], tile_sep, tile_diagram, gathered, widened(perambulator))
    return elemental, correlator.T


def local(eigvecs, *rest):
    devices = lax.axis_size(AXIS)
    small = eigvecs.size * eigvecs.dtype.itemsize * devices <= GATHER_BYTES
    if small and devices & (devices - 1) == 0:
        return by_gathered_vectors(eigvecs, *rest)
    return by_gathered_elementals(eigvecs, *rest)


def solution(mesh):
    return jax.shard_map(
        local,
        mesh=mesh,
        in_specs=(
            P("groups", "space", None, None, None),
            P("groups"),
            P(("groups", "space"), None, None, None),
            P(("groups", "space"), None),
            P(("groups", "space")),
            P(("groups", "space")),
        ),
        out_specs=(P(("groups", "space"), None, None, None), P(("groups", "space"), None)),
        check_vma=False,
    )
```

time: 24 us -> 23.5 us (0.979)
  waiting for transfers between devices: 4.45 us -> 6.45 us
  starting transfers between devices: 13.3 us -> 11.4 us
  local copies, waits for them, and re-layouts: 1.32 us -> 0.29 us
  other arithmetic: 0.2 us -> 0.92 us
  Pallas kernels: 3.8 us -> 3.43 us
    ppermute x15 -> x10, waiting for transfers between devices: 4.45 us -> 6.45 us  [swap(): return lax.ppermute(block, AXIS, [(i, i ^ offset) for i in range(size)])]
    ppermute x15 -> x10, starting transfers between devices: 13.3 us -> 11.4 us  [swap(): return lax.ppermute(block, AXIS, [(i, i ^ offset) for i in range(size)])]
    squeeze x1, local copies, waits for them, and re-layouts: 1.3 us -> 0.1 us  [widened(): return jnp.concatenate([perambulator[:, 0], perambulator[:, 1]], 2)]
    sin x1, other arithmetic: 0.04 us -> 0.7 us  [phases(): return (jnp.cos(angle), jnp.sin(angle))]
    pallas_call x1, Pallas kernels: 3.8 us -> 3.43 us  [by_gathered_vectors(): pl.pallas_call(functools.partial(fused_kernel, [owners for _, owners in h...]
  transfers between devices with their start and end apart: 15 -> 10, of which waited for: 9 -> 5; matrix products, arithmetic and copies ran while one was open for 6% -> 5% of each run, Pallas kernels for 0% -> 0%
where the time goes in v3:
time: 23.5 us; the launch traced here: 23.3 us
  starting transfers between devices  11.4 us (49%)
  waiting for transfers between devices  6.45 us (27%)
  Pallas kernels  3.43 us (15%)
  other arithmetic  0.92 us (4%)
  between operations  0.75 us (3%)
  local copies, waits for them, and re-layouts  0.29 us (1%)
    ppermute x10, starting transfers between devices, swap(): return lax.ppermute(block, AXIS, [(i, i ^ offset) for i in range(size)])  11.4 us
    ppermute x10, waiting for transfers between devices, swap(): return lax.ppermute(block, AXIS, [(i, i ^ offset) for i in range(size)])  6.45 us
    pallas_call x1, Pallas kernels, by_gathered_vectors(): pl.pallas_call(functools.partial(fused_kernel, [owners for _, owners in h...  3.43 us
    sin x1, other arithmetic, phases(): return (jnp.cos(angle), jnp.sin(angle))  0.7 us
  transfers between devices with their start and end apart: 10, of which 5 were waited for; matrix products, arithmetic and copies ran while one was open for 5% of the time, Pallas kernels for 0%

profile of v3, /device:TPU:0, one launch (start us, length us, event | category | flops | bytes accessed | tf_op | source)
XLA Modules:
  0.0 23.3 jit_solution(16446930471628408576)
XLA Ops:
  0.6 4.1 %collective-permute-start = (bf16[16,24,128]{2,1,0:T(8,128)(2,1)}, bf16[16,24,128]{2,1,0:T(8,128)(2,1)S(1)}, u32[]{:S(2)}, u32[]{:S(2)}) collective-permute-start(bf16[16,24,128]{2,1,0:T(8,128)(2,1)} %bitcast.24), channel_id=1, source_target_pairs={{0,8},{1,9},{2,10},{3,11},{4,12},{5,13},{6,14},{7,15},{8,0},{9,1},... | collective-permute-start | bytes 294920 | tf_op jit(solution)/shard_map/ppermute | solution.py:24
  4.7 1.5 %collective-permute-start.6 = (bf16[16,24,128]{2,1,0:T(8,128)(2,1)}, bf16[16,24,128]{2,1,0:T(8,128)(2,1)S(1)}, u32[]{:S(2)}, u32[]{:S(2)}) collective-permute-start(bf16[16,24,128]{2,1,0:T(8,128)(2,1)} %bitcast.25), channel_id=1, source_target_pairs={{0,2},{1,3},{2,0},{3,1},{4,6},{5,7},{6,4},{7,5},{8,10},{9,11},{10,... | collective-permute-start | bytes 294920 | tf_op jit(solution)/shard_map/ppermute | solution.py:24
  6.3 1.6 %collective-permute-start.5 = (bf16[16,24,128]{2,1,0:T(8,128)(2,1)}, bf16[16,24,128]{2,1,0:T(8,128)(2,1)S(1)}, u32[]{:S(2)}, u32[]{:S(2)}) collective-permute-start(bf16[16,24,128]{2,1,0:T(8,128)(2,1)} %bitcast.26), channel_id=1, source_target_pairs={{0,4},{1,5},{2,6},{3,7},{4,0},{5,1},{6,2},{7,3},{8,12},{9,13},{10,... | collective-permute-start | bytes 294920 | tf_op jit(solution)/shard_map/ppermute | solution.py:24
  7.8 0.4 %collective-permute-start.4 = (bf16[16,24,128]{2,1,0:T(8,128)(2,1)}, bf16[16,24,128]{2,1,0:T(8,128)(2,1)S(1)}, u32[]{:S(2)}, u32[]{:S(2)}) collective-permute-start(bf16[16,24,128]{2,1,0:T(8,128)(2,1)} %bitcast.27), channel_id=1, source_target_pairs={{0,6},{1,7},{2,4},{3,5},{4,2},{5,3},{6,0},{7,1},{8,14},{9,15},{10,... | collective-permute-start | bytes 294920 | tf_op jit(solution)/shard_map/ppermute | solution.py:24
  8.2 0.7 %fusion = (f32[64]{0:T(128)S(1)}, f32[64]{0:T(128)S(1)}) fusion(s32[64]{0:T(128)} %param.7), kind=kLoop, calls=%fused_computation.6 | loop fusion | flops 128 | bytes 768 | tf_op jit(solution)/shard_map/sin | solution.py:19
  8.9 0.1 reshape.13.cos_ref
  9.0 0.1 reshape.14.sin_ref
  9.1 0.9 %collective-permute-done.refs_3_ = bf16[16,24,128]{2,1,0:T(8,128)(2,1)S(1)} collective-permute-done((bf16[16,24,128]{2,1,0:T(8,128)(2,1)}, bf16[16,24,128]{2,1,0:T(8,128)(2,1)S(1)}, u32[]{:S(2)}, u32[]{:S(2)}) %collective-permute-start) | collective-permute-done | bytes 98336 | tf_op jit(solution)/shard_map/ppermute | solution.py:24
  10.0 1.4 %collective-permute-start.3 = (bf16[16,24,128]{2,1,0:T(8,128)(2,1)S(1)}, bf16[16,24,128]{2,1,0:T(8,128)(2,1)S(1)}, u32[]{:S(2)}, u32[]{:S(2)}) collective-permute-start(bf16[16,24,128]{2,1,0:T(8,128)(2,1)S(1)} %collective-permute-done.refs_3_), channel_id=1, source_target_pairs={{0,2},{1,3},{2,0},{3,1},{4,6},{5,7},{6,4},{7,5},{8,10},{9,11},{10,... | collective-permute-start | bytes 294920 | tf_op jit(solution)/shard_map/ppermute | solution.py:24
  11.4 0.9 %collective-permute-start.2 = (bf16[16,24,128]{2,1,0:T(8,128)(2,1)S(1)}, bf16[16,24,128]{2,1,0:T(8,128)(2,1)S(1)}, u32[]{:S(2)}, u32[]{:S(2)}) collective-permute-start(bf16[16,24,128]{2,1,0:T(8,128)(2,1)S(1)} %collective-permute-done.refs_3_), channel_id=1, source_target_pairs={{0,4},{1,5},{2,6},{3,7},{4,0},{5,1},{6,2},{7,3},{8,12},{9,13},{10,... | collective-permute-start | bytes 294920 | tf_op jit(solution)/shard_map/ppermute | solution.py:24
  12.3 1.4 %collective-permute-start.1 = (bf16[16,24,128]{2,1,0:T(8,128)(2,1)S(1)}, bf16[16,24,128]{2,1,0:T(8,128)(2,1)S(1)}, u32[]{:S(2)}, u32[]{:S(2)}) collective-permute-start(bf16[16,24,128]{2,1,0:T(8,128)(2,1)S(1)} %collective-permute-done.refs_3_), channel_id=1, source_target_pairs={{0,6},{1,7},{2,4},{3,5},{4,2},{5,3},{6,0},{7,1},{8,14},{9,15},{10,... | collective-permute-start | bytes 294920 | tf_op jit(solution)/shard_map/ppermute | solution.py:24
  13.7 0.1 pad_maximum_fusion.1
  13.7 0.1 collective-permute-start.7
  13.8 1.8 %collective-permute-done.3 = bf16[16,24,128]{2,1,0:T(8,128)(2,1)S(1)} collective-permute-done((bf16[16,24,128]{2,1,0:T(8,128)(2,1)S(1)}, bf16[16,24,128]{2,1,0:T(8,128)(2,1)S(1)}, u32[]{:S(2)}, u32[]{:S(2)}) %collective-permute-start.3) | collective-permute-done | bytes 98336 | tf_op jit(solution)/shard_map/ppermute | solution.py:24
  15.7 1.2 %collective-permute-done.2 = bf16[16,24,128]{2,1,0:T(8,128)(2,1)S(1)} collective-permute-done((bf16[16,24,128]{2,1,0:T(8,128)(2,1)S(1)}, bf16[16,24,128]{2,1,0:T(8,128)(2,1)S(1)}, u32[]{:S(2)}, u32[]{:S(2)}) %collective-permute-start.2) | collective-permute-done | bytes 98336 | tf_op jit(solution)/shard_map/ppermute | solution.py:24
  16.9 1.3 %collective-permute-done.1 = bf16[16,24,128]{2,1,0:T(8,128)(2,1)S(1)} collective-permute-done((bf16[16,24,128]{2,1,0:T(8,128)(2,1)S(1)}, bf16[16,24,128]{2,1,0:T(8,128)(2,1)S(1)}, u32[]{:S(2)}, u32[]{:S(2)}) %collective-permute-start.1) | collective-permute-done | bytes 98336 | tf_op jit(solution)/shard_map/ppermute | solution.py:24
  18.2 0.1 collective-permute-start.8
  18.3 0.1 slice_bitcast_fusion.1
  18.4 0.0 copy-start
  18.4 0.0 copy-start.1
  18.4 0.0 copy-start.2
  18.4 0.1 pad_maximum_fusion.tiles_ref
  18.6 1.2 %collective-permute-done.8.refs_2_ = bf16[3,16,24,128]{3,2,1,0:T(8,128)(2,1)S(1)} collective-permute-done((bf16[3,16,24,128]{3,2,1,0:T(8,128)(2,1)S(1)}, bf16[3,16,24,128]{3,2,1,0:T(8,128)(2,1)S(1)}, u32[]{:S(2)}, u32[]{:S(2)}) %collective-permute-start.8) | collective-permute-done | bytes 294944 | tf_op jit(solution)/shard_map/ppermute | solution.py:24
  19.9 3.4 %shard_map.77 = (bf16[1,2,128,128]{3,2,1,0:T(8,128)(2,1)}, f32[2,16]{1,0:T(2,128)}) custom-call(f32[16,4]{1,0:T(8,128)S(1)} %reshape.13.cos_ref, f32[16,4]{1,0:T(8,128)S(1)} %reshape.14.sin_ref, s32[16]{0:T(128)S(1)} %bitcast.30, s32[16]{0:T(128)S(1)} %copy-done.2, s32[16]{0:T(128)S(1)} %copy-done.3, bf16[16,24,128]{2,1,0:T(8,128)(2,1)S(1)} %bitcast.29, ...), custom_call_target="tpu_custom_call" | custom-call | tf_op jit(solution)/shard_map/pallas_call | solution.py:165
  (14 shorter events, 0.1 us)
Async XLA Ops:
  0.6 17.6 %copy-start.4 = (bf16[16,2,128,128]{3,2,1,0:T(8,128)(2,1)S(1)}, bf16[16,2,128,128]{3,2,1,0:T(8,128)(2,1)}, u32[]{:S(2)}) copy-start(bf16[16,2,128,128]{3,2,1,0:T(8,128)(2,1)} %param.8) | copy-start | bytes 3145732
  0.6 9.3 %collective-permute-start = (bf16[16,24,128]{2,1,0:T(8,128)(2,1)}, bf16[16,24,128]{2,1,0:T(8,128)(2,1)S(1)}, u32[]{:S(2)}, u32[]{:S(2)}) collective-permute-start(bf16[16,24,128]{2,1,0:T(8,128)(2,1)} %bitcast.24), channel_id=1, source_target_pairs={{0,8},{1,9},{2,10},{3,11},{4,12},{5,13},{6,14},{7,15},{8,0},{9,1},... | collective-permute-start | bytes 294920 | tf_op jit(solution)/shard_map/ppermute | solution.py:24
  4.7 6.6 %collective-permute-start.6 = (bf16[16,24,128]{2,1,0:T(8,128)(2,1)}, bf16[16,24,128]{2,1,0:T(8,128)(2,1)S(1)}, u32[]{:S(2)}, u32[]{:S(2)}) collective-permute-start(bf16[16,24,128]{2,1,0:T(8,128)(2,1)} %bitcast.25), channel_id=1, source_target_pairs={{0,2},{1,3},{2,0},{3,1},{4,6},{5,7},{6,4},{7,5},{8,10},{9,11},{10,... | collective-permute-start | bytes 294920 | tf_op jit(solution)/shard_map/ppermute | solution.py:24
  6.3 6.0 %collective-permute-start.5 = (bf16[16,24,128]{2,1,0:T(8,128)(2,1)}, bf16[16,24,128]{2,1,0:T(8,128)(2,1)S(1)}, u32[]{:S(2)}, u32[]{:S(2)}) collective-permute-start(bf16[16,24,128]{2,1,0:T(8,128)(2,1)} %bitcast.26), channel_id=1, source_target_pairs={{0,4},{1,5},{2,6},{3,7},{4,0},{5,1},{6,2},{7,3},{8,12},{9,13},{10,... | collective-permute-start | bytes 294920 | tf_op jit(solution)/shard_map/ppermute | solution.py:24
  7.8 5.8 %collective-permute-start.4 = (bf16[16,24,128]{2,1,0:T(8,128)(2,1)}, bf16[16,24,128]{2,1,0:T(8,128)(2,1)S(1)}, u32[]{:S(2)}, u32[]{:S(2)}) collective-permute-start(bf16[16,24,128]{2,1,0:T(8,128)(2,1)} %bitcast.27), channel_id=1, source_target_pairs={{0,6},{1,7},{2,4},{3,5},{4,2},{5,3},{6,0},{7,1},{8,14},{9,15},{10,... | collective-permute-start | bytes 294920 | tf_op jit(solution)/shard_map/ppermute | solution.py:24
  8.2 10.4 %collective-permute-start.9 = (bf16[16,24,128]{2,1,0:T(8,128)(2,1)}, bf16[16,24,128]{2,1,0:T(8,128)(2,1)S(1)}, u32[]{:S(2)}, u32[]{:S(2)}) collective-permute-start(bf16[16,24,128]{2,1,0:T(8,128)(2,1)} %bitcast.28), channel_id=1, source_target_pairs={{0,1},{1,0},{2,3},{3,2},{4,5},{5,4},{6,7},{7,6},{8,9},{9,8},{10,11... | collective-permute-start | bytes 294920 | tf_op jit(solution)/shard_map/ppermute | solution.py:24
  10.0 5.7 %collective-permute-start.3 = (bf16[16,24,128]{2,1,0:T(8,128)(2,1)S(1)}, bf16[16,24,128]{2,1,0:T(8,128)(2,1)S(1)}, u32[]{:S(2)}, u32[]{:S(2)}) collective-permute-start(bf16[16,24,128]{2,1,0:T(8,128)(2,1)S(1)} %collective-permute-done.refs_3_), channel_id=1, source_target_pairs={{0,2},{1,3},{2,0},{3,1},{4,6},{5,7},{6,4},{7,5},{8,10},{9,11},{10,... | collective-permute-start | bytes 294920 | tf_op jit(solution)/shard_map/ppermute | solution.py:24
  11.4 5.5 %collective-permute-start.2 = (bf16[16,24,128]{2,1,0:T(8,128)(2,1)S(1)}, bf16[16,24,128]{2,1,0:T(8,128)(2,1)S(1)}, u32[]{:S(2)}, u32[]{:S(2)}) collective-permute-start(bf16[16,24,128]{2,1,0:T(8,128)(2,1)S(1)} %collective-permute-done.refs_3_), channel_id=1, source_target_pairs={{0,4},{1,5},{2,6},{3,7},{4,0},{5,1},{6,2},{7,3},{8,12},{9,13},{10,... | collective-permute-start | bytes 294920 | tf_op jit(solution)/shard_map/ppermute | solution.py:24
  12.3 5.9 %collective-permute-start.1 = (bf16[16,24,128]{2,1,0:T(8,128)(2,1)S(1)}, bf16[16,24,128]{2,1,0:T(8,128)(2,1)S(1)}, u32[]{:S(2)}, u32[]{:S(2)}) collective-permute-start(bf16[16,24,128]{2,1,0:T(8,128)(2,1)S(1)} %collective-permute-done.refs_3_), channel_id=1, source_target_pairs={{0,6},{1,7},{2,4},{3,5},{4,2},{5,3},{6,0},{7,1},{8,14},{9,15},{10,... | collective-permute-start | bytes 294920 | tf_op jit(solution)/shard_map/ppermute | solution.py:24
  13.7 4.9 %collective-permute-start.7 = (bf16[4,16,24,128]{3,2,1,0:T(8,128)(2,1)S(1)}, bf16[4,16,24,128]{3,2,1,0:T(8,128)(2,1)S(1)}, u32[]{:S(2)}, u32[]{:S(2)}) collective-permute-start(bf16[4,16,24,128]{3,2,1,0:T(8,128)(2,1)S(1)} %pad_maximum_fusion.1), channel_id=1, source_target_pairs={{0,1},{1,0},{2,3},{3,2},{4,5},{5,4},{6,7},{7,6},{8,9},{9,8},{10,11... | collective-permute-start | bytes 1179656 | tf_op jit(solution)/shard_map/ppermute | solution.py:24
  18.2 1.6 %collective-permute-start.8 = (bf16[3,16,24,128]{3,2,1,0:T(8,128)(2,1)S(1)}, bf16[3,16,24,128]{3,2,1,0:T(8,128)(2,1)S(1)}, u32[]{:S(2)}, u32[]{:S(2)}) collective-permute-start(bf16[3,16,24,128]{3,2,1,0:T(8,128)(2,1)S(1)} %pad_maximum_fusion.2.refs_0_), channel_id=1, source_target_pairs={{0,1},{1,0},{2,3},{3,2},{4,5},{5,4},{6,7},{7,6},{8,9},{9,8},{10,11... | collective-permute-start | bytes 884744 | tf_op jit(solution)/shard_map/ppermute | solution.py:24
  18.4 1.5 %copy-start = (bf16[16,4,2,3,128]{4,2,3,1,0:T(2,128)(2,1)S(1)}, bf16[16,4,2,3,128]{4,2,3,1,0:T(2,128)(2,1)}, u32[]{:S(2)}) copy-start(bf16[16,4,2,3,128]{4,2,3,1,0:T(2,128)(2,1)} %param.6) | copy-start | bytes 294916
  18.4 1.4 %copy-start.1 = (s32[16,1]{0,1:T(1,128)S(1)}, s32[16,1]{0,1:T(1,128)}, u32[]{:S(2)}) copy-start(s32[16,1]{0,1:T(1,128)} %param.9) | copy-start | bytes 196
  18.4 1.4 %copy-start.2 = (s32[16]{0:T(128)S(1)}, s32[16]{0:T(128)}, u32[]{:S(2)}) copy-start(s32[16]{0:T(128)} %sep_any.1) | copy-start | bytes 196
  18.4 1.4 %copy-start.3 = (s32[16]{0:T(128)S(1)}, s32[16]{0:T(128)}, u32[]{:S(2)}) copy-start(s32[16]{0:T(128)} %diagram_any.1) | copy-start | bytes 196

commit v4 on v3

--- a/solution.py
+++ b/solution.py
@@ -110,26 +110,37 @@
     )
 
 
-def fused_kernel(pieces, cos_ref, sin_ref, sink_any, sep_any, diagram_any, own_any, tiles_ref, *refs):
-    held = refs[: len(pieces)]
-    elemental_any, corr_ref, plain, turned, re_ref, im_ref, block_ref, out_ref, *rest = refs[len(pieces) :]
-    ids, sems, tables = rest[:3], rest[3], rest[4:]
+def early_kernel(pieces, later, *refs):
+    held, refs = refs[: len(pieces)], refs[len(pieces) :]
+    cos_ref, sin_ref, sum_ref, later_ref, *tables = refs
+    loads, owners = block_list(held, pieces)
+    times, rows = sum_ref.shape[0], later_ref.shape[1] // len(later)
+    me = lax.axis_index(AXIS).astype(jnp.int32)
+    fill_tables(owners, rows, me, (cos_ref, sin_ref), tables)
+    fill_tables(later, rows, me, (cos_ref, sin_ref), [later_ref.at[i] for i in range(4)])
+    for t in range(times):
+        sum_ref[t] = slice_values(loads, t, tables)
+
+
+def late_kernel(pieces, *refs):
+    held, refs = refs[: len(pieces)], refs[len(pieces) :]
+    sink_any, sep_any, diagram_any, own_any, tiles_ref, sum_ref, tables_ref, *refs = refs
+    elemental_any, corr_ref, plain, turned, re_ref, im_ref, block_ref, out_ref, *ids, sems = refs
     loads_in = [
         pltpu.make_async_copy(source, target, sems.at[i])
         for i, (source, target) in enumerate(zip((own_any, sink_any, sep_any, diagram_any), (block_ref, *ids)))
     ]
     for load in loads_in:
         load.start()
-    loads, owners = block_list((block_ref, *held), ((0,), *pieces))
-    times, rows, n = block_ref.shape
-    me = lax.axis_index(AXIS).astype(jnp.int32)
-    fill_tables(owners, rows, me, (cos_ref, sin_ref), tables)
+    loads, _ = block_list((block_ref, *held), ((0,), *pieces))
+    tables = [tables_ref.at[i] for i in range(4)]
+    times, n = plain.shape[:2]
     loads_in[0].wait()
     for t in range(times):
-        value = slice_values(loads, t, tables).astype(jnp.bfloat16)
+        value = (sum_ref[t] + slice_values(loads, t, tables)).astype(jnp.bfloat16)
         plain[t] = value
         turned[t] = jnp.concatenate([-value[:, n:], value[:, :n]], 1)
-    own = plain[me]
+    own = plain[lax.axis_index(AXIS).astype(jnp.int32)]
     out_ref[0, 0] = own[:, :n]
     out_ref[0, 1] = own[:, n:]
     store = pltpu.make_async_copy(out_ref, elemental_any, sems.at[4])
@@ -157,18 +168,33 @@
     so, sn = step([own, near], 1)
     rest = stacked([fd, fb, fy])
     [sr] = step([rest], 1)
-    held = [rest, sn, sr, far, d, b, y, so]
+    early, late = [rest, sn, near, so], [sr]
     cosine, sine = (value.reshape(devices, sites) for value in phases(phase_index))
     tiles = perambulator.shape[0]
     vmem = pl.BlockSpec(memory_space=pltpu.VMEM)
     anywhere = pl.BlockSpec(memory_space=pl.ANY)
+    early_pieces = [owners for _, owners in early]
+    late_pieces = [owners for _, owners in late]
+    later = (0, *sum(late_pieces, ()))
+    total, tables = pl.pallas_call(
+        functools.partial(early_kernel, early_pieces, later),
+        out_shape=(
+            jax.ShapeDtypeStruct((times, n, 2 * n), jnp.float32),
+            jax.ShapeDtypeStruct((4, len(later) * rows, n), jnp.float32),
+        ),
+        in_specs=[vmem] * (len(early) + 2),
+        out_specs=(vmem, vmem),
+        scratch_shapes=[pltpu.VMEM((sum(map(len, early_pieces)) * rows, n), jnp.float32)] * 4,
+        compiler_params=pltpu.CompilerParams(vmem_limit_bytes=VMEM_LIMIT),
+        name="early",
+    )(*[array for array, _ in early], cosine, sine)
     elemental, correlator = pl.pallas_call(
-        functools.partial(fused_kernel, [owners for _, owners in held]),
+        functools.partial(late_kernel, late_pieces),
         out_shape=(
             jax.ShapeDtypeStruct((1, 2, n, n), jnp.bfloat16),
             jax.ShapeDtypeStruct((2, tiles), jnp.float32),
         ),
-        in_specs=[vmem] * 2 + [anywhere] * 4 + [vmem] * (1 + len(held)),
+        in_specs=[vmem] * len(late) + [anywhere] * 4 + [vmem] * 3,
         out_specs=(anywhere, vmem),
         scratch_shapes=[
             pltpu.VMEM((times, n, 2 * n), jnp.bfloat16),
@@ -179,10 +205,10 @@
             pltpu.VMEM((1, 2, n, n), jnp.bfloat16),
             *[pltpu.SMEM((tiles,), jnp.int32)] * 3,
             pltpu.SemaphoreType.DMA((5,)),
-        ]
-        + [pltpu.VMEM((devices * rows, n), jnp.float32)] * 4,
+        ],
         compiler_params=pltpu.CompilerParams(vmem_limit_bytes=VMEM_LIMIT),
-    )(cosine, sine, tile_sink[:, 0], tile_sep, tile_diagram, block, widened(perambulator), *[array for array, _ in held])
+        name="late",
+    )(*[array for array, _ in late], tile_sink[:, 0], tile_sep, tile_diagram, block, widened(perambulator), total, tables)
     return elemental, correlator.T
 
 

time: 23.5 us -> 22.3 us (0.949)
  waiting for transfers between devices: 6.45 us -> 5.03 us
  starting transfers between devices: 11.4 us -> 11.7 us
    ppermute x10, waiting for transfers between devices: 6.45 us -> 5.03 us  [swap(): return lax.ppermute(block, AXIS, [(i, i ^ offset) for i in range(size)])]
    ppermute x10, starting transfers between devices: 11.4 us -> 11.7 us  [swap(): return lax.ppermute(block, AXIS, [(i, i ^ offset) for i in range(size)])]
    pallas_call x1 -> x2, Pallas kernels: 3.43 us -> 3.45 us  [the longest x1 2.2 us: by_gathered_vectors(): pl.pallas_call(functools.partial(late_kernel, late_pieces), out_shape=(ja...]
  transfers between devices with their start and end apart: 10 -> 10, of which waited for: 5 -> 5; matrix products, arithmetic and copies ran while one was open for 5% -> 5% of each run, Pallas kernels for 0% -> 6%
where the time goes in v4:
time: 22.3 us; the launch traced here: 22.1 us
  starting transfers between devices  11.7 us (52%)
  waiting for transfers between devices  5.03 us (23%)
  Pallas kernels  3.45 us (15%)
  other arithmetic  0.92 us (4%)
  between operations  0.78 us (3%)
  local copies, waits for them, and re-layouts  0.26 us (1%)
    ppermute x10, starting transfers between devices, swap(): return lax.ppermute(block, AXIS, [(i, i ^ offset) for i in range(size)])  11.7 us
    ppermute x10, waiting for transfers between devices, swap(): return lax.ppermute(block, AXIS, [(i, i ^ offset) for i in range(size)])  5.03 us
    pallas_call x1, Pallas kernels, by_gathered_vectors(): pl.pallas_call(functools.partial(late_kernel, late_pieces), out_shape=(ja...  2.2 us
    pallas_call x1, Pallas kernels, by_gathered_vectors(): pl.pallas_call(functools.partial(early_kernel, early_pieces, later), out_...  1.26 us
    sin x1, other arithmetic, phases(): return (jnp.cos(angle), jnp.sin(angle))  0.7 us
  transfers between devices with their start and end apart: 10, of which 5 were waited for; matrix products, arithmetic and copies ran while one was open for 5% of the time, Pallas kernels for 6%

profile of v4, /device:TPU:0, one launch (start us, length us, event | category | flops | bytes accessed | tf_op | source)
XLA Modules:
  0.0 22.1 jit_solution(10049857469985354977)
XLA Ops:
  0.6 4.1 %collective-permute-start = (bf16[16,24,128]{2,1,0:T(8,128)(2,1)}, bf16[16,24,128]{2,1,0:T(8,128)(2,1)S(1)}, u32[]{:S(2)}, u32[]{:S(2)}) collective-permute-start(bf16[16,24,128]{2,1,0:T(8,128)(2,1)} %bitcast.20), channel_id=1, source_target_pairs={{0,8},{1,9},{2,10},{3,11},{4,12},{5,13},{6,14},{7,15},{8,0},{9,1},... | collective-permute-start | bytes 294920 | tf_op jit(solution)/shard_map/ppermute | solution.py:24
  4.7 2.5 %collective-permute-start.5 = (bf16[16,24,128]{2,1,0:T(8,128)(2,1)}, bf16[16,24,128]{2,1,0:T(8,128)(2,1)S(1)}, u32[]{:S(2)}, u32[]{:S(2)}) collective-permute-start(bf16[16,24,128]{2,1,0:T(8,128)(2,1)} %bitcast.21), channel_id=1, source_target_pairs={{0,6},{1,7},{2,4},{3,5},{4,2},{5,3},{6,0},{7,1},{8,14},{9,15},{10,... | collective-permute-start | bytes 294920 | tf_op jit(solution)/shard_map/ppermute | solution.py:24
  7.3 0.4 %collective-permute-start.6 = (bf16[16,24,128]{2,1,0:T(8,128)(2,1)}, bf16[16,24,128]{2,1,0:T(8,128)(2,1)S(1)}, u32[]{:S(2)}, u32[]{:S(2)}) collective-permute-start(bf16[16,24,128]{2,1,0:T(8,128)(2,1)} %bitcast.22), channel_id=1, source_target_pairs={{0,4},{1,5},{2,6},{3,7},{4,0},{5,1},{6,2},{7,3},{8,12},{9,13},{10,... | collective-permute-start | bytes 294920 | tf_op jit(solution)/shard_map/ppermute | solution.py:24
  7.7 0.5 %collective-permute-start.7 = (bf16[16,24,128]{2,1,0:T(8,128)(2,1)}, bf16[16,24,128]{2,1,0:T(8,128)(2,1)S(1)}, u32[]{:S(2)}, u32[]{:S(2)}) collective-permute-start(bf16[16,24,128]{2,1,0:T(8,128)(2,1)} %bitcast.23), channel_id=1, source_target_pairs={{0,2},{1,3},{2,0},{3,1},{4,6},{5,7},{6,4},{7,5},{8,10},{9,11},{10,... | collective-permute-start | bytes 294920 | tf_op jit(solution)/shard_map/ppermute | solution.py:24
  8.2 0.7 %fusion = (f32[64]{0:T(128)S(1)}, f32[64]{0:T(128)S(1)}) fusion(s32[64]{0:T(128)} %param.7), kind=kLoop, calls=%fused_computation.6 | loop fusion | flops 128 | bytes 768 | tf_op jit(solution)/shard_map/sin | solution.py:19
  8.9 0.1 reshape.14.refs_4_
  9.0 0.1 reshape.15.refs_5_
  9.1 0.7 %collective-permute-done = bf16[16,24,128]{2,1,0:T(8,128)(2,1)S(1)} collective-permute-done((bf16[16,24,128]{2,1,0:T(8,128)(2,1)}, bf16[16,24,128]{2,1,0:T(8,128)(2,1)S(1)}, u32[]{:S(2)}, u32[]{:S(2)}) %collective-permute-start) | collective-permute-done | bytes 98336 | tf_op jit(solution)/shard_map/ppermute | solution.py:24
  9.8 1.9 %collective-permute-start.1 = (bf16[16,24,128]{2,1,0:T(8,128)(2,1)S(1)}, bf16[16,24,128]{2,1,0:T(8,128)(2,1)S(1)}, u32[]{:S(2)}, u32[]{:S(2)}) collective-permute-start(bf16[16,24,128]{2,1,0:T(8,128)(2,1)S(1)} %collective-permute-done), channel_id=1, source_target_pairs={{0,6},{1,7},{2,4},{3,5},{4,2},{5,3},{6,0},{7,1},{8,14},{9,15},{10,... | collective-permute-start | bytes 294920 | tf_op jit(solution)/shard_map/ppermute | solution.py:24
  11.7 0.6 %collective-permute-done.5 = bf16[16,24,128]{2,1,0:T(8,128)(2,1)S(1)} collective-permute-done((bf16[16,24,128]{2,1,0:T(8,128)(2,1)}, bf16[16,24,128]{2,1,0:T(8,128)(2,1)S(1)}, u32[]{:S(2)}, u32[]{:S(2)}) %collective-permute-start.5) | collective-permute-done | bytes 98336 | tf_op jit(solution)/shard_map/ppermute | solution.py:24
  12.3 1.3 %collective-permute-start.2 = (bf16[16,24,128]{2,1,0:T(8,128)(2,1)S(1)}, bf16[16,24,128]{2,1,0:T(8,128)(2,1)S(1)}, u32[]{:S(2)}, u32[]{:S(2)}) collective-permute-start(bf16[16,24,128]{2,1,0:T(8,128)(2,1)S(1)} %collective-permute-done), channel_id=1, source_target_pairs={{0,4},{1,5},{2,6},{3,7},{4,0},{5,1},{6,2},{7,3},{8,12},{9,13},{10,... | collective-permute-start | bytes 294920 | tf_op jit(solution)/shard_map/ppermute | solution.py:24
  13.6 0.7 %collective-permute-start.3 = (bf16[16,24,128]{2,1,0:T(8,128)(2,1)S(1)}, bf16[16,24,128]{2,1,0:T(8,128)(2,1)S(1)}, u32[]{:S(2)}, u32[]{:S(2)}) collective-permute-start(bf16[16,24,128]{2,1,0:T(8,128)(2,1)S(1)} %collective-permute-done), channel_id=1, source_target_pairs={{0,2},{1,3},{2,0},{3,1},{4,6},{5,7},{6,4},{7,5},{8,10},{9,11},{10,... | collective-permute-start | bytes 294920 | tf_op jit(solution)/shard_map/ppermute | solution.py:24
  14.3 0.1 pad_maximum_fusion.1.refs_2_
  14.4 0.1 collective-permute-start.8
  14.4 1.8 %collective-permute-done.1 = bf16[16,24,128]{2,1,0:T(8,128)(2,1)S(1)} collective-permute-done((bf16[16,24,128]{2,1,0:T(8,128)(2,1)S(1)}, bf16[16,24,128]{2,1,0:T(8,128)(2,1)S(1)}, u32[]{:S(2)}, u32[]{:S(2)}) %collective-permute-start.1) | collective-permute-done | bytes 98336 | tf_op jit(solution)/shard_map/ppermute | solution.py:24
  16.2 1.3 %collective-permute-done.2 = bf16[16,24,128]{2,1,0:T(8,128)(2,1)S(1)} collective-permute-done((bf16[16,24,128]{2,1,0:T(8,128)(2,1)S(1)}, bf16[16,24,128]{2,1,0:T(8,128)(2,1)S(1)}, u32[]{:S(2)}, u32[]{:S(2)}) %collective-permute-start.2) | collective-permute-done | bytes 98336 | tf_op jit(solution)/shard_map/ppermute | solution.py:24
  17.5 0.7 %collective-permute-done.3 = bf16[16,24,128]{2,1,0:T(8,128)(2,1)S(1)} collective-permute-done((bf16[16,24,128]{2,1,0:T(8,128)(2,1)S(1)}, bf16[16,24,128]{2,1,0:T(8,128)(2,1)S(1)}, u32[]{:S(2)}, u32[]{:S(2)}) %collective-permute-start.3) | collective-permute-done | bytes 98336 | tf_op jit(solution)/shard_map/ppermute | solution.py:24
  18.2 0.1 collective-permute-start.4
  18.3 0.1 slice_bitcast_fusion.1
  18.4 0.0 copy-start
  18.5 0.1 pad_maximum_fusion.refs_5_
  18.6 1.3 %early.1 = (f32[16,128,256]{2,1,0:T(8,128)S(1)}, f32[4,96,128]{2,1,0:T(8,128)S(1)}) custom-call(bf16[3,16,24,128]{3,2,1,0:T(8,128)(2,1)S(1)} %pad_maximum_fusion.2.refs_0_, bf16[4,16,24,128]{3,2,1,0:T(8,128)(2,1)S(1)} %collective-permute-done.8.refs_1_, bf16[4,16,24,128]{3,2,1,0:T(8,128)(2,1)S(1)} %pad_maximum_fusion.1.refs_2_, ...), custom_call_target="tpu_custom_call" | custom-call | tf_op jit(solution)/shard_map/early/pallas_call | solution.py:179
  19.9 0.0 collective-permute-done.4.refs_0_
  19.9 2.2 %late.1 = (bf16[1,2,128,128]{3,2,1,0:T(8,128)(2,1)}, f32[2,16]{1,0:T(2,128)}) custom-call(bf16[3,16,24,128]{3,2,1,0:T(8,128)(2,1)S(1)} %collective-permute-done.4.refs_0_, s32[16]{0:T(128)S(1)} %bitcast.26, s32[16]{0:T(128)S(1)} %copy-done.2, s32[16]{0:T(128)S(1)} %copy-done.3, bf16[16,24,128]{2,1,0:T(8,128)(2,1)S(1)} %bitcast.25, ...), custom_call_target="tpu_custom_call" | custom-call | tf_op jit(solution)/shard_map/late/pallas_call | solution.py:191
  (15 shorter events, 0.1 us)
Async XLA Ops:
  0.6 17.7 %copy-start.4 = (bf16[16,2,128,128]{3,2,1,0:T(8,128)(2,1)S(1)}, bf16[16,2,128,128]{3,2,1,0:T(8,128)(2,1)}, u32[]{:S(2)}) copy-start(bf16[16,2,128,128]{3,2,1,0:T(8,128)(2,1)} %param.8) | copy-start | bytes 3145732
  0.6 9.1 %collective-permute-start = (bf16[16,24,128]{2,1,0:T(8,128)(2,1)}, bf16[16,24,128]{2,1,0:T(8,128)(2,1)S(1)}, u32[]{:S(2)}, u32[]{:S(2)}) collective-permute-start(bf16[16,24,128]{2,1,0:T(8,128)(2,1)} %bitcast.20), channel_id=1, source_target_pairs={{0,8},{1,9},{2,10},{3,11},{4,12},{5,13},{6,14},{7,15},{8,0},{9,1},... | collective-permute-start | bytes 294920 | tf_op jit(solution)/shard_map/ppermute | solution.py:24
  4.7 7.6 %collective-permute-start.5 = (bf16[16,24,128]{2,1,0:T(8,128)(2,1)}, bf16[16,24,128]{2,1,0:T(8,128)(2,1)S(1)}, u32[]{:S(2)}, u32[]{:S(2)}) collective-permute-start(bf16[16,24,128]{2,1,0:T(8,128)(2,1)} %bitcast.21), channel_id=1, source_target_pairs={{0,6},{1,7},{2,4},{3,5},{4,2},{5,3},{6,0},{7,1},{8,14},{9,15},{10,... | collective-permute-start | bytes 294920 | tf_op jit(solution)/shard_map/ppermute | solution.py:24
  7.3 6.3 %collective-permute-start.6 = (bf16[16,24,128]{2,1,0:T(8,128)(2,1)}, bf16[16,24,128]{2,1,0:T(8,128)(2,1)S(1)}, u32[]{:S(2)}, u32[]{:S(2)}) collective-permute-start(bf16[16,24,128]{2,1,0:T(8,128)(2,1)} %bitcast.22), channel_id=1, source_target_pairs={{0,4},{1,5},{2,6},{3,7},{4,0},{5,1},{6,2},{7,3},{8,12},{9,13},{10,... | collective-permute-start | bytes 294920 | tf_op jit(solution)/shard_map/ppermute | solution.py:24
  7.7 6.6 %collective-permute-start.7 = (bf16[16,24,128]{2,1,0:T(8,128)(2,1)}, bf16[16,24,128]{2,1,0:T(8,128)(2,1)S(1)}, u32[]{:S(2)}, u32[]{:S(2)}) collective-permute-start(bf16[16,24,128]{2,1,0:T(8,128)(2,1)} %bitcast.23), channel_id=1, source_target_pairs={{0,2},{1,3},{2,0},{3,1},{4,6},{5,7},{6,4},{7,5},{8,10},{9,11},{10,... | collective-permute-start | bytes 294920 | tf_op jit(solution)/shard_map/ppermute | solution.py:24
  8.2 10.4 %collective-permute-start.9 = (bf16[16,24,128]{2,1,0:T(8,128)(2,1)}, bf16[16,24,128]{2,1,0:T(8,128)(2,1)S(1)}, u32[]{:S(2)}, u32[]{:S(2)}) collective-permute-start(bf16[16,24,128]{2,1,0:T(8,128)(2,1)} %bitcast.24), channel_id=1, source_target_pairs={{0,1},{1,0},{2,3},{3,2},{4,5},{5,4},{6,7},{7,6},{8,9},{9,8},{10,11... | collective-permute-start | bytes 294920 | tf_op jit(solution)/shard_map/ppermute | solution.py:24
  9.8 6.4 %collective-permute-start.1 = (bf16[16,24,128]{2,1,0:T(8,128)(2,1)S(1)}, bf16[16,24,128]{2,1,0:T(8,128)(2,1)S(1)}, u32[]{:S(2)}, u32[]{:S(2)}) collective-permute-start(bf16[16,24,128]{2,1,0:T(8,128)(2,1)S(1)} %collective-permute-done), channel_id=1, source_target_pairs={{0,6},{1,7},{2,4},{3,5},{4,2},{5,3},{6,0},{7,1},{8,14},{9,15},{10,... | collective-permute-start | bytes 294920 | tf_op jit(solution)/shard_map/ppermute | solution.py:24
  12.3 5.2 %collective-permute-start.2 = (bf16[16,24,128]{2,1,0:T(8,128)(2,1)S(1)}, bf16[16,24,128]{2,1,0:T(8,128)(2,1)S(1)}, u32[]{:S(2)}, u32[]{:S(2)}) collective-permute-start(bf16[16,24,128]{2,1,0:T(8,128)(2,1)S(1)} %collective-permute-done), channel_id=1, source_target_pairs={{0,4},{1,5},{2,6},{3,7},{4,0},{5,1},{6,2},{7,3},{8,12},{9,13},{10,... | collective-permute-start | bytes 294920 | tf_op jit(solution)/shard_map/ppermute | solution.py:24
  13.6 4.6 %collective-permute-start.3 = (bf16[16,24,128]{2,1,0:T(8,128)(2,1)S(1)}, bf16[16,24,128]{2,1,0:T(8,128)(2,1)S(1)}, u32[]{:S(2)}, u32[]{:S(2)}) collective-permute-start(bf16[16,24,128]{2,1,0:T(8,128)(2,1)S(1)} %collective-permute-done), channel_id=1, source_target_pairs={{0,2},{1,3},{2,0},{3,1},{4,6},{5,7},{6,4},{7,5},{8,10},{9,11},{10,... | collective-permute-start | bytes 294920 | tf_op jit(solution)/shard_map/ppermute | solution.py:24
  14.4 4.2 %collective-permute-start.8 = (bf16[4,16,24,128]{3,2,1,0:T(8,128)(2,1)S(1)}, bf16[4,16,24,128]{3,2,1,0:T(8,128)(2,1)S(1)}, u32[]{:S(2)}, u32[]{:S(2)}) collective-permute-start(bf16[4,16,24,128]{3,2,1,0:T(8,128)(2,1)S(1)} %pad_maximum_fusion.1.refs_2_), channel_id=1, source_target_pairs={{0,1},{1,0},{2,3},{3,2},{4,5},{5,4},{6,7},{7,6},{8,9},{9,8},{10,11... | collective-permute-start | bytes 1179656 | tf_op jit(solution)/shard_map/ppermute | solution.py:24
  18.2 1.6 %collective-permute-start.4 = (bf16[3,16,24,128]{3,2,1,0:T(8,128)(2,1)S(1)}, bf16[3,16,24,128]{3,2,1,0:T(8,128)(2,1)S(1)}, u32[]{:S(2)}, u32[]{:S(2)}) collective-permute-start(bf16[3,16,24,128]{3,2,1,0:T(8,128)(2,1)S(1)} %pad_maximum_fusion.2.refs_0_), channel_id=1, source_target_pairs={{0,1},{1,0},{2,3},{3,2},{4,5},{5,4},{6,7},{7,6},{8,9},{9,8},{10,11... | collective-permute-start | bytes 884744 | tf_op jit(solution)/shard_map/ppermute | solution.py:24
  18.4 1.5 %copy-start = (bf16[16,4,2,3,128]{4,2,3,1,0:T(2,128)(2,1)S(1)}, bf16[16,4,2,3,128]{4,2,3,1,0:T(2,128)(2,1)}, u32[]{:S(2)}) copy-start(bf16[16,4,2,3,128]{4,2,3,1,0:T(2,128)(2,1)} %param.6) | copy-start | bytes 294916
  18.4 1.5 %copy-start.1 = (s32[16,1]{0,1:T(1,128)S(1)}, s32[16,1]{0,1:T(1,128)}, u32[]{:S(2)}) copy-start(s32[16,1]{0,1:T(1,128)} %param.9) | copy-start | bytes 196
  18.4 1.5 %copy-start.2 = (s32[16]{0:T(128)S(1)}, s32[16]{0:T(128)}, u32[]{:S(2)}) copy-start(s32[16]{0:T(128)} %refs_2_.1) | copy-start | bytes 196
  18.4 1.5 %copy-start.3 = (s32[16]{0:T(128)S(1)}, s32[16]{0:T(128)}, u32[]{:S(2)}) copy-start(s32[16]{0:T(128)} %refs_3_.1) | copy-start | bytes 196

commit v5 on v4

--- a/solution.py
+++ b/solution.py
@@ -164,8 +164,9 @@
     [far] = step([own], 8)
     [d], [b], [y] = step([own], 6), step([own], 4), step([own], 2)
     [fd], [fb], [fy] = step([far], 6), step([far], 4), step([far], 2)
-    near = stacked([far, d, b, y])
-    so, sn = step([own, near], 1)
+    [so] = step([own], 1)
+    near = stacked([far, y, b, d])
+    [sn] = step([near], 1)
     rest = stacked([fd, fb, fy])
     [sr] = step([rest], 1)
     early, late = [rest, sn, near, so], [sr]

time: 22.3 us -> 21.9 us (0.982)
  starting transfers between devices: 11.7 us -> 11.4 us
    ppermute x10, starting transfers between devices: 11.7 us -> 11.4 us  [swap(): return lax.ppermute(block, AXIS, [(i, i ^ offset) for i in range(size)])]
where the time goes in v5:
time: 21.9 us; the launch traced here: 21.7 us
  starting transfers between devices  11.4 us (52%)
  waiting for transfers between devices  4.92 us (22%)
  Pallas kernels  3.46 us (16%)
  other arithmetic  0.92 us (4%)
  between operations  0.78 us (4%)
  local copies, waits for them, and re-layouts  0.26 us (1%)
    ppermute x10, starting transfers between devices, swap(): return lax.ppermute(block, AXIS, [(i, i ^ offset) for i in range(size)])  11.4 us
    ppermute x10, waiting for transfers between devices, swap(): return lax.ppermute(block, AXIS, [(i, i ^ offset) for i in range(size)])  4.92 us
    pallas_call x1, Pallas kernels, by_gathered_vectors(): pl.pallas_call(functools.partial(late_kernel, late_pieces), out_shape=(ja...  2.2 us
    pallas_call x1, Pallas kernels, by_gathered_vectors(): pl.pallas_call(functools.partial(early_kernel, early_pieces, later), out_...  1.26 us
    sin x1, other arithmetic, phases(): return (jnp.cos(angle), jnp.sin(angle))  0.7 us
  transfers between devices with their start and end apart: 10, of which 5 were waited for; matrix products, arithmetic and copies ran while one was open for 5% of the time, Pallas kernels for 6%

profile of v5, /device:TPU:0, one launch (start us, length us, event | category | flops | bytes accessed | tf_op | source)
XLA Modules:
  0.0 21.7 jit_solution(3118294162577107253)
XLA Ops:
  0.6 4.1 %collective-permute-start = (bf16[16,24,128]{2,1,0:T(8,128)(2,1)}, bf16[16,24,128]{2,1,0:T(8,128)(2,1)S(1)}, u32[]{:S(2)}, u32[]{:S(2)}) collective-permute-start(bf16[16,24,128]{2,1,0:T(8,128)(2,1)} %bitcast.20), channel_id=1, source_target_pairs={{0,8},{1,9},{2,10},{3,11},{4,12},{5,13},{6,14},{7,15},{8,0},{9,1},... | collective-permute-start | bytes 294920 | tf_op jit(solution)/shard_map/ppermute | solution.py:24
  4.7 1.5 %collective-permute-start.5 = (bf16[16,24,128]{2,1,0:T(8,128)(2,1)}, bf16[16,24,128]{2,1,0:T(8,128)(2,1)S(1)}, u32[]{:S(2)}, u32[]{:S(2)}) collective-permute-start(bf16[16,24,128]{2,1,0:T(8,128)(2,1)} %bitcast.21), channel_id=1, source_target_pairs={{0,2},{1,3},{2,0},{3,1},{4,6},{5,7},{6,4},{7,5},{8,10},{9,11},{10,... | collective-permute-start | bytes 294920 | tf_op jit(solution)/shard_map/ppermute | solution.py:24
  6.3 1.6 %collective-permute-start.6 = (bf16[16,24,128]{2,1,0:T(8,128)(2,1)}, bf16[16,24,128]{2,1,0:T(8,128)(2,1)S(1)}, u32[]{:S(2)}, u32[]{:S(2)}) collective-permute-start(bf16[16,24,128]{2,1,0:T(8,128)(2,1)} %bitcast.22), channel_id=1, source_target_pairs={{0,4},{1,5},{2,6},{3,7},{4,0},{5,1},{6,2},{7,3},{8,12},{9,13},{10,... | collective-permute-start | bytes 294920 | tf_op jit(solution)/shard_map/ppermute | solution.py:24
  7.8 0.4 %collective-permute-start.7 = (bf16[16,24,128]{2,1,0:T(8,128)(2,1)}, bf16[16,24,128]{2,1,0:T(8,128)(2,1)S(1)}, u32[]{:S(2)}, u32[]{:S(2)}) collective-permute-start(bf16[16,24,128]{2,1,0:T(8,128)(2,1)} %bitcast.23), channel_id=1, source_target_pairs={{0,6},{1,7},{2,4},{3,5},{4,2},{5,3},{6,0},{7,1},{8,14},{9,15},{10,... | collective-permute-start | bytes 294920 | tf_op jit(solution)/shard_map/ppermute | solution.py:24
  8.2 0.7 %fusion = (f32[64]{0:T(128)S(1)}, f32[64]{0:T(128)S(1)}) fusion(s32[64]{0:T(128)} %param.7), kind=kLoop, calls=%fused_computation.6 | loop fusion | flops 128 | bytes 768 | tf_op jit(solution)/shard_map/sin | solution.py:19
  8.9 0.1 reshape.14.refs_4_
  9.0 0.1 reshape.15.refs_5_
  9.1 0.9 %collective-permute-done = bf16[16,24,128]{2,1,0:T(8,128)(2,1)S(1)} collective-permute-done((bf16[16,24,128]{2,1,0:T(8,128)(2,1)}, bf16[16,24,128]{2,1,0:T(8,128)(2,1)S(1)}, u32[]{:S(2)}, u32[]{:S(2)}) %collective-permute-start) | collective-permute-done | bytes 98336 | tf_op jit(solution)/shard_map/ppermute | solution.py:24
  10.0 1.8 %collective-permute-start.1 = (bf16[16,24,128]{2,1,0:T(8,128)(2,1)S(1)}, bf16[16,24,128]{2,1,0:T(8,128)(2,1)S(1)}, u32[]{:S(2)}, u32[]{:S(2)}) collective-permute-start(bf16[16,24,128]{2,1,0:T(8,128)(2,1)S(1)} %collective-permute-done), channel_id=1, source_target_pairs={{0,6},{1,7},{2,4},{3,5},{4,2},{5,3},{6,0},{7,1},{8,14},{9,15},{10,... | collective-permute-start | bytes 294920 | tf_op jit(solution)/shard_map/ppermute | solution.py:24
  11.7 1.1 %collective-permute-start.2 = (bf16[16,24,128]{2,1,0:T(8,128)(2,1)S(1)}, bf16[16,24,128]{2,1,0:T(8,128)(2,1)S(1)}, u32[]{:S(2)}, u32[]{:S(2)}) collective-permute-start(bf16[16,24,128]{2,1,0:T(8,128)(2,1)S(1)} %collective-permute-done), channel_id=1, source_target_pairs={{0,4},{1,5},{2,6},{3,7},{4,0},{5,1},{6,2},{7,3},{8,12},{9,13},{10,... | collective-permute-start | bytes 294920 | tf_op jit(solution)/shard_map/ppermute | solution.py:24
  12.8 0.8 %collective-permute-start.3 = (bf16[16,24,128]{2,1,0:T(8,128)(2,1)S(1)}, bf16[16,24,128]{2,1,0:T(8,128)(2,1)S(1)}, u32[]{:S(2)}, u32[]{:S(2)}) collective-permute-start(bf16[16,24,128]{2,1,0:T(8,128)(2,1)S(1)} %collective-permute-done), channel_id=1, source_target_pairs={{0,2},{1,3},{2,0},{3,1},{4,6},{5,7},{6,4},{7,5},{8,10},{9,11},{10,... | collective-permute-start | bytes 294920 | tf_op jit(solution)/shard_map/ppermute | solution.py:24
  13.6 0.4 %collective-permute-done.7 = bf16[16,24,128]{2,1,0:T(8,128)(2,1)S(1)} collective-permute-done((bf16[16,24,128]{2,1,0:T(8,128)(2,1)}, bf16[16,24,128]{2,1,0:T(8,128)(2,1)S(1)}, u32[]{:S(2)}, u32[]{:S(2)}) %collective-permute-start.7) | collective-permute-done | bytes 98336 | tf_op jit(solution)/shard_map/ppermute | solution.py:24
  14.0 0.1 pad_maximum_fusion.1.refs_2_
  14.0 0.1 collective-permute-start.8
  14.1 2.4 %collective-permute-done.1 = bf16[16,24,128]{2,1,0:T(8,128)(2,1)S(1)} collective-permute-done((bf16[16,24,128]{2,1,0:T(8,128)(2,1)S(1)}, bf16[16,24,128]{2,1,0:T(8,128)(2,1)S(1)}, u32[]{:S(2)}, u32[]{:S(2)}) %collective-permute-start.1) | collective-permute-done | bytes 98336 | tf_op jit(solution)/shard_map/ppermute | solution.py:24
  16.6 1.1 %collective-permute-done.2 = bf16[16,24,128]{2,1,0:T(8,128)(2,1)S(1)} collective-permute-done((bf16[16,24,128]{2,1,0:T(8,128)(2,1)S(1)}, bf16[16,24,128]{2,1,0:T(8,128)(2,1)S(1)}, u32[]{:S(2)}, u32[]{:S(2)}) %collective-permute-start.2) | collective-permute-done | bytes 98336 | tf_op jit(solution)/shard_map/ppermute | solution.py:24
  17.6 0.1 collective-permute-done.3
  17.8 0.1 collective-permute-start.4
  17.9 0.1 slice_bitcast_fusion.1
  18.0 0.0 copy-start
  18.0 0.1 pad_maximum_fusion.refs_5_
  18.2 1.3 %early.1 = (f32[16,128,256]{2,1,0:T(8,128)S(1)}, f32[4,96,128]{2,1,0:T(8,128)S(1)}) custom-call(bf16[3,16,24,128]{3,2,1,0:T(8,128)(2,1)S(1)} %pad_maximum_fusion.2.refs_0_, bf16[4,16,24,128]{3,2,1,0:T(8,128)(2,1)S(1)} %collective-permute-done.8.refs_1_, bf16[4,16,24,128]{3,2,1,0:T(8,128)(2,1)S(1)} %pad_maximum_fusion.1.refs_2_, ...), custom_call_target="tpu_custom_call" | custom-call | tf_op jit(solution)/shard_map/early/pallas_call | solution.py:180
  19.5 0.0 collective-permute-done.4.refs_0_
  19.5 2.2 %late.1 = (bf16[1,2,128,128]{3,2,1,0:T(8,128)(2,1)}, f32[2,16]{1,0:T(2,128)}) custom-call(bf16[3,16,24,128]{3,2,1,0:T(8,128)(2,1)S(1)} %collective-permute-done.4.refs_0_, s32[16]{0:T(128)S(1)} %bitcast.26, s32[16]{0:T(128)S(1)} %copy-done.2, s32[16]{0:T(128)S(1)} %copy-done.3, bf16[16,24,128]{2,1,0:T(8,128)(2,1)S(1)} %bitcast.25, ...), custom_call_target="tpu_custom_call" | custom-call | tf_op jit(solution)/shard_map/late/pallas_call | solution.py:192
  (15 shorter events, 0.1 us)
Async XLA Ops:
  0.6 17.3 %copy-start.4 = (bf16[16,2,128,128]{3,2,1,0:T(8,128)(2,1)S(1)}, bf16[16,2,128,128]{3,2,1,0:T(8,128)(2,1)}, u32[]{:S(2)}) copy-start(bf16[16,2,128,128]{3,2,1,0:T(8,128)(2,1)} %param.8) | copy-start | bytes 3145732
  0.6 9.3 %collective-permute-start = (bf16[16,24,128]{2,1,0:T(8,128)(2,1)}, bf16[16,24,128]{2,1,0:T(8,128)(2,1)S(1)}, u32[]{:S(2)}, u32[]{:S(2)}) collective-permute-start(bf16[16,24,128]{2,1,0:T(8,128)(2,1)} %bitcast.20), channel_id=1, source_target_pairs={{0,8},{1,9},{2,10},{3,11},{4,12},{5,13},{6,14},{7,15},{8,0},{9,1},... | collective-permute-start | bytes 294920 | tf_op jit(solution)/shard_map/ppermute | solution.py:24
  4.7 7.0 %collective-permute-start.5 = (bf16[16,24,128]{2,1,0:T(8,128)(2,1)}, bf16[16,24,128]{2,1,0:T(8,128)(2,1)S(1)}, u32[]{:S(2)}, u32[]{:S(2)}) collective-permute-start(bf16[16,24,128]{2,1,0:T(8,128)(2,1)} %bitcast.21), channel_id=1, source_target_pairs={{0,2},{1,3},{2,0},{3,1},{4,6},{5,7},{6,4},{7,5},{8,10},{9,11},{10,... | collective-permute-start | bytes 294920 | tf_op jit(solution)/shard_map/ppermute | solution.py:24
  6.3 6.6 %collective-permute-start.6 = (bf16[16,24,128]{2,1,0:T(8,128)(2,1)}, bf16[16,24,128]{2,1,0:T(8,128)(2,1)S(1)}, u32[]{:S(2)}, u32[]{:S(2)}) collective-permute-start(bf16[16,24,128]{2,1,0:T(8,128)(2,1)} %bitcast.22), channel_id=1, source_target_pairs={{0,4},{1,5},{2,6},{3,7},{4,0},{5,1},{6,2},{7,3},{8,12},{9,13},{10,... | collective-permute-start | bytes 294920 | tf_op jit(solution)/shard_map/ppermute | solution.py:24
  7.8 6.2 %collective-permute-start.7 = (bf16[16,24,128]{2,1,0:T(8,128)(2,1)}, bf16[16,24,128]{2,1,0:T(8,128)(2,1)S(1)}, u32[]{:S(2)}, u32[]{:S(2)}) collective-permute-start(bf16[16,24,128]{2,1,0:T(8,128)(2,1)} %bitcast.23), channel_id=1, source_target_pairs={{0,6},{1,7},{2,4},{3,5},{4,2},{5,3},{6,0},{7,1},{8,14},{9,15},{10,... | collective-permute-start | bytes 294920 | tf_op jit(solution)/shard_map/ppermute | solution.py:24
  8.2 10.0 %collective-permute-start.9 = (bf16[16,24,128]{2,1,0:T(8,128)(2,1)}, bf16[16,24,128]{2,1,0:T(8,128)(2,1)S(1)}, u32[]{:S(2)}, u32[]{:S(2)}) collective-permute-start(bf16[16,24,128]{2,1,0:T(8,128)(2,1)} %bitcast.24), channel_id=1, source_target_pairs={{0,1},{1,0},{2,3},{3,2},{4,5},{5,4},{6,7},{7,6},{8,9},{9,8},{10,11... | collective-permute-start | bytes 294920 | tf_op jit(solution)/shard_map/ppermute | solution.py:24
  10.0 6.6 %collective-permute-start.1 = (bf16[16,24,128]{2,1,0:T(8,128)(2,1)S(1)}, bf16[16,24,128]{2,1,0:T(8,128)(2,1)S(1)}, u32[]{:S(2)}, u32[]{:S(2)}) collective-permute-start(bf16[16,24,128]{2,1,0:T(8,128)(2,1)S(1)} %collective-permute-done), channel_id=1, source_target_pairs={{0,6},{1,7},{2,4},{3,5},{4,2},{5,3},{6,0},{7,1},{8,14},{9,15},{10,... | collective-permute-start | bytes 294920 | tf_op jit(solution)/shard_map/ppermute | solution.py:24
  11.7 5.9 %collective-permute-start.2 = (bf16[16,24,128]{2,1,0:T(8,128)(2,1)S(1)}, bf16[16,24,128]{2,1,0:T(8,128)(2,1)S(1)}, u32[]{:S(2)}, u32[]{:S(2)}) collective-permute-start(bf16[16,24,128]{2,1,0:T(8,128)(2,1)S(1)} %collective-permute-done), channel_id=1, source_target_pairs={{0,4},{1,5},{2,6},{3,7},{4,0},{5,1},{6,2},{7,3},{8,12},{9,13},{10,... | collective-permute-start | bytes 294920 | tf_op jit(solution)/shard_map/ppermute | solution.py:24
  12.8 4.9 %collective-permute-start.3 = (bf16[16,24,128]{2,1,0:T(8,128)(2,1)S(1)}, bf16[16,24,128]{2,1,0:T(8,128)(2,1)S(1)}, u32[]{:S(2)}, u32[]{:S(2)}) collective-permute-start(bf16[16,24,128]{2,1,0:T(8,128)(2,1)S(1)} %collective-permute-done), channel_id=1, source_target_pairs={{0,2},{1,3},{2,0},{3,1},{4,6},{5,7},{6,4},{7,5},{8,10},{9,11},{10,... | collective-permute-start | bytes 294920 | tf_op jit(solution)/shard_map/ppermute | solution.py:24
  14.0 4.1 %collective-permute-start.8 = (bf16[4,16,24,128]{3,2,1,0:T(8,128)(2,1)S(1)}, bf16[4,16,24,128]{3,2,1,0:T(8,128)(2,1)S(1)}, u32[]{:S(2)}, u32[]{:S(2)}) collective-permute-start(bf16[4,16,24,128]{3,2,1,0:T(8,128)(2,1)S(1)} %pad_maximum_fusion.1.refs_2_), channel_id=1, source_target_pairs={{0,1},{1,0},{2,3},{3,2},{4,5},{5,4},{6,7},{7,6},{8,9},{9,8},{10,11... | collective-permute-start | bytes 1179656 | tf_op jit(solution)/shard_map/ppermute | solution.py:24
  17.8 1.6 %collective-permute-start.4 = (bf16[3,16,24,128]{3,2,1,0:T(8,128)(2,1)S(1)}, bf16[3,16,24,128]{3,2,1,0:T(8,128)(2,1)S(1)}, u32[]{:S(2)}, u32[]{:S(2)}) collective-permute-start(bf16[3,16,24,128]{3,2,1,0:T(8,128)(2,1)S(1)} %pad_maximum_fusion.2.refs_0_), channel_id=1, source_target_pairs={{0,1},{1,0},{2,3},{3,2},{4,5},{5,4},{6,7},{7,6},{8,9},{9,8},{10,11... | collective-permute-start | bytes 884744 | tf_op jit(solution)/shard_map/ppermute | solution.py:24
  18.0 1.5 %copy-start = (bf16[16,4,2,3,128]{4,2,3,1,0:T(2,128)(2,1)S(1)}, bf16[16,4,2,3,128]{4,2,3,1,0:T(2,128)(2,1)}, u32[]{:S(2)}) copy-start(bf16[16,4,2,3,128]{4,2,3,1,0:T(2,128)(2,1)} %param.6) | copy-start | bytes 294916
  18.0 1.5 %copy-start.1 = (s32[16,1]{0,1:T(1,128)S(1)}, s32[16,1]{0,1:T(1,128)}, u32[]{:S(2)}) copy-start(s32[16,1]{0,1:T(1,128)} %param.9) | copy-start | bytes 196
  18.0 1.5 %copy-start.2 = (s32[16]{0:T(128)S(1)}, s32[16]{0:T(128)}, u32[]{:S(2)}) copy-start(s32[16]{0:T(128)} %refs_2_.1) | copy-start | bytes 196
  18.0 1.5 %copy-start.3 = (s32[16]{0:T(128)S(1)}, s32[16]{0:T(128)}, u32[]{:S(2)}) copy-start(s32[16]{0:T(128)} %refs_3_.1) | copy-start | bytes 196

commit v6 on v4

--- a/solution.py
+++ b/solution.py
@@ -161,14 +161,19 @@
     rows = sites * colors * parts
     block = eigvecs.transpose(0, 1, 3, 2, 4).reshape(times, rows, n)
     own = (block, (0,))
-    [far] = step([own], 8)
-    [d], [b], [y] = step([own], 6), step([own], 4), step([own], 2)
-    [fd], [fb], [fy] = step([far], 6), step([far], 4), step([far], 2)
-    near = stacked([far, d, b, y])
-    so, sn = step([own, near], 1)
-    rest = stacked([fd, fb, fy])
-    [sr] = step([rest], 1)
-    early, late = [rest, sn, near, so], [sr]
+    outer, bit = [own], devices // 2
+    while bit >= 8:
+        outer += step(outer, bit)
+        bit //= 2
+    far = outer[1:]
+    d, b, y = (step([own], offset) for offset in (6, 4, 2))
+    far_d, far_b, far_y = (step(far, offset) for offset in (6, 4, 2))
+    [side] = step([own], 1)
+    near = stacked([*far, *y, *b, *d])
+    [side_near] = step([near], 1)
+    rest = stacked([*far_d, *far_b, *far_y])
+    [side_rest] = step([rest], 1)
+    early, late = [rest, near, side_near, side], [side_rest]
     cosine, sine = (value.reshape(devices, sites) for value in phases(phase_index))
     tiles = perambulator.shape[0]
     vmem = pl.BlockSpec(memory_space=pltpu.VMEM)
@@ -257,8 +262,11 @@
 
 def local(eigvecs, *rest):
     devices = lax.axis_size(AXIS)
+    times, sites, parts, colors, _ = eigvecs.shape
     small = eigvecs.size * eigvecs.dtype.itemsize * devices <= GATHER_BYTES
-    if small and devices & (devices - 1) == 0:
+    paired = devices >= 16 and devices & (devices - 1) == 0
+    whole = times == devices and sites * parts * colors % 8 == 0
+    if small and paired and whole:
         return by_gathered_vectors(eigvecs, *rest)
     return by_gathered_elementals(eigvecs, *rest)
 

time: 22.3 us -> 21.9 us (0.982)
  starting transfers between devices: 11.7 us -> 11.4 us
    ppermute x10, starting transfers between devices: 11.7 us -> 11.4 us  [swap(): return lax.ppermute(block, AXIS, [(i, i ^ offset) for i in range(size)])]
where the time goes in v6:
time: 21.9 us; the launch traced here: 21.7 us
  starting transfers between devices  11.4 us (52%)
  waiting for transfers between devices  4.92 us (22%)
  Pallas kernels  3.42 us (16%)
  other arithmetic  0.92 us (4%)
  between operations  0.78 us (4%)
  local copies, waits for them, and re-layouts  0.26 us (1%)
    ppermute x10, starting transfers between devices, swap(): return lax.ppermute(block, AXIS, [(i, i ^ offset) for i in range(size)])  11.4 us
    ppermute x10, waiting for transfers between devices, swap(): return lax.ppermute(block, AXIS, [(i, i ^ offset) for i in range(size)])  4.92 us
    pallas_call x1, Pallas kernels, by_gathered_vectors(): pl.pallas_call(functools.partial(late_kernel, late_pieces), out_shape=(ja...  2.16 us
    pallas_call x1, Pallas kernels, by_gathered_vectors(): pl.pallas_call(functools.partial(early_kernel, early_pieces, later), out_...  1.26 us
    sin x1, other arithmetic, phases(): return (jnp.cos(angle), jnp.sin(angle))  0.7 us
  transfers between devices with their start and end apart: 10, of which 5 were waited for; matrix products, arithmetic and copies ran while one was open for 5% of the time, Pallas kernels for 6%

profile of v6, /device:TPU:0, one launch (start us, length us, event | category | flops | bytes accessed | tf_op | source)
XLA Modules:
  0.0 21.7 jit_solution(16875165404930835119)
XLA Ops:
  0.6 4.1 %collective-permute-start = (bf16[16,24,128]{2,1,0:T(8,128)(2,1)}, bf16[16,24,128]{2,1,0:T(8,128)(2,1)S(1)}, u32[]{:S(2)}, u32[]{:S(2)}) collective-permute-start(bf16[16,24,128]{2,1,0:T(8,128)(2,1)} %bitcast.20), channel_id=1, source_target_pairs={{0,8},{1,9},{2,10},{3,11},{4,12},{5,13},{6,14},{7,15},{8,0},{9,1},... | collective-permute-start | bytes 294920 | tf_op jit(solution)/shard_map/ppermute | solution.py:24
  4.7 1.5 %collective-permute-start.5 = (bf16[16,24,128]{2,1,0:T(8,128)(2,1)}, bf16[16,24,128]{2,1,0:T(8,128)(2,1)S(1)}, u32[]{:S(2)}, u32[]{:S(2)}) collective-permute-start(bf16[16,24,128]{2,1,0:T(8,128)(2,1)} %bitcast.21), channel_id=1, source_target_pairs={{0,2},{1,3},{2,0},{3,1},{4,6},{5,7},{6,4},{7,5},{8,10},{9,11},{10,... | collective-permute-start | bytes 294920 | tf_op jit(solution)/shard_map/ppermute | solution.py:24
  6.3 1.6 %collective-permute-start.6 = (bf16[16,24,128]{2,1,0:T(8,128)(2,1)}, bf16[16,24,128]{2,1,0:T(8,128)(2,1)S(1)}, u32[]{:S(2)}, u32[]{:S(2)}) collective-permute-start(bf16[16,24,128]{2,1,0:T(8,128)(2,1)} %bitcast.22), channel_id=1, source_target_pairs={{0,4},{1,5},{2,6},{3,7},{4,0},{5,1},{6,2},{7,3},{8,12},{9,13},{10,... | collective-permute-start | bytes 294920 | tf_op jit(solution)/shard_map/ppermute | solution.py:24
  7.8 0.4 %collective-permute-start.7 = (bf16[16,24,128]{2,1,0:T(8,128)(2,1)}, bf16[16,24,128]{2,1,0:T(8,128)(2,1)S(1)}, u32[]{:S(2)}, u32[]{:S(2)}) collective-permute-start(bf16[16,24,128]{2,1,0:T(8,128)(2,1)} %bitcast.23), channel_id=1, source_target_pairs={{0,6},{1,7},{2,4},{3,5},{4,2},{5,3},{6,0},{7,1},{8,14},{9,15},{10,... | collective-permute-start | bytes 294920 | tf_op jit(solution)/shard_map/ppermute | solution.py:24
  8.2 0.7 %fusion = (f32[64]{0:T(128)S(1)}, f32[64]{0:T(128)S(1)}) fusion(s32[64]{0:T(128)} %param.7), kind=kLoop, calls=%fused_computation.6 | loop fusion | flops 128 | bytes 768 | tf_op jit(solution)/shard_map/sin | solution.py:19
  8.9 0.1 reshape.14.refs_4_
  9.0 0.1 reshape.15.refs_5_
  9.1 0.9 %collective-permute-done = bf16[16,24,128]{2,1,0:T(8,128)(2,1)S(1)} collective-permute-done((bf16[16,24,128]{2,1,0:T(8,128)(2,1)}, bf16[16,24,128]{2,1,0:T(8,128)(2,1)S(1)}, u32[]{:S(2)}, u32[]{:S(2)}) %collective-permute-start) | collective-permute-done | bytes 98336 | tf_op jit(solution)/shard_map/ppermute | solution.py:24
  10.0 1.8 %collective-permute-start.1 = (bf16[16,24,128]{2,1,0:T(8,128)(2,1)S(1)}, bf16[16,24,128]{2,1,0:T(8,128)(2,1)S(1)}, u32[]{:S(2)}, u32[]{:S(2)}) collective-permute-start(bf16[16,24,128]{2,1,0:T(8,128)(2,1)S(1)} %collective-permute-done), channel_id=1, source_target_pairs={{0,6},{1,7},{2,4},{3,5},{4,2},{5,3},{6,0},{7,1},{8,14},{9,15},{10,... | collective-permute-start | bytes 294920 | tf_op jit(solution)/shard_map/ppermute | solution.py:24
  11.7 1.1 %collective-permute-start.2 = (bf16[16,24,128]{2,1,0:T(8,128)(2,1)S(1)}, bf16[16,24,128]{2,1,0:T(8,128)(2,1)S(1)}, u32[]{:S(2)}, u32[]{:S(2)}) collective-permute-start(bf16[16,24,128]{2,1,0:T(8,128)(2,1)S(1)} %collective-permute-done), channel_id=1, source_target_pairs={{0,4},{1,5},{2,6},{3,7},{4,0},{5,1},{6,2},{7,3},{8,12},{9,13},{10,... | collective-permute-start | bytes 294920 | tf_op jit(solution)/shard_map/ppermute | solution.py:24
  12.8 0.8 %collective-permute-start.3 = (bf16[16,24,128]{2,1,0:T(8,128)(2,1)S(1)}, bf16[16,24,128]{2,1,0:T(8,128)(2,1)S(1)}, u32[]{:S(2)}, u32[]{:S(2)}) collective-permute-start(bf16[16,24,128]{2,1,0:T(8,128)(2,1)S(1)} %collective-permute-done), channel_id=1, source_target_pairs={{0,2},{1,3},{2,0},{3,1},{4,6},{5,7},{6,4},{7,5},{8,10},{9,11},{10,... | collective-permute-start | bytes 294920 | tf_op jit(solution)/shard_map/ppermute | solution.py:24
  13.6 0.4 %collective-permute-done.7 = bf16[16,24,128]{2,1,0:T(8,128)(2,1)S(1)} collective-permute-done((bf16[16,24,128]{2,1,0:T(8,128)(2,1)}, bf16[16,24,128]{2,1,0:T(8,128)(2,1)S(1)}, u32[]{:S(2)}, u32[]{:S(2)}) %collective-permute-start.7) | collective-permute-done | bytes 98336 | tf_op jit(solution)/shard_map/ppermute | solution.py:24
  14.0 0.1 pad_maximum_fusion.1.refs_1_
  14.0 0.1 collective-permute-start.8
  14.1 2.4 %collective-permute-done.1 = bf16[16,24,128]{2,1,0:T(8,128)(2,1)S(1)} collective-permute-done((bf16[16,24,128]{2,1,0:T(8,128)(2,1)S(1)}, bf16[16,24,128]{2,1,0:T(8,128)(2,1)S(1)}, u32[]{:S(2)}, u32[]{:S(2)}) %collective-permute-start.1) | collective-permute-done | bytes 98336 | tf_op jit(solution)/shard_map/ppermute | solution.py:24
  16.6 1.1 %collective-permute-done.2 = bf16[16,24,128]{2,1,0:T(8,128)(2,1)S(1)} collective-permute-done((bf16[16,24,128]{2,1,0:T(8,128)(2,1)S(1)}, bf16[16,24,128]{2,1,0:T(8,128)(2,1)S(1)}, u32[]{:S(2)}, u32[]{:S(2)}) %collective-permute-start.2) | collective-permute-done | bytes 98336 | tf_op jit(solution)/shard_map/ppermute | solution.py:24
  17.6 0.1 collective-permute-done.3
  17.8 0.1 collective-permute-start.4
  17.9 0.1 slice_bitcast_fusion.1
  18.0 0.0 copy-start.2
  18.0 0.1 pad_maximum_fusion.refs_5_
  18.2 1.3 %early.1 = (f32[16,128,256]{2,1,0:T(8,128)S(1)}, f32[4,96,128]{2,1,0:T(8,128)S(1)}) custom-call(bf16[3,16,24,128]{3,2,1,0:T(8,128)(2,1)S(1)} %pad_maximum_fusion.2.refs_0_, bf16[4,16,24,128]{3,2,1,0:T(8,128)(2,1)S(1)} %pad_maximum_fusion.1.refs_1_, bf16[4,16,24,128]{3,2,1,0:T(8,128)(2,1)S(1)} %collective-permute-done.8.refs_2_, ...), custom_call_target="tpu_custom_call" | custom-call | tf_op jit(solution)/shard_map/early/pallas_call | solution.py:184
  19.5 0.0 collective-permute-done.4.refs_0_
  19.5 2.2 %late.1 = (bf16[1,2,128,128]{3,2,1,0:T(8,128)(2,1)}, f32[2,16]{1,0:T(2,128)}) custom-call(bf16[3,16,24,128]{3,2,1,0:T(8,128)(2,1)S(1)} %collective-permute-done.4.refs_0_, s32[16]{0:T(128)S(1)} %bitcast.26, s32[16]{0:T(128)S(1)} %copy-done.2, s32[16]{0:T(128)S(1)} %copy-done.3, bf16[16,24,128]{2,1,0:T(8,128)(2,1)S(1)} %bitcast.25, ...), custom_call_target="tpu_custom_call" | custom-call | tf_op jit(solution)/shard_map/late/pallas_call | solution.py:196
  (15 shorter events, 0.1 us)
Async XLA Ops:
  0.6 17.3 %copy-start.4 = (bf16[16,2,128,128]{3,2,1,0:T(8,128)(2,1)S(1)}, bf16[16,2,128,128]{3,2,1,0:T(8,128)(2,1)}, u32[]{:S(2)}) copy-start(bf16[16,2,128,128]{3,2,1,0:T(8,128)(2,1)} %param.8) | copy-start | bytes 3145732
  0.6 9.3 %collective-permute-start = (bf16[16,24,128]{2,1,0:T(8,128)(2,1)}, bf16[16,24,128]{2,1,0:T(8,128)(2,1)S(1)}, u32[]{:S(2)}, u32[]{:S(2)}) collective-permute-start(bf16[16,24,128]{2,1,0:T(8,128)(2,1)} %bitcast.20), channel_id=1, source_target_pairs={{0,8},{1,9},{2,10},{3,11},{4,12},{5,13},{6,14},{7,15},{8,0},{9,1},... | collective-permute-start | bytes 294920 | tf_op jit(solution)/shard_map/ppermute | solution.py:24
  4.7 7.0 %collective-permute-start.5 = (bf16[16,24,128]{2,1,0:T(8,128)(2,1)}, bf16[16,24,128]{2,1,0:T(8,128)(2,1)S(1)}, u32[]{:S(2)}, u32[]{:S(2)}) collective-permute-start(bf16[16,24,128]{2,1,0:T(8,128)(2,1)} %bitcast.21), channel_id=1, source_target_pairs={{0,2},{1,3},{2,0},{3,1},{4,6},{5,7},{6,4},{7,5},{8,10},{9,11},{10,... | collective-permute-start | bytes 294920 | tf_op jit(solution)/shard_map/ppermute | solution.py:24
  6.3 6.6 %collective-permute-start.6 = (bf16[16,24,128]{2,1,0:T(8,128)(2,1)}, bf16[16,24,128]{2,1,0:T(8,128)(2,1)S(1)}, u32[]{:S(2)}, u32[]{:S(2)}) collective-permute-start(bf16[16,24,128]{2,1,0:T(8,128)(2,1)} %bitcast.22), channel_id=1, source_target_pairs={{0,4},{1,5},{2,6},{3,7},{4,0},{5,1},{6,2},{7,3},{8,12},{9,13},{10,... | collective-permute-start | bytes 294920 | tf_op jit(solution)/shard_map/ppermute | solution.py:24
  7.8 6.2 %collective-permute-start.7 = (bf16[16,24,128]{2,1,0:T(8,128)(2,1)}, bf16[16,24,128]{2,1,0:T(8,128)(2,1)S(1)}, u32[]{:S(2)}, u32[]{:S(2)}) collective-permute-start(bf16[16,24,128]{2,1,0:T(8,128)(2,1)} %bitcast.23), channel_id=1, source_target_pairs={{0,6},{1,7},{2,4},{3,5},{4,2},{5,3},{6,0},{7,1},{8,14},{9,15},{10,... | collective-permute-start | bytes 294920 | tf_op jit(solution)/shard_map/ppermute | solution.py:24
  8.2 10.0 %collective-permute-start.9 = (bf16[16,24,128]{2,1,0:T(8,128)(2,1)}, bf16[16,24,128]{2,1,0:T(8,128)(2,1)S(1)}, u32[]{:S(2)}, u32[]{:S(2)}) collective-permute-start(bf16[16,24,128]{2,1,0:T(8,128)(2,1)} %bitcast.24), channel_id=1, source_target_pairs={{0,1},{1,0},{2,3},{3,2},{4,5},{5,4},{6,7},{7,6},{8,9},{9,8},{10,11... | collective-permute-start | bytes 294920 | tf_op jit(solution)/shard_map/ppermute | solution.py:24
  10.0 6.6 %collective-permute-start.1 = (bf16[16,24,128]{2,1,0:T(8,128)(2,1)S(1)}, bf16[16,24,128]{2,1,0:T(8,128)(2,1)S(1)}, u32[]{:S(2)}, u32[]{:S(2)}) collective-permute-start(bf16[16,24,128]{2,1,0:T(8,128)(2,1)S(1)} %collective-permute-done), channel_id=1, source_target_pairs={{0,6},{1,7},{2,4},{3,5},{4,2},{5,3},{6,0},{7,1},{8,14},{9,15},{10,... | collective-permute-start | bytes 294920 | tf_op jit(solution)/shard_map/ppermute | solution.py:24
  11.7 5.9 %collective-permute-start.2 = (bf16[16,24,128]{2,1,0:T(8,128)(2,1)S(1)}, bf16[16,24,128]{2,1,0:T(8,128)(2,1)S(1)}, u32[]{:S(2)}, u32[]{:S(2)}) collective-permute-start(bf16[16,24,128]{2,1,0:T(8,128)(2,1)S(1)} %collective-permute-done), channel_id=1, source_target_pairs={{0,4},{1,5},{2,6},{3,7},{4,0},{5,1},{6,2},{7,3},{8,12},{9,13},{10,... | collective-permute-start | bytes 294920 | tf_op jit(solution)/shard_map/ppermute | solution.py:24
  12.8 4.9 %collective-permute-start.3 = (bf16[16,24,128]{2,1,0:T(8,128)(2,1)S(1)}, bf16[16,24,128]{2,1,0:T(8,128)(2,1)S(1)}, u32[]{:S(2)}, u32[]{:S(2)}) collective-permute-start(bf16[16,24,128]{2,1,0:T(8,128)(2,1)S(1)} %collective-permute-done), channel_id=1, source_target_pairs={{0,2},{1,3},{2,0},{3,1},{4,6},{5,7},{6,4},{7,5},{8,10},{9,11},{10,... | collective-permute-start | bytes 294920 | tf_op jit(solution)/shard_map/ppermute | solution.py:24
  14.0 4.1 %collective-permute-start.8 = (bf16[4,16,24,128]{3,2,1,0:T(8,128)(2,1)S(1)}, bf16[4,16,24,128]{3,2,1,0:T(8,128)(2,1)S(1)}, u32[]{:S(2)}, u32[]{:S(2)}) collective-permute-start(bf16[4,16,24,128]{3,2,1,0:T(8,128)(2,1)S(1)} %pad_maximum_fusion.1.refs_1_), channel_id=1, source_target_pairs={{0,1},{1,0},{2,3},{3,2},{4,5},{5,4},{6,7},{7,6},{8,9},{9,8},{10,11... | collective-permute-start | bytes 1179656 | tf_op jit(solution)/shard_map/ppermute | solution.py:24
  17.8 1.6 %collective-permute-start.4 = (bf16[3,16,24,128]{3,2,1,0:T(8,128)(2,1)S(1)}, bf16[3,16,24,128]{3,2,1,0:T(8,128)(2,1)S(1)}, u32[]{:S(2)}, u32[]{:S(2)}) collective-permute-start(bf16[3,16,24,128]{3,2,1,0:T(8,128)(2,1)S(1)} %pad_maximum_fusion.2.refs_0_), channel_id=1, source_target_pairs={{0,1},{1,0},{2,3},{3,2},{4,5},{5,4},{6,7},{7,6},{8,9},{9,8},{10,11... | collective-permute-start | bytes 884744 | tf_op jit(solution)/shard_map/ppermute | solution.py:24
  18.0 1.5 %copy-start = (bf16[16,4,2,3,128]{4,2,3,1,0:T(2,128)(2,1)S(1)}, bf16[16,4,2,3,128]{4,2,3,1,0:T(2,128)(2,1)}, u32[]{:S(2)}) copy-start(bf16[16,4,2,3,128]{4,2,3,1,0:T(2,128)(2,1)} %param.6) | copy-start | bytes 294916
  18.0 1.5 %copy-start.1 = (s32[16,1]{0,1:T(1,128)S(1)}, s32[16,1]{0,1:T(1,128)}, u32[]{:S(2)}) copy-start(s32[16,1]{0,1:T(1,128)} %param.9) | copy-start | bytes 196
  18.0 1.5 %copy-start.2 = (s32[16]{0:T(128)S(1)}, s32[16]{0:T(128)}, u32[]{:S(2)}) copy-start(s32[16]{0:T(128)} %refs_2_.1) | copy-start | bytes 196
  18.0 1.5 %copy-start.3 = (s32[16]{0:T(128)S(1)}, s32[16]{0:T(128)}, u32[]{:S(2)}) copy-start(s32[16]{0:T(128)} %refs_3_.1) | copy-start | bytes 196

commit v7 on v6

--- a/solution.py
+++ b/solution.py
@@ -124,18 +124,17 @@
 
 def late_kernel(pieces, *refs):
     held, refs = refs[: len(pieces)], refs[len(pieces) :]
-    sink_any, sep_any, diagram_any, own_any, tiles_ref, sum_ref, tables_ref, *refs = refs
-    elemental_any, corr_ref, plain, turned, re_ref, im_ref, block_ref, out_ref, *ids, sems = refs
+    sink_any, sep_any, diagram_any, block_ref, tiles_ref, sum_ref, tables_ref, *refs = refs
+    elemental_any, corr_ref, plain, turned, re_ref, im_ref, out_ref, *ids, sems = refs
     loads_in = [
         pltpu.make_async_copy(source, target, sems.at[i])
-        for i, (source, target) in enumerate(zip((own_any, sink_any, sep_any, diagram_any), (block_ref, *ids)))
+        for i, (source, target) in enumerate(zip((sink_any, sep_any, diagram_any), ids))
     ]
     for load in loads_in:
         load.start()
     loads, _ = block_list((block_ref, *held), ((0,), *pieces))
     tables = [tables_ref.at[i] for i in range(4)]
     times, n = plain.shape[:2]
-    loads_in[0].wait()
     for t in range(times):
         value = (sum_ref[t] + slice_values(loads, t, tables)).astype(jnp.bfloat16)
         plain[t] = value
@@ -143,9 +142,9 @@
     own = plain[lax.axis_index(AXIS).astype(jnp.int32)]
     out_ref[0, 0] = own[:, :n]
     out_ref[0, 1] = own[:, n:]
-    store = pltpu.make_async_copy(out_ref, elemental_any, sems.at[4])
+    store = pltpu.make_async_copy(out_ref, elemental_any, sems.at[3])
     store.start()
-    for load in loads_in[1:]:
+    for load in loads_in:
         load.wait()
     contract(ids, plain, turned, tiles_ref, re_ref, im_ref, corr_ref)
     store.wait()
@@ -199,17 +198,16 @@
             jax.ShapeDtypeStruct((1, 2, n, n), jnp.bfloat16),
             jax.ShapeDtypeStruct((2, tiles), jnp.float32),
         ),
-        in_specs=[vmem] * len(late) + [anywhere] * 4 + [vmem] * 3,
+        in_specs=[vmem] * len(late) + [anywhere] * 3 + [vmem] * 4,
         out_specs=(anywhere, vmem),
         scratch_shapes=[
             pltpu.VMEM((times, n, 2 * n), jnp.bfloat16),
             pltpu.VMEM((times, n, 2 * n), jnp.bfloat16),
             pltpu.VMEM((tiles, n), jnp.float32),
             pltpu.VMEM((tiles, n), jnp.float32),
-            pltpu.VMEM(block.shape, block.dtype),
             pltpu.VMEM((1, 2, n, n), jnp.bfloat16),
             *[pltpu.SMEM((tiles,), jnp.int32)] * 3,
-            pltpu.SemaphoreType.DMA((5,)),
+            pltpu.SemaphoreType.DMA((4,)),
         ],
         compiler_params=pltpu.CompilerParams(vmem_limit_bytes=VMEM_LIMIT),
         name="late",

time: 21.9 us -> 22 us (level)
  no operation moved by 1% of the time
where the time goes in v7:
time: 22 us; the launch traced here: 21.8 us
  starting transfers between devices  11.4 us (52%)
  waiting for transfers between devices  4.92 us (22%)
  Pallas kernels  3.56 us (16%)
  other arithmetic  0.92 us (4%)
  between operations  0.78 us (4%)
  local copies, waits for them, and re-layouts  0.26 us (1%)
    ppermute x10, starting transfers between devices, swap(): return lax.ppermute(block, AXIS, [(i, i ^ offset) for i in range(size)])  11.4 us
    ppermute x10, waiting for transfers between devices, swap(): return lax.ppermute(block, AXIS, [(i, i ^ offset) for i in range(size)])  4.92 us
    pallas_call x1, Pallas kernels, by_gathered_vectors(): pl.pallas_call(functools.partial(late_kernel, late_pieces), out_shape=(ja...  2.3 us
    pallas_call x1, Pallas kernels, by_gathered_vectors(): pl.pallas_call(functools.partial(early_kernel, early_pieces, later), out_...  1.26 us
    sin x1, other arithmetic, phases(): return (jnp.cos(angle), jnp.sin(angle))  0.7 us
  transfers between devices with their start and end apart: 10, of which 5 were waited for; matrix products, arithmetic and copies ran while one was open for 5% of the time, Pallas kernels for 6%

profile of v7, /device:TPU:0, one launch (start us, length us, event | category | flops | bytes accessed | tf_op | source)
XLA Modules:
  0.0 21.8 jit_solution(5237172024319594825)
XLA Ops:
  0.6 4.1 %collective-permute-start = (bf16[16,24,128]{2,1,0:T(8,128)(2,1)}, bf16[16,24,128]{2,1,0:T(8,128)(2,1)S(1)}, u32[]{:S(2)}, u32[]{:S(2)}) collective-permute-start(bf16[16,24,128]{2,1,0:T(8,128)(2,1)} %bitcast.20), channel_id=1, source_target_pairs={{0,8},{1,9},{2,10},{3,11},{4,12},{5,13},{6,14},{7,15},{8,0},{9,1},... | collective-permute-start | bytes 294920 | tf_op jit(solution)/shard_map/ppermute | solution.py:24
  4.7 1.5 %collective-permute-start.5 = (bf16[16,24,128]{2,1,0:T(8,128)(2,1)}, bf16[16,24,128]{2,1,0:T(8,128)(2,1)S(1)}, u32[]{:S(2)}, u32[]{:S(2)}) collective-permute-start(bf16[16,24,128]{2,1,0:T(8,128)(2,1)} %bitcast.21), channel_id=1, source_target_pairs={{0,2},{1,3},{2,0},{3,1},{4,6},{5,7},{6,4},{7,5},{8,10},{9,11},{10,... | collective-permute-start | bytes 294920 | tf_op jit(solution)/shard_map/ppermute | solution.py:24
  6.3 1.6 %collective-permute-start.6 = (bf16[16,24,128]{2,1,0:T(8,128)(2,1)}, bf16[16,24,128]{2,1,0:T(8,128)(2,1)S(1)}, u32[]{:S(2)}, u32[]{:S(2)}) collective-permute-start(bf16[16,24,128]{2,1,0:T(8,128)(2,1)} %bitcast.22), channel_id=1, source_target_pairs={{0,4},{1,5},{2,6},{3,7},{4,0},{5,1},{6,2},{7,3},{8,12},{9,13},{10,... | collective-permute-start | bytes 294920 | tf_op jit(solution)/shard_map/ppermute | solution.py:24
  7.8 0.4 %collective-permute-start.7 = (bf16[16,24,128]{2,1,0:T(8,128)(2,1)}, bf16[16,24,128]{2,1,0:T(8,128)(2,1)S(1)}, u32[]{:S(2)}, u32[]{:S(2)}) collective-permute-start(bf16[16,24,128]{2,1,0:T(8,128)(2,1)} %bitcast.23), channel_id=1, source_target_pairs={{0,6},{1,7},{2,4},{3,5},{4,2},{5,3},{6,0},{7,1},{8,14},{9,15},{10,... | collective-permute-start | bytes 294920 | tf_op jit(solution)/shard_map/ppermute | solution.py:24
  8.2 0.7 %fusion = (f32[64]{0:T(128)S(1)}, f32[64]{0:T(128)S(1)}) fusion(s32[64]{0:T(128)} %param.7), kind=kLoop, calls=%fused_computation.6 | loop fusion | flops 128 | bytes 768 | tf_op jit(solution)/shard_map/sin | solution.py:19
  8.9 0.1 reshape.14.refs_4_
  9.0 0.1 reshape.15.refs_5_
  9.1 0.9 %collective-permute-done = bf16[16,24,128]{2,1,0:T(8,128)(2,1)S(1)} collective-permute-done((bf16[16,24,128]{2,1,0:T(8,128)(2,1)}, bf16[16,24,128]{2,1,0:T(8,128)(2,1)S(1)}, u32[]{:S(2)}, u32[]{:S(2)}) %collective-permute-start) | collective-permute-done | bytes 98336 | tf_op jit(solution)/shard_map/ppermute | solution.py:24
  10.0 1.8 %collective-permute-start.1 = (bf16[16,24,128]{2,1,0:T(8,128)(2,1)S(1)}, bf16[16,24,128]{2,1,0:T(8,128)(2,1)S(1)}, u32[]{:S(2)}, u32[]{:S(2)}) collective-permute-start(bf16[16,24,128]{2,1,0:T(8,128)(2,1)S(1)} %collective-permute-done), channel_id=1, source_target_pairs={{0,6},{1,7},{2,4},{3,5},{4,2},{5,3},{6,0},{7,1},{8,14},{9,15},{10,... | collective-permute-start | bytes 294920 | tf_op jit(solution)/shard_map/ppermute | solution.py:24
  11.7 1.1 %collective-permute-start.2 = (bf16[16,24,128]{2,1,0:T(8,128)(2,1)S(1)}, bf16[16,24,128]{2,1,0:T(8,128)(2,1)S(1)}, u32[]{:S(2)}, u32[]{:S(2)}) collective-permute-start(bf16[16,24,128]{2,1,0:T(8,128)(2,1)S(1)} %collective-permute-done), channel_id=1, source_target_pairs={{0,4},{1,5},{2,6},{3,7},{4,0},{5,1},{6,2},{7,3},{8,12},{9,13},{10,... | collective-permute-start | bytes 294920 | tf_op jit(solution)/shard_map/ppermute | solution.py:24
  12.8 0.8 %collective-permute-start.3 = (bf16[16,24,128]{2,1,0:T(8,128)(2,1)S(1)}, bf16[16,24,128]{2,1,0:T(8,128)(2,1)S(1)}, u32[]{:S(2)}, u32[]{:S(2)}) collective-permute-start(bf16[16,24,128]{2,1,0:T(8,128)(2,1)S(1)} %collective-permute-done), channel_id=1, source_target_pairs={{0,2},{1,3},{2,0},{3,1},{4,6},{5,7},{6,4},{7,5},{8,10},{9,11},{10,... | collective-permute-start | bytes 294920 | tf_op jit(solution)/shard_map/ppermute | solution.py:24
  13.6 0.4 %collective-permute-done.7 = bf16[16,24,128]{2,1,0:T(8,128)(2,1)S(1)} collective-permute-done((bf16[16,24,128]{2,1,0:T(8,128)(2,1)}, bf16[16,24,128]{2,1,0:T(8,128)(2,1)S(1)}, u32[]{:S(2)}, u32[]{:S(2)}) %collective-permute-start.7) | collective-permute-done | bytes 98336 | tf_op jit(solution)/shard_map/ppermute | solution.py:24
  14.0 0.1 pad_maximum_fusion.1.refs_1_
  14.0 0.1 collective-permute-start.8
  14.1 2.4 %collective-permute-done.1 = bf16[16,24,128]{2,1,0:T(8,128)(2,1)S(1)} collective-permute-done((bf16[16,24,128]{2,1,0:T(8,128)(2,1)S(1)}, bf16[16,24,128]{2,1,0:T(8,128)(2,1)S(1)}, u32[]{:S(2)}, u32[]{:S(2)}) %collective-permute-start.1) | collective-permute-done | bytes 98336 | tf_op jit(solution)/shard_map/ppermute | solution.py:24
  16.6 1.1 %collective-permute-done.2 = bf16[16,24,128]{2,1,0:T(8,128)(2,1)S(1)} collective-permute-done((bf16[16,24,128]{2,1,0:T(8,128)(2,1)S(1)}, bf16[16,24,128]{2,1,0:T(8,128)(2,1)S(1)}, u32[]{:S(2)}, u32[]{:S(2)}) %collective-permute-start.2) | collective-permute-done | bytes 98336 | tf_op jit(solution)/shard_map/ppermute | solution.py:24
  17.6 0.1 collective-permute-done.3
  17.8 0.1 collective-permute-start.4
  17.9 0.1 slice_bitcast_fusion.1
  18.0 0.0 copy-start
  18.0 0.1 pad_maximum_fusion.refs_5_
  18.2 1.3 %early.1 = (f32[16,128,256]{2,1,0:T(8,128)S(1)}, f32[4,96,128]{2,1,0:T(8,128)S(1)}) custom-call(bf16[3,16,24,128]{3,2,1,0:T(8,128)(2,1)S(1)} %pad_maximum_fusion.2.refs_0_, bf16[4,16,24,128]{3,2,1,0:T(8,128)(2,1)S(1)} %pad_maximum_fusion.1.refs_1_, bf16[4,16,24,128]{3,2,1,0:T(8,128)(2,1)S(1)} %collective-permute-done.8.refs_2_, ...), custom_call_target="tpu_custom_call" | custom-call | tf_op jit(solution)/shard_map/early/pallas_call | solution.py:183
  19.5 0.0 collective-permute-done.4.refs_0_
  19.5 2.3 %late.1 = (bf16[1,2,128,128]{3,2,1,0:T(8,128)(2,1)}, f32[2,16]{1,0:T(2,128)}) custom-call(bf16[3,16,24,128]{3,2,1,0:T(8,128)(2,1)S(1)} %collective-permute-done.4.refs_0_, s32[16]{0:T(128)S(1)} %bitcast.26, s32[16]{0:T(128)S(1)} %copy-done.2, s32[16]{0:T(128)S(1)} %copy-done.3, bf16[16,24,128]{2,1,0:T(8,128)(2,1)S(1)} %bitcast.25, ...), custom_call_target="tpu_custom_call" | custom-call | tf_op jit(solution)/shard_map/late/pallas_call | solution.py:195
  (15 shorter events, 0.1 us)
Async XLA Ops:
  0.6 17.3 %copy-start.4 = (bf16[16,2,128,128]{3,2,1,0:T(8,128)(2,1)S(1)}, bf16[16,2,128,128]{3,2,1,0:T(8,128)(2,1)}, u32[]{:S(2)}) copy-start(bf16[16,2,128,128]{3,2,1,0:T(8,128)(2,1)} %param.8) | copy-start | bytes 3145732
  0.6 9.3 %collective-permute-start = (bf16[16,24,128]{2,1,0:T(8,128)(2,1)}, bf16[16,24,128]{2,1,0:T(8,128)(2,1)S(1)}, u32[]{:S(2)}, u32[]{:S(2)}) collective-permute-start(bf16[16,24,128]{2,1,0:T(8,128)(2,1)} %bitcast.20), channel_id=1, source_target_pairs={{0,8},{1,9},{2,10},{3,11},{4,12},{5,13},{6,14},{7,15},{8,0},{9,1},... | collective-permute-start | bytes 294920 | tf_op jit(solution)/shard_map/ppermute | solution.py:24
  4.7 7.0 %collective-permute-start.5 = (bf16[16,24,128]{2,1,0:T(8,128)(2,1)}, bf16[16,24,128]{2,1,0:T(8,128)(2,1)S(1)}, u32[]{:S(2)}, u32[]{:S(2)}) collective-permute-start(bf16[16,24,128]{2,1,0:T(8,128)(2,1)} %bitcast.21), channel_id=1, source_target_pairs={{0,2},{1,3},{2,0},{3,1},{4,6},{5,7},{6,4},{7,5},{8,10},{9,11},{10,... | collective-permute-start | bytes 294920 | tf_op jit(solution)/shard_map/ppermute | solution.py:24
  6.3 6.6 %collective-permute-start.6 = (bf16[16,24,128]{2,1,0:T(8,128)(2,1)}, bf16[16,24,128]{2,1,0:T(8,128)(2,1)S(1)}, u32[]{:S(2)}, u32[]{:S(2)}) collective-permute-start(bf16[16,24,128]{2,1,0:T(8,128)(2,1)} %bitcast.22), channel_id=1, source_target_pairs={{0,4},{1,5},{2,6},{3,7},{4,0},{5,1},{6,2},{7,3},{8,12},{9,13},{10,... | collective-permute-start | bytes 294920 | tf_op jit(solution)/shard_map/ppermute | solution.py:24
  7.8 6.2 %collective-permute-start.7 = (bf16[16,24,128]{2,1,0:T(8,128)(2,1)}, bf16[16,24,128]{2,1,0:T(8,128)(2,1)S(1)}, u32[]{:S(2)}, u32[]{:S(2)}) collective-permute-start(bf16[16,24,128]{2,1,0:T(8,128)(2,1)} %bitcast.23), channel_id=1, source_target_pairs={{0,6},{1,7},{2,4},{3,5},{4,2},{5,3},{6,0},{7,1},{8,14},{9,15},{10,... | collective-permute-start | bytes 294920 | tf_op jit(solution)/shard_map/ppermute | solution.py:24
  8.2 10.0 %collective-permute-start.9 = (bf16[16,24,128]{2,1,0:T(8,128)(2,1)}, bf16[16,24,128]{2,1,0:T(8,128)(2,1)S(1)}, u32[]{:S(2)}, u32[]{:S(2)}) collective-permute-start(bf16[16,24,128]{2,1,0:T(8,128)(2,1)} %bitcast.24), channel_id=1, source_target_pairs={{0,1},{1,0},{2,3},{3,2},{4,5},{5,4},{6,7},{7,6},{8,9},{9,8},{10,11... | collective-permute-start | bytes 294920 | tf_op jit(solution)/shard_map/ppermute | solution.py:24
  10.0 6.6 %collective-permute-start.1 = (bf16[16,24,128]{2,1,0:T(8,128)(2,1)S(1)}, bf16[16,24,128]{2,1,0:T(8,128)(2,1)S(1)}, u32[]{:S(2)}, u32[]{:S(2)}) collective-permute-start(bf16[16,24,128]{2,1,0:T(8,128)(2,1)S(1)} %collective-permute-done), channel_id=1, source_target_pairs={{0,6},{1,7},{2,4},{3,5},{4,2},{5,3},{6,0},{7,1},{8,14},{9,15},{10,... | collective-permute-start | bytes 294920 | tf_op jit(solution)/shard_map/ppermute | solution.py:24
  11.7 5.9 %collective-permute-start.2 = (bf16[16,24,128]{2,1,0:T(8,128)(2,1)S(1)}, bf16[16,24,128]{2,1,0:T(8,128)(2,1)S(1)}, u32[]{:S(2)}, u32[]{:S(2)}) collective-permute-start(bf16[16,24,128]{2,1,0:T(8,128)(2,1)S(1)} %collective-permute-done), channel_id=1, source_target_pairs={{0,4},{1,5},{2,6},{3,7},{4,0},{5,1},{6,2},{7,3},{8,12},{9,13},{10,... | collective-permute-start | bytes 294920 | tf_op jit(solution)/shard_map/ppermute | solution.py:24
  12.8 4.9 %collective-permute-start.3 = (bf16[16,24,128]{2,1,0:T(8,128)(2,1)S(1)}, bf16[16,24,128]{2,1,0:T(8,128)(2,1)S(1)}, u32[]{:S(2)}, u32[]{:S(2)}) collective-permute-start(bf16[16,24,128]{2,1,0:T(8,128)(2,1)S(1)} %collective-permute-done), channel_id=1, source_target_pairs={{0,2},{1,3},{2,0},{3,1},{4,6},{5,7},{6,4},{7,5},{8,10},{9,11},{10,... | collective-permute-start | bytes 294920 | tf_op jit(solution)/shard_map/ppermute | solution.py:24
  14.0 4.1 %collective-permute-start.8 = (bf16[4,16,24,128]{3,2,1,0:T(8,128)(2,1)S(1)}, bf16[4,16,24,128]{3,2,1,0:T(8,128)(2,1)S(1)}, u32[]{:S(2)}, u32[]{:S(2)}) collective-permute-start(bf16[4,16,24,128]{3,2,1,0:T(8,128)(2,1)S(1)} %pad_maximum_fusion.1.refs_1_), channel_id=1, source_target_pairs={{0,1},{1,0},{2,3},{3,2},{4,5},{5,4},{6,7},{7,6},{8,9},{9,8},{10,11... | collective-permute-start | bytes 1179656 | tf_op jit(solution)/shard_map/ppermute | solution.py:24
  17.8 1.6 %collective-permute-start.4 = (bf16[3,16,24,128]{3,2,1,0:T(8,128)(2,1)S(1)}, bf16[3,16,24,128]{3,2,1,0:T(8,128)(2,1)S(1)}, u32[]{:S(2)}, u32[]{:S(2)}) collective-permute-start(bf16[3,16,24,128]{3,2,1,0:T(8,128)(2,1)S(1)} %pad_maximum_fusion.2.refs_0_), channel_id=1, source_target_pairs={{0,1},{1,0},{2,3},{3,2},{4,5},{5,4},{6,7},{7,6},{8,9},{9,8},{10,11... | collective-permute-start | bytes 884744 | tf_op jit(solution)/shard_map/ppermute | solution.py:24
  18.0 1.5 %copy-start = (bf16[16,4,2,3,128]{4,2,3,1,0:T(2,128)(2,1)S(1)}, bf16[16,4,2,3,128]{4,2,3,1,0:T(2,128)(2,1)}, u32[]{:S(2)}) copy-start(bf16[16,4,2,3,128]{4,2,3,1,0:T(2,128)(2,1)} %param.6) | copy-start | bytes 294916
  18.0 1.5 %copy-start.1 = (s32[16,1]{0,1:T(1,128)S(1)}, s32[16,1]{0,1:T(1,128)}, u32[]{:S(2)}) copy-start(s32[16,1]{0,1:T(1,128)} %param.9) | copy-start | bytes 196
  18.0 1.5 %copy-start.2 = (s32[16]{0:T(128)S(1)}, s32[16]{0:T(128)}, u32[]{:S(2)}) copy-start(s32[16]{0:T(128)} %refs_2_.1) | copy-start | bytes 196
  18.0 1.5 %copy-start.3 = (s32[16]{0:T(128)S(1)}, s32[16]{0:T(128)}, u32[]{:S(2)}) copy-start(s32[16]{0:T(128)} %refs_3_.1) | copy-start | bytes 196

commit v8 on v6

--- a/solution.py
+++ b/solution.py
@@ -58,12 +58,12 @@
     return jnp.where(flipped, source, sink), jnp.where(flipped, sink, source), jnp.where(flipped, -1.0, 1.0)
 
 
-def contract(ids, plain, turned, tiles_ref, re_ref, im_ref, corr_ref):
-    count = tiles_ref.shape[0]
+def contract(ids, plain, turned, tiles, re_ref, im_ref, corr_ref):
+    count = tiles[0].shape[0]
 
     def one(i, carry):
         a, b, sign = pick(*ids, i, plain.shape[0])
-        re, im = tile_terms(plain[a], plain[b], turned[a], turned[b], tiles_ref[i])
+        re, im = tile_terms(plain[a], plain[b], turned[a], turned[b], jnp.concatenate([tiles[0][i], tiles[1][i]], 1))
         re_ref[pl.ds(i, 1), :] = re
         im_ref[pl.ds(i, 1), :] = im * sign
         return carry
@@ -124,7 +124,8 @@
 
 def late_kernel(pieces, *refs):
     held, refs = refs[: len(pieces)], refs[len(pieces) :]
-    sink_any, sep_any, diagram_any, own_any, tiles_ref, sum_ref, tables_ref, *refs = refs
+    sink_any, sep_any, diagram_any, own_any, *tiles, sum_ref, tables_ref = refs[:8]
+    refs = refs[8:]
     elemental_any, corr_ref, plain, turned, re_ref, im_ref, block_ref, out_ref, *ids, sems = refs
     loads_in = [
         pltpu.make_async_copy(source, target, sems.at[i])
@@ -147,12 +148,12 @@
     store.start()
     for load in loads_in[1:]:
         load.wait()
-    contract(ids, plain, turned, tiles_ref, re_ref, im_ref, corr_ref)
+    contract(ids, plain, turned, tiles, re_ref, im_ref, corr_ref)
     store.wait()
 
 
-def widened(perambulator):
-    return jnp.concatenate([perambulator[:, 0], perambulator[:, 1]], 2)
+def halves(perambulator):
+    return perambulator[:, 0], perambulator[:, 1]
 
 
 def by_gathered_vectors(eigvecs, phase_index, perambulator, tile_sink, tile_sep, tile_diagram):
@@ -199,7 +200,7 @@
             jax.ShapeDtypeStruct((1, 2, n, n), jnp.bfloat16),
             jax.ShapeDtypeStruct((2, tiles), jnp.float32),
         ),
-        in_specs=[vmem] * len(late) + [anywhere] * 4 + [vmem] * 3,
+        in_specs=[vmem] * len(late) + [anywhere] * 4 + [vmem] * 4,
         out_specs=(anywhere, vmem),
         scratch_shapes=[
             pltpu.VMEM((times, n, 2 * n), jnp.bfloat16),
@@ -213,11 +214,11 @@
         ],
         compiler_params=pltpu.CompilerParams(vmem_limit_bytes=VMEM_LIMIT),
         name="late",
-    )(*[array for array, _ in late], tile_sink[:, 0], tile_sep, tile_diagram, block, widened(perambulator), total, tables)
+    )(*[array for array, _ in late], tile_sink[:, 0], tile_sep, tile_diagram, block, *halves(perambulator), total, tables)
     return elemental, correlator.T
 
 
-def contract_kernel(sink_ref, sep_ref, diagram_ref, elementals_ref, tiles_ref, corr_ref, plain, turned, re_ref, im_ref):
+def contract_kernel(sink_ref, sep_ref, diagram_ref, elementals_ref, re_tiles, im_tiles, corr_ref, plain, turned, re_ref, im_ref):
     times = elementals_ref.shape[0]
 
     def widen(t, carry):
@@ -227,7 +228,7 @@
         return carry
 
     lax.fori_loop(0, times, widen, 0)
-    contract((sink_ref, sep_ref, diagram_ref), plain, turned, tiles_ref, re_ref, im_ref, corr_ref)
+    contract((sink_ref, sep_ref, diagram_ref), plain, turned, (re_tiles, im_tiles), re_ref, im_ref, corr_ref)
 
 
 def by_gathered_elementals(eigvecs, phase_index, perambulator, tile_sink, tile_sep, tile_diagram):
@@ -247,7 +248,7 @@
     correlator = pl.pallas_call(
         contract_kernel,
         out_shape=jax.ShapeDtypeStruct((2, tiles), jnp.float32),
-        in_specs=[smem] * 3 + [vmem] * 2,
+        in_specs=[smem] * 3 + [vmem] * 3,
         out_specs=vmem,
         scratch_shapes=[
             pltpu.VMEM((times, n, 2 * n), jnp.bfloat16),
@@ -256,7 +257,7 @@
             pltpu.VMEM((tiles, n), jnp.float32),
         ],
         compiler_params=pltpu.CompilerParams(vmem_limit_bytes=VMEM_LIMIT),
-    )(tile_sink[:, 0], tile_sep, tile_diagram, gathered, widened(perambulator))
+    )(tile_sink[:, 0], tile_sep, tile_diagram, gathered, *halves(perambulator))
     return elemental, correlator.T
 
 

time: 21.9 us -> 22 us (level)
  waiting for transfers between devices: 4.92 us -> 5.73 us
  other arithmetic: 0.92 us -> 0.13 us
    ppermute x10, waiting for transfers between devices: 4.92 us -> 5.73 us  [swap(): return lax.ppermute(block, AXIS, [(i, i ^ offset) for i in range(size)])]
    sin x1, other arithmetic: 0.7 us -> 0.04 us  [phases(): return (jnp.cos(angle), jnp.sin(angle))]
  transfers between devices with their start and end apart: 10 -> 10, of which waited for: 5 -> 5; matrix products, arithmetic and copies ran while one was open for 5% -> 2% of each run, Pallas kernels for 6% -> 6%
where the time goes in v8:
time: 22 us; the launch traced here: 21.8 us
  starting transfers between devices  11.4 us (52%)
  waiting for transfers between devices  5.73 us (26%)
  Pallas kernels  3.47 us (16%)
  between operations  0.79 us (4%)
  local copies, waits for them, and re-layouts  0.3 us (1%)
    ppermute x10, starting transfers between devices, swap(): return lax.ppermute(block, AXIS, [(i, i ^ offset) for i in range(size)])  11.4 us
    ppermute x10, waiting for transfers between devices, swap(): return lax.ppermute(block, AXIS, [(i, i ^ offset) for i in range(size)])  5.73 us
    pallas_call x1, Pallas kernels, by_gathered_vectors(): pl.pallas_call(functools.partial(late_kernel, late_pieces), out_shape=(ja...  2.21 us
    pallas_call x1, Pallas kernels, by_gathered_vectors(): pl.pallas_call(functools.partial(early_kernel, early_pieces, later), out_...  1.26 us
  transfers between devices with their start and end apart: 10, of which 5 were waited for; matrix products, arithmetic and copies ran while one was open for 2% of the time, Pallas kernels for 6%

profile of v8, /device:TPU:0, one launch (start us, length us, event | category | flops | bytes accessed | tf_op | source)
XLA Modules:
  0.0 21.8 jit_solution(18321881841427969607)
XLA Ops:
  0.6 4.1 %collective-permute-start = (bf16[16,24,128]{2,1,0:T(8,128)(2,1)}, bf16[16,24,128]{2,1,0:T(8,128)(2,1)S(1)}, u32[]{:S(2)}, u32[]{:S(2)}) collective-permute-start(bf16[16,24,128]{2,1,0:T(8,128)(2,1)} %bitcast.20), channel_id=1, source_target_pairs={{0,8},{1,9},{2,10},{3,11},{4,12},{5,13},{6,14},{7,15},{8,0},{9,1},... | collective-permute-start | bytes 294920 | tf_op jit(solution)/shard_map/ppermute | solution.py:24
  4.8 1.5 %collective-permute-start.5 = (bf16[16,24,128]{2,1,0:T(8,128)(2,1)}, bf16[16,24,128]{2,1,0:T(8,128)(2,1)S(1)}, u32[]{:S(2)}, u32[]{:S(2)}) collective-permute-start(bf16[16,24,128]{2,1,0:T(8,128)(2,1)} %bitcast.21), channel_id=1, source_target_pairs={{0,2},{1,3},{2,0},{3,1},{4,6},{5,7},{6,4},{7,5},{8,10},{9,11},{10,... | collective-permute-start | bytes 294920 | tf_op jit(solution)/shard_map/ppermute | solution.py:24
  6.3 1.6 %collective-permute-start.6 = (bf16[16,24,128]{2,1,0:T(8,128)(2,1)}, bf16[16,24,128]{2,1,0:T(8,128)(2,1)S(1)}, u32[]{:S(2)}, u32[]{:S(2)}) collective-permute-start(bf16[16,24,128]{2,1,0:T(8,128)(2,1)} %bitcast.22), channel_id=1, source_target_pairs={{0,4},{1,5},{2,6},{3,7},{4,0},{5,1},{6,2},{7,3},{8,12},{9,13},{10,... | collective-permute-start | bytes 294920 | tf_op jit(solution)/shard_map/ppermute | solution.py:24
  7.8 0.4 %collective-permute-start.7 = (bf16[16,24,128]{2,1,0:T(8,128)(2,1)}, bf16[16,24,128]{2,1,0:T(8,128)(2,1)S(1)}, u32[]{:S(2)}, u32[]{:S(2)}) collective-permute-start(bf16[16,24,128]{2,1,0:T(8,128)(2,1)} %bitcast.23), channel_id=1, source_target_pairs={{0,6},{1,7},{2,4},{3,5},{4,2},{5,3},{6,0},{7,1},{8,14},{9,15},{10,... | collective-permute-start | bytes 294920 | tf_op jit(solution)/shard_map/ppermute | solution.py:24
  8.2 1.7 %collective-permute-done = bf16[16,24,128]{2,1,0:T(8,128)(2,1)S(1)} collective-permute-done((bf16[16,24,128]{2,1,0:T(8,128)(2,1)}, bf16[16,24,128]{2,1,0:T(8,128)(2,1)S(1)}, u32[]{:S(2)}, u32[]{:S(2)}) %collective-permute-start) | collective-permute-done | bytes 98336 | tf_op jit(solution)/shard_map/ppermute | solution.py:24
  10.0 1.7 %collective-permute-start.1 = (bf16[16,24,128]{2,1,0:T(8,128)(2,1)S(1)}, bf16[16,24,128]{2,1,0:T(8,128)(2,1)S(1)}, u32[]{:S(2)}, u32[]{:S(2)}) collective-permute-start(bf16[16,24,128]{2,1,0:T(8,128)(2,1)S(1)} %collective-permute-done), channel_id=1, source_target_pairs={{0,6},{1,7},{2,4},{3,5},{4,2},{5,3},{6,0},{7,1},{8,14},{9,15},{10,... | collective-permute-start | bytes 294920 | tf_op jit(solution)/shard_map/ppermute | solution.py:24
  11.7 1.2 %collective-permute-start.2 = (bf16[16,24,128]{2,1,0:T(8,128)(2,1)S(1)}, bf16[16,24,128]{2,1,0:T(8,128)(2,1)S(1)}, u32[]{:S(2)}, u32[]{:S(2)}) collective-permute-start(bf16[16,24,128]{2,1,0:T(8,128)(2,1)S(1)} %collective-permute-done), channel_id=1, source_target_pairs={{0,4},{1,5},{2,6},{3,7},{4,0},{5,1},{6,2},{7,3},{8,12},{9,13},{10,... | collective-permute-start | bytes 294920 | tf_op jit(solution)/shard_map/ppermute | solution.py:24
  12.8 0.8 %collective-permute-start.3 = (bf16[16,24,128]{2,1,0:T(8,128)(2,1)S(1)}, bf16[16,24,128]{2,1,0:T(8,128)(2,1)S(1)}, u32[]{:S(2)}, u32[]{:S(2)}) collective-permute-start(bf16[16,24,128]{2,1,0:T(8,128)(2,1)S(1)} %collective-permute-done), channel_id=1, source_target_pairs={{0,2},{1,3},{2,0},{3,1},{4,6},{5,7},{6,4},{7,5},{8,10},{9,11},{10,... | collective-permute-start | bytes 294920 | tf_op jit(solution)/shard_map/ppermute | solution.py:24
  13.6 1.1 %collective-permute-done.7 = bf16[16,24,128]{2,1,0:T(8,128)(2,1)S(1)} collective-permute-done((bf16[16,24,128]{2,1,0:T(8,128)(2,1)}, bf16[16,24,128]{2,1,0:T(8,128)(2,1)S(1)}, u32[]{:S(2)}, u32[]{:S(2)}) %collective-permute-start.7) | collective-permute-done | bytes 98336 | tf_op jit(solution)/shard_map/ppermute | solution.py:24
  14.7 0.1 pad_maximum_fusion.refs_1_
  14.7 0.0 copy-start
  14.7 0.0 copy-start.1
  14.8 0.0 copy-start.3
  14.8 0.1 collective-permute-start.8
  14.9 1.9 %collective-permute-done.1 = bf16[16,24,128]{2,1,0:T(8,128)(2,1)S(1)} collective-permute-done((bf16[16,24,128]{2,1,0:T(8,128)(2,1)S(1)}, bf16[16,24,128]{2,1,0:T(8,128)(2,1)S(1)}, u32[]{:S(2)}, u32[]{:S(2)}) %collective-permute-start.1) | collective-permute-done | bytes 98336 | tf_op jit(solution)/shard_map/ppermute | solution.py:24
  16.7 0.9 %collective-permute-done.2 = bf16[16,24,128]{2,1,0:T(8,128)(2,1)S(1)} collective-permute-done((bf16[16,24,128]{2,1,0:T(8,128)(2,1)S(1)}, bf16[16,24,128]{2,1,0:T(8,128)(2,1)S(1)}, u32[]{:S(2)}, u32[]{:S(2)}) %collective-permute-start.2) | collective-permute-done | bytes 98336 | tf_op jit(solution)/shard_map/ppermute | solution.py:24
  17.6 0.1 collective-permute-done.3
  17.8 0.1 collective-permute-start.4
  17.9 0.1 slice_bitcast_fusion
  18.1 0.1 reshape.14.refs_4_
  18.2 0.1 reshape.15.refs_5_
  18.2 0.0 collective-permute-done.9.refs_3_
  18.3 1.3 %early.1 = (f32[16,128,256]{2,1,0:T(8,128)S(1)}, f32[4,96,128]{2,1,0:T(8,128)S(1)}) custom-call(bf16[3,16,24,128]{3,2,1,0:T(8,128)(2,1)S(1)} %pad_maximum_fusion.1.refs_0_, bf16[4,16,24,128]{3,2,1,0:T(8,128)(2,1)S(1)} %pad_maximum_fusion.refs_1_, bf16[4,16,24,128]{3,2,1,0:T(8,128)(2,1)S(1)} %collective-permute-done.8.refs_2_, ...), custom_call_target="tpu_custom_call" | custom-call | tf_op jit(solution)/shard_map/early/pallas_call | solution.py:185
  19.6 2.2 %late.1 = (bf16[1,2,128,128]{3,2,1,0:T(8,128)(2,1)}, f32[2,16]{1,0:T(2,128)}) custom-call(bf16[3,16,24,128]{3,2,1,0:T(8,128)(2,1)S(1)} %collective-permute-done.4.refs_0_, s32[16]{0:T(128)S(1)} %bitcast.26, s32[16]{0:T(128)S(1)} %copy-done.2, s32[16]{0:T(128)S(1)} %copy-done.3, bf16[16,24,128]{2,1,0:T(8,128)(2,1)S(1)} %bitcast.25, ...), custom_call_target="tpu_custom_call" | custom-call | tf_op jit(solution)/shard_map/late/pallas_call | solution.py:197
  (16 shorter events, 0.1 us)
Async XLA Ops:
  0.6 17.3 %copy-start.4 = (bf16[16,2,128,128]{3,2,1,0:T(8,128)(2,1)S(1)}, bf16[16,2,128,128]{3,2,1,0:T(8,128)(2,1)}, u32[]{:S(2)}) copy-start(bf16[16,2,128,128]{3,2,1,0:T(8,128)(2,1)} %param.8) | copy-start | bytes 3145732
  0.6 17.4 %copy-start.5 = (s32[64]{0:T(128)S(1)}, s32[64]{0:T(128)}, u32[]{:S(2)}) copy-start(s32[64]{0:T(128)} %param.7) | copy-start | bytes 772
  0.6 9.3 %collective-permute-start = (bf16[16,24,128]{2,1,0:T(8,128)(2,1)}, bf16[16,24,128]{2,1,0:T(8,128)(2,1)S(1)}, u32[]{:S(2)}, u32[]{:S(2)}) collective-permute-start(bf16[16,24,128]{2,1,0:T(8,128)(2,1)} %bitcast.20), channel_id=1, source_target_pairs={{0,8},{1,9},{2,10},{3,11},{4,12},{5,13},{6,14},{7,15},{8,0},{9,1},... | collective-permute-start | bytes 294920 | tf_op jit(solution)/shard_map/ppermute | solution.py:24
  4.8 6.9 %collective-permute-start.5 = (bf16[16,24,128]{2,1,0:T(8,128)(2,1)}, bf16[16,24,128]{2,1,0:T(8,128)(2,1)S(1)}, u32[]{:S(2)}, u32[]{:S(2)}) collective-permute-start(bf16[16,24,128]{2,1,0:T(8,128)(2,1)} %bitcast.21), channel_id=1, source_target_pairs={{0,2},{1,3},{2,0},{3,1},{4,6},{5,7},{6,4},{7,5},{8,10},{9,11},{10,... | collective-permute-start | bytes 294920 | tf_op jit(solution)/shard_map/ppermute | solution.py:24
  6.3 6.6 %collective-permute-start.6 = (bf16[16,24,128]{2,1,0:T(8,128)(2,1)}, bf16[16,24,128]{2,1,0:T(8,128)(2,1)S(1)}, u32[]{:S(2)}, u32[]{:S(2)}) collective-permute-start(bf16[16,24,128]{2,1,0:T(8,128)(2,1)} %bitcast.22), channel_id=1, source_target_pairs={{0,4},{1,5},{2,6},{3,7},{4,0},{5,1},{6,2},{7,3},{8,12},{9,13},{10,... | collective-permute-start | bytes 294920 | tf_op jit(solution)/shard_map/ppermute | solution.py:24
  7.8 6.8 %collective-permute-start.7 = (bf16[16,24,128]{2,1,0:T(8,128)(2,1)}, bf16[16,24,128]{2,1,0:T(8,128)(2,1)S(1)}, u32[]{:S(2)}, u32[]{:S(2)}) collective-permute-start(bf16[16,24,128]{2,1,0:T(8,128)(2,1)} %bitcast.23), channel_id=1, source_target_pairs={{0,6},{1,7},{2,4},{3,5},{4,2},{5,3},{6,0},{7,1},{8,14},{9,15},{10,... | collective-permute-start | bytes 294920 | tf_op jit(solution)/shard_map/ppermute | solution.py:24
  8.2 10.0 %collective-permute-start.9 = (bf16[16,24,128]{2,1,0:T(8,128)(2,1)}, bf16[16,24,128]{2,1,0:T(8,128)(2,1)S(1)}, u32[]{:S(2)}, u32[]{:S(2)}) collective-permute-start(bf16[16,24,128]{2,1,0:T(8,128)(2,1)} %bitcast.24), channel_id=1, source_target_pairs={{0,1},{1,0},{2,3},{3,2},{4,5},{5,4},{6,7},{7,6},{8,9},{9,8},{10,11... | collective-permute-start | bytes 294920 | tf_op jit(solution)/shard_map/ppermute | solution.py:24
  10.0 6.8 %collective-permute-start.1 = (bf16[16,24,128]{2,1,0:T(8,128)(2,1)S(1)}, bf16[16,24,128]{2,1,0:T(8,128)(2,1)S(1)}, u32[]{:S(2)}, u32[]{:S(2)}) collective-permute-start(bf16[16,24,128]{2,1,0:T(8,128)(2,1)S(1)} %collective-permute-done), channel_id=1, source_target_pairs={{0,6},{1,7},{2,4},{3,5},{4,2},{5,3},{6,0},{7,1},{8,14},{9,15},{10,... | collective-permute-start | bytes 294920 | tf_op jit(solution)/shard_map/ppermute | solution.py:24
  11.7 6.0 %collective-permute-start.2 = (bf16[16,24,128]{2,1,0:T(8,128)(2,1)S(1)}, bf16[16,24,128]{2,1,0:T(8,128)(2,1)S(1)}, u32[]{:S(2)}, u32[]{:S(2)}) collective-permute-start(bf16[16,24,128]{2,1,0:T(8,128)(2,1)S(1)} %collective-permute-done), channel_id=1, source_target_pairs={{0,4},{1,5},{2,6},{3,7},{4,0},{5,1},{6,2},{7,3},{8,12},{9,13},{10,... | collective-permute-start | bytes 294920 | tf_op jit(solution)/shard_map/ppermute | solution.py:24
  12.8 4.9 %collective-permute-start.3 = (bf16[16,24,128]{2,1,0:T(8,128)(2,1)S(1)}, bf16[16,24,128]{2,1,0:T(8,128)(2,1)S(1)}, u32[]{:S(2)}, u32[]{:S(2)}) collective-permute-start(bf16[16,24,128]{2,1,0:T(8,128)(2,1)S(1)} %collective-permute-done), channel_id=1, source_target_pairs={{0,2},{1,3},{2,0},{3,1},{4,6},{5,7},{6,4},{7,5},{8,10},{9,11},{10,... | collective-permute-start | bytes 294920 | tf_op jit(solution)/shard_map/ppermute | solution.py:24
  14.7 4.8 %copy-start = (bf16[16,4,2,3,128]{4,2,3,1,0:T(2,128)(2,1)S(1)}, bf16[16,4,2,3,128]{4,2,3,1,0:T(2,128)(2,1)}, u32[]{:S(2)}) copy-start(bf16[16,4,2,3,128]{4,2,3,1,0:T(2,128)(2,1)} %param.6) | copy-start | bytes 294916
  14.7 4.8 %copy-start.1 = (s32[16,1]{0,1:T(1,128)S(1)}, s32[16,1]{0,1:T(1,128)}, u32[]{:S(2)}) copy-start(s32[16,1]{0,1:T(1,128)} %param.9) | copy-start | bytes 196
  14.8 4.8 %copy-start.2 = (s32[16]{0:T(128)S(1)}, s32[16]{0:T(128)}, u32[]{:S(2)}) copy-start(s32[16]{0:T(128)} %refs_2_.1) | copy-start | bytes 196
  14.8 4.8 %copy-start.3 = (s32[16]{0:T(128)S(1)}, s32[16]{0:T(128)}, u32[]{:S(2)}) copy-start(s32[16]{0:T(128)} %refs_3_.1) | copy-start | bytes 196
  14.8 3.5 %collective-permute-start.8 = (bf16[4,16,24,128]{3,2,1,0:T(8,128)(2,1)S(1)}, bf16[4,16,24,128]{3,2,1,0:T(8,128)(2,1)S(1)}, u32[]{:S(2)}, u32[]{:S(2)}) collective-permute-start(bf16[4,16,24,128]{3,2,1,0:T(8,128)(2,1)S(1)} %pad_maximum_fusion.refs_1_), channel_id=1, source_target_pairs={{0,1},{1,0},{2,3},{3,2},{4,5},{5,4},{6,7},{7,6},{8,9},{9,8},{10,11... | collective-permute-start | bytes 1179656 | tf_op jit(solution)/shard_map/ppermute | solution.py:24
  17.8 1.7 %collective-permute-start.4 = (bf16[3,16,24,128]{3,2,1,0:T(8,128)(2,1)S(1)}, bf16[3,16,24,128]{3,2,1,0:T(8,128)(2,1)S(1)}, u32[]{:S(2)}, u32[]{:S(2)}) collective-permute-start(bf16[3,16,24,128]{3,2,1,0:T(8,128)(2,1)S(1)} %pad_maximum_fusion.1.refs_0_), channel_id=1, source_target_pairs={{0,1},{1,0},{2,3},{3,2},{4,5},{5,4},{6,7},{7,6},{8,9},{9,8},{10,11... | collective-permute-start | bytes 884744 | tf_op jit(solution)/shard_map/ppermute | solution.py:24
